TPU v7x, 32 devices: a whole 2x2x4 slice. The times are simulated.
32 devices in a mesh: view: 4 (over y, core), block: 8 (over z, x).
Axes of the slice: x: 2, y: 2, z: 4, core: 2. Of those that a mesh axis runs over, the one named last changes fastest.
Arguments:
- estimate0: float32 [512, 64, 256], P('block'), may hold values from 0.5 to 1.5
- pieces: bfloat16 [4, 128, 4, 64, 256], P('view', 'block'), may hold values from 0.19921875 to 2
- dest_block: int32 [4, 128, 1], replicated, may hold values from 0 to 7; in each aligned block of 16 rows (0 to 15, 16 to 31, ..., all dimensions but the last counted through in order) at most 2 rows name the same one
- slot_index: int32 [4, 128], replicated, may hold values from 0 to 15
- psf_shift: int32 [4, 3], replicated, may hold values from -3 to 3
- psf_taps: float32 [4, 3, 21], replicated, may hold values from 0.05 to 1
- background: float32 [4], replicated, may hold values from 0.1 to 0.5
Outputs:
- estimate: float32 [512, 64, 256], P('block')
Inputs may be any that keep to these rules, and one draw needn't show every extreme that they name: `dest_block`: among the 16 pieces held by one device (aligned blocks of 16 rows, views and pieces taken together), no slab is named more than 2 times.
All inputs are finite; a program needn't handle non-finite values.
Results may differ from a plain program's by a relative error of at most 0.0014.
Values may be sent and summed in bfloat16 or wider, within the bound.
A program may use at most 128 MiB of HBM per device.

v0:
```python
import jax
import jax.numpy as jnp
from jax import lax
from jax.sharding import PartitionSpec as P

CAP = 2
ITERS = 2
HALO = 13


HIGHEST = lax.Precision.HIGHEST


def with_halo(cells, sides, width):
    for axis, dim in sides:
        count = lax.axis_size(axis)
        ends = count - 1
        head = lax.slice_in_dim(cells, 0, width, axis=dim)
        tail = lax.slice_in_dim(cells, cells.shape[dim] - width, cells.shape[dim], axis=dim)
        cells = jnp.concatenate(
            [
                lax.ppermute(tail, axis, [(i, (i + 1) % count) for i in range(ends)]),
                cells,
                lax.ppermute(head, axis, [((i + 1) % count, i) for i in range(ends)]),
            ],
            axis=dim,
        )
    return cells


def band_matrix(kernel, shift, row_count, column_count, lead_offset):
    tap_count = kernel.shape[0]
    radius = (tap_count - 1) // 2
    difference = (
        lax.broadcasted_iota(jnp.int32, (row_count, column_count), 1)
        - lax.broadcasted_iota(jnp.int32, (row_count, column_count), 0)
        - lead_offset
        - shift
        + radius
    )
    tap_hits = difference[:, :, None] == jnp.arange(tap_count, dtype=jnp.int32)[None, None, :]
    return jnp.sum(jnp.where(tap_hits, kernel[None, None, :], 0.0), axis=2)


def column_sums(kernel, shift, length):
    tap_count = kernel.shape[-1]
    radius = (tap_count - 1) // 2
    source = (
        jnp.arange(length, dtype=jnp.int32)[None, :, None]
        - shift[:, None, None]
        - jnp.arange(tap_count, dtype=jnp.int32)[None, None, :]
        + radius
    )
    inside = (source >= 0) & (source < length)
    return jnp.sum(jnp.where(inside, kernel[:, None, :], 0.0), axis=2)


def blur_plane(volume, band_rows, band_columns):
    along_rows = jnp.einsum("yv,zvx->zyx", band_rows, volume, precision=HIGHEST)
    return jnp.einsum("zyv,xv->zyx", along_rows, band_columns, precision=HIGHEST)


def adjoint_plane(volume, band_rows, band_columns):
    along_rows = jnp.einsum("vy,zvx->zyx", band_rows, volume, precision=HIGHEST)
    return jnp.einsum("zyv,vx->zyx", along_rows, band_columns, precision=HIGHEST)


def along_depth(matrix, volume):
    flattened = volume.reshape(volume.shape[0], volume.shape[1] * volume.shape[2])
    result = jnp.dot(matrix, flattened, precision=HIGHEST)
    return result.reshape(matrix.shape[0], volume.shape[1], volume.shape[2])


def shards(estimate0, pieces, dest_block, slot_index, psf_shift, psf_taps, background):
    block_count = lax.axis_size("block")
    view_count = lax.axis_size("view")
    my_view = lax.axis_index("view")
    my_block = lax.axis_index("block")
    slab_depth = estimate0.shape[0]
    plane_rows = estimate0.shape[1]
    plane_columns = estimate0.shape[2]
    slot_count = pieces.shape[1]
    piece_depth = pieces.shape[2]
    plane_size = piece_depth * plane_rows * plane_columns
    kernel = psf_taps / jnp.sum(psf_taps, axis=2, keepdims=True)
    own_kernel = lax.dynamic_index_in_dim(kernel, my_view, 0, keepdims=False)
    own_shift = lax.dynamic_index_in_dim(psf_shift, my_view, 0, keepdims=False)
    offset = lax.dynamic_index_in_dim(background, my_view, 0, keepdims=False)
    band_rows = band_matrix(own_kernel[1], own_shift[1], plane_rows, plane_rows, 0)
    band_columns = band_matrix(own_kernel[2], own_shift[2], plane_columns, plane_columns, 0)
    targets = dest_block[:, :, 0]
    global_slot = targets * slot_count + slot_index
    slot_total = block_count * slot_count
    slot_hits = (
        global_slot[:, :, None] == jnp.arange(slot_total, dtype=jnp.int32)[None, None, :]
    ).astype(jnp.int32)
    counts_all = jnp.sum(slot_hits, axis=1)
    view_targets = lax.dynamic_index_in_dim(targets, my_view, 0, keepdims=False).reshape(
        block_count, slot_count
    )
    view_slots = lax.dynamic_index_in_dim(slot_index, my_view, 0, keepdims=False).reshape(
        block_count, slot_count
    )
    earlier = lax.broadcasted_iota(jnp.int32, (slot_count, slot_count), 1) < lax.broadcasted_iota(
        jnp.int32, (slot_count, slot_count), 0
    )
    same_target = view_targets[:, :, None] == view_targets[:, None, :]
    ranks = jnp.sum((same_target & earlier[None, :, :]).astype(jnp.int32), axis=2)
    own_targets = lax.dynamic_index_in_dim(view_targets, my_block, 0, keepdims=False)
    own_ranks = lax.dynamic_index_in_dim(ranks, my_block, 0, keepdims=False)
    buffer_slots = jnp.arange(block_count * CAP, dtype=jnp.int32)
    chooser = (buffer_slots[:, None] == (own_targets * CAP + own_ranks)[None, :]).astype(
        jnp.bfloat16
    )
    outgoing = jnp.dot(
        chooser, pieces[0].reshape(slot_count, plane_size), preferred_element_type=jnp.float32
    )
    outgoing = outgoing.astype(jnp.bfloat16).reshape(block_count, CAP * plane_size)
    incoming = lax.all_to_all(outgoing, "block", split_axis=0, concat_axis=0, tiled=True)
    sources = lax.broadcasted_iota(jnp.int32, (block_count, slot_count), 0)
    column_index = jnp.where(view_targets == my_block, sources * CAP + ranks, -1)
    slot_match = (
        view_slots[:, :, None] == jnp.arange(slot_count, dtype=jnp.int32)[None, None, :]
    ).astype(jnp.float32)
    column_match = (column_index[:, :, None] == buffer_slots[None, None, :]).astype(jnp.float32)
    placement = jnp.einsum("sjt,sjc->tc", slot_match, column_match)
    placed = jnp.dot(
        placement.astype(jnp.bfloat16),
        incoming.reshape(block_count * CAP, plane_size),
        preferred_element_type=jnp.float32,
    )
    view_counts = lax.dynamic_index_in_dim(counts_all, my_view, 0, keepdims=False)
    slab_counts = lax.dynamic_slice_in_dim(view_counts, my_block * slot_count, slot_count)
    average = placed / jnp.maximum(slab_counts, 1).astype(jnp.float32)[:, None]
    average = average.reshape(slab_depth, plane_rows, plane_columns)

    def depth_adjoint(one_kernel, one_shift):
        return band_matrix(one_kernel, one_shift, slab_depth + 2 * HALO, slab_depth, -HALO).T

    plane_mask = jnp.repeat((counts_all > 0).astype(jnp.float32), piece_depth, axis=1)
    padded_mask = jnp.pad(plane_mask, ((0, 0), (HALO, HALO)))
    window = lax.dynamic_slice_in_dim(padded_mask, my_block * slab_depth, slab_depth + 2 * HALO, 1)
    adjoint_all = jax.vmap(depth_adjoint)(kernel[:, 0], psf_shift[:, 0])
    weight_depth = jnp.einsum("vze,ve->vz", adjoint_all, window, precision=HIGHEST)
    weight_rows = column_sums(kernel[:, 1], psf_shift[:, 1], plane_rows)
    weight_columns = column_sums(kernel[:, 2], psf_shift[:, 2], plane_columns)
    weight = jnp.einsum(
        "vz,vy,vx->zyx", weight_depth, weight_rows, weight_columns, precision=HIGHEST
    )
    floor_weight = jnp.maximum(weight, 1.0)
    backward_depth = depth_adjoint(own_kernel[0], own_shift[0])
    rim_width = HALO
    forward_depth = band_matrix(
        own_kernel[0], own_shift[0], slab_depth, slab_depth + 2 * HALO, HALO
    )
    share_rows = plane_rows // view_count
    estimate_share = lax.dynamic_slice_in_dim(estimate0, my_view * share_rows, share_rows, 1)
    weight_share = lax.dynamic_slice_in_dim(floor_weight, my_view * share_rows, share_rows, 1)
    for iteration in range(ITERS):
        rim_cells = with_halo(
            estimate_share.astype(jnp.bfloat16), (("block", 0),), rim_width
        ).astype(estimate_share.dtype)
        extended = lax.all_gather(
            rim_cells.astype(jnp.bfloat16), "view", axis=1, tiled=True
        ).astype(rim_cells.dtype)
        blurred = blur_plane(along_depth(forward_depth, extended), band_rows, band_columns) + offset
        quotient = average / blurred
        partial_value = adjoint_plane(quotient, band_rows, band_columns)
        widened = with_halo(partial_value.astype(jnp.bfloat16), (("block", 0),), HALO).astype(
            partial_value.dtype
        )
        summed = lax.psum_scatter(
            along_depth(backward_depth, widened), "view", scatter_dimension=1, tiled=True
        )
        estimate_share = estimate_share * summed / weight_share
    estimate = lax.all_gather(estimate_share, "view", axis=1, tiled=True)
    return estimate


def solution(mesh):
    return jax.shard_map(
        shards,
        mesh=mesh,
        in_specs=(
            P("block", None, None),
            P("view", "block", None, None, None),
            P(),
            P(),
            P(),
            P(),
            P(),
        ),
        out_specs=P("block", None, None),
        check_vma=False,
    )
```

profile of v0, /device:TPU:0, one launch (start us, length us, event | category | flops | bytes accessed | tf_op | source)
XLA Modules:
  0.0 413.8 jit_solution(15959017639147534249)
XLA Ops:
  6.5 1.3 constant_dynamic-slice_fusion.8
  8.5 4.8 %collective-permute-start = (bf16[13,16,256]{2,0,1:T(8,128)(2,1)S(1)}, bf16[13,16,256]{2,0,1:T(8,128)(2,1)S(1)}, u32[]{:S(2)}, u32[]{:S(2)}) collective-permute-start(bf16[13,16,256]{2,0,1:T(8,128)(2,1)S(1)} %get-tuple-element.16), channel_id=1, source_target_pairs={{0,1},{1,2},{2,3},{3,4},{4,5},{5,6},{6,7},{8,9},{9,10},{10,11},{11... | collective-permute-start | bytes 319496 | tf_op jit(solution)/shard_map/ppermute | solution.py:22
  13.3 1.3 collective-permute-start.1
  14.8 3.2 reshape_squeeze.3
  18.2 1.9 collective-permute-done.1
  21.8 2.3 convolution_convert_fusion
  24.1 4.5 %all_to_all.8 = bf16[8,1,131072]{2,1,0:T(2,128)(2,1)} reshape(bf16[16,65536]{1,0:T(8,128)(2,1)S(1)} %convolution_convert_fusion) | data formatting | bytes 4194304 | tf_op jit(solution)/shard_map/all_to_all | solution.py:119
  29.1 13.1 %reduce.15 = bf16[8,131072]{1,0:T(8,128)(2,1)S(1)} reduce(bf16[8,1,131072]{2,1,0:T(2,128)(2,1)} %all_to_all.8, bf16[]{:T(256)} %broadcast.164), dimensions={1}, to_apply=%all_to_all.8.reduce_sub_computation | reduce | bytes 4194306 | tf_op jit(solution)/shard_map/all_to_all | solution.py:119
  42.2 3.2 reshape.239
  45.4 6.0 %all-to-all-start = ((bf16[8,2,65536]{2,1,0:T(2,128)(2,1)}), bf16[8,2,65536]{2,1,0:T(2,128)(2,1)S(1)}, u32[]{:S(2)}, u32[]{:S(2)}) async-start(bf16[8,2,65536]{2,1,0:T(2,128)(2,1)} %reshape.239), calls=%async_computation | async-start | bytes 4194304 | tf_op jit(solution)/shard_map/all_to_all | solution.py:119
  56.4 42.2 %all-to-all-done = bf16[8,2,65536]{2,1,0:T(2,128)(2,1)S(1)} async-done(((bf16[8,2,65536]{2,1,0:T(2,128)(2,1)}), bf16[8,2,65536]{2,1,0:T(2,128)(2,1)S(1)}, u32[]{:S(2)}, u32[]{:S(2)}) %all-to-all-start) | async-done | bytes 2097184 | tf_op jit(solution)/shard_map/all_to_all | solution.py:119
  98.6 4.3 %reshape.240 = bf16[8,1,131072]{2,1,0:T(2,128)(2,1)} reshape(bf16[8,2,65536]{2,1,0:T(2,128)(2,1)S(1)} %all-to-all-done) | data formatting | bytes 4194304
  102.9 12.4 %reduce.2 = bf16[8,131072]{1,0:T(8,128)(2,1)S(1)} reduce(bf16[8,1,131072]{2,1,0:T(2,128)(2,1)} %reshape.240, bf16[]{:T(256)} %constant.98), dimensions={1}, to_apply=%all_to_all.7.reduce_sub_computation | reduce | bytes 4194306 | tf_op jit(solution)/shard_map/all_to_all | solution.py:119
  115.3 2.2 reshape.206
  117.5 4.5 %convolution_divide_fusion = f32[16,65536]{1,0:T(8,128)} fusion(bf16[16,65536]{1,0:T(8,128)(2,1)} %reshape.206, f32[16]{0:T(128)S(1)} %convert_bitcast_fusion, s32[8,16]{1,0:T(8,128)S(1)} %add_select_fusion, s32[8,16]{1,0:T(8,128)S(1)} %eq.147), kind=kOutput, calls=%fused_computation.1 | convolution fusion | flops 34672896 | bytes 6292544 | tf_op jit(solution)/shard_map/dot_general | solution.py:127
  122.0 3.8 reshape.207
  125.8 2.2 slice_bitcast_fusion.3
  128.0 3.2 fusion.24
  131.2 6.7 %fusion.10 = f32[64,256,64]{1,2,0:T(8,128)S(1)} fusion(f32[64,64,256]{2,0,1:T(8,128)S(1)} %fusion.24, f32[64,64]{1,0:T(8,128)S(1)} %select_reduce_fusion.2), kind=kOutput, calls=%fused_computation.14 | convolution fusion | flops 805306368 | bytes 8404992 | tf_op jit(solution)/shard_map/yv,zvx->zyx/dot_general | solution.py:59
  137.9 4.1 %fusion.6 = f32[64,64,256]{2,1,0:T(8,128)S(1)} fusion(f32[64,256,64]{1,2,0:T(8,128)S(1)} %fusion.10, f32[256,256]{1,0:T(8,128)S(1)} %select_reduce_fusion), kind=kOutput, calls=%fused_computation.10 | convolution fusion | flops 3221225472 | bytes 8650752 | tf_op jit(solution)/shard_map/zyv,xv->zyx/dot_general | solution.py:60
  142.1 5.3 %fusion.15 = f32[64,256,64]{1,2,0:T(8,128)S(1)} fusion(f32[64,64,256]{2,1,0:T(8,128)S(1)} %copy-done, f32[64,64,256]{2,1,0:T(8,128)S(1)} %fusion.6, f32[]{:T(128)} %bitcast.17, f32[64,64]{1,0:T(8,128)S(1)} %select_reduce_fusion.2), kind=kOutput, calls=%fused_computation.19 | convolution fusion | flops 807403520 | bytes 12599300 | tf_op jit(solution)/shard_map/vy,zvx->zyx/dot_general | solution.py:64
  147.4 3.6 fusion.28
  151.1 3.4 collective-permute-start.2
  154.5 1.3 collective-permute-start.3
  156.6 15.3 %collective-permute-done.2 = bf16[13,64,256]{2,1,0:T(8,128)(2,1)S(1)} collective-permute-done((bf16[13,64,256]{2,1,0:T(8,128)(2,1)S(1)}, bf16[13,64,256]{2,1,0:T(8,128)(2,1)S(1)}, u32[]{:S(2)}, u32[]{:S(2)}) %collective-permute-start.2) | collective-permute-done | bytes 426016 | tf_op jit(solution)/shard_map/ppermute | solution.py:22
  172.5 4.8 %fusion.22 = f32[64,64,256]{2,0,1:T(8,128)} fusion(bf16[64,256,90]{1,0,2:T(8,128)(2,1)S(1)} %slice_bitcast_fusion.2, f32[90,64]{0,1:T(8,128)S(1)} %select_reduce_fusion.4), kind=kOutput, calls=%fused_computation.26 | convolution fusion | flops 1132462080 | bytes 7166464 | tf_op jit(solution)/shard_map/dot_general | solution.py:70
  179.4 5.7 %fusion.40 = f32[64,64,256]{2,1,0:T(8,128)} fusion(f32[4,64]{1,0:T(4,128)S(1)} %bitcast.144, f32[4,64]{0,1:T(8,128)S(1)} %copy.53, f32[4,256]{1,0:T(4,128)S(1)} %select_reduce_fusion.5), kind=kOutput, calls=%fused_computation.64 | convolution fusion | flops 50348032 | bytes 4200448 | tf_op jit(solution)/shard_map/vz,vy,vx->zyx/dot_general | solution.py:147
  185.1 38.0 %reduce-scatter.3.cloned.1.call-done = f32[64,16,256]{2,0,1:T(8,128)} async-done(((f32[64,64,256]{2,0,1:T(8,128)}), f32[64,16,256]{2,0,1:T(8,128)}) %reduce-scatter.3.cloned.1.call-update) | async-done | bytes 1048592 | tf_op jit(solution)/shard_map/reduce_scatter | solution.py:172
  223.1 2.3 fusion.72
  225.4 3.4 collective-permute-start.4
  228.8 1.3 collective-permute-start.5
  230.1 1.4 collective-permute-done.4
  231.5 4.1 collective-permute-done.5
  237.4 27.3 %all-gather.6.cloned.1.call-done = bf16[90,64,256]{2,1,0:T(8,128)(2,1)} async-done(((bf16[90,16,256]{2,1,0:T(8,128)(2,1)}), bf16[90,64,256]{2,1,0:T(8,128)(2,1)}) %all-gather.6.cloned.1.call-update) | async-done | bytes 2949136 | tf_op jit(solution)/shard_map/all_gather | solution.py:163
  264.8 2.2 slice_bitcast_fusion.1
  267.0 3.2 fusion.20
  270.2 6.7 %fusion.8 = f32[64,256,64]{1,2,0:T(8,128)S(1)} fusion(f32[64,64,256]{2,0,1:T(8,128)S(1)} %fusion.20, f32[64,64]{1,0:T(8,128)S(1)} %select_reduce_fusion.2), kind=kOutput, calls=%fused_computation.12 | convolution fusion | flops 805306368 | bytes 8404992 | tf_op jit(solution)/shard_map/yv,zvx->zyx/dot_general | solution.py:59
  276.9 4.0 fusion.2
  280.9 5.3 %fusion.12 = f32[64,256,64]{1,2,0:T(8,128)S(1)} fusion(f32[64,64,256]{2,1,0:T(8,128)S(1)} %copy-done.1, f32[64,64,256]{2,1,0:T(8,128)S(1)} %fusion.2, f32[]{:T(128)} %bitcast.17, f32[64,64]{1,0:T(8,128)S(1)} %select_reduce_fusion.2), kind=kOutput, calls=%fused_computation.16 | convolution fusion | flops 807403520 | bytes 12599300 | tf_op jit(solution)/shard_map/vy,zvx->zyx/dot_general | solution.py:64
  286.2 3.6 fusion.31
  289.9 3.4 collective-permute-start.6
  293.3 1.3 collective-permute-start.7
  294.6 17.3 %collective-permute-done.6 = bf16[13,64,256]{2,1,0:T(8,128)(2,1)S(1)} collective-permute-done((bf16[13,64,256]{2,1,0:T(8,128)(2,1)S(1)}, bf16[13,64,256]{2,1,0:T(8,128)(2,1)S(1)}, u32[]{:S(2)}, u32[]{:S(2)}) %collective-permute-start.6) | collective-permute-done | bytes 426016 | tf_op jit(solution)/shard_map/ppermute | solution.py:22
  312.5 4.8 %fusion.18 = f32[64,64,256]{2,0,1:T(8,128)} fusion(bf16[64,256,90]{1,0,2:T(8,128)(2,1)S(1)} %slice_bitcast_fusion, f32[90,64]{0,1:T(8,128)S(1)} %select_reduce_fusion.4), kind=kOutput, calls=%fused_computation.22 | convolution fusion | flops 1132462080 | bytes 7166464 | tf_op jit(solution)/shard_map/dot_general | solution.py:70
  317.5 45.4 %reduce-scatter.5.cloned.1.call-done = f32[64,16,256]{2,0,1:T(8,128)} async-done(((f32[64,64,256]{2,0,1:T(8,128)}), f32[64,16,256]{2,0,1:T(8,128)}) %reduce-scatter.5.cloned.1.call-update) | async-done | bytes 1048592 | tf_op jit(solution)/shard_map/reduce_scatter | solution.py:172
  362.9 2.8 multiply_divide_fusion
  365.7 34.7 %all-gather.8.cloned.1.call-done = f32[64,64,256]{2,0,1:T(8,128)} async-done(((f32[64,16,256]{2,0,1:T(8,128)}), f32[64,64,256]{2,0,1:T(8,128)}) %all-gather.8.cloned.1.call-update) | async-done | bytes 4194320 | tf_op jit(solution)/shard_map/all_gather | solution.py:176
  400.3 6.6 %copy.60 = f32[64,64,256]{2,1,0:T(8,128)} copy(f32[64,64,256]{2,0,1:T(8,128)} %all-gather.8.cloned.1.call-done) | data formatting | bytes 8388608 | tf_op jit(solution)/shard_map/all_gather | solution.py:176
  (85 shorter events, 14.4 us)
Async XLA Ops:
  6.5 8.1 %copy-start.4 = (s32[4,128,1]{1,2,0:T(1,128)S(1)}, s32[4,128,1]{1,2,0:T(1,128)}, u32[]{:S(2)}) copy-start(s32[4,128,1]{1,2,0:T(1,128)} %param.9) | copy-start | bytes 6148
  6.5 119.2 %all-gather.4.cloned.1.call-start = ((), (), s32[]{:S(2)}) async-start(), calls=%async_computation.3 | async-start | bytes 3686400 | tf_op jit(solution)/shard_map/all_gather | solution.py:163
  8.5 9.8 %collective-permute-start = (bf16[13,16,256]{2,0,1:T(8,128)(2,1)S(1)}, bf16[13,16,256]{2,0,1:T(8,128)(2,1)S(1)}, u32[]{:S(2)}, u32[]{:S(2)}) collective-permute-start(bf16[13,16,256]{2,0,1:T(8,128)(2,1)S(1)} %get-tuple-element.16), channel_id=1, source_target_pairs={{0,1},{1,2},{2,3},{3,4},{4,5},{5,6},{6,7},{8,9},{9,10},{10,11},{11... | collective-permute-start | bytes 319496 | tf_op jit(solution)/shard_map/ppermute | solution.py:22
  13.3 6.9 %collective-permute-start.1 = (bf16[13,16,256]{2,0,1:T(8,128)(2,1)S(1)}, bf16[13,16,256]{2,0,1:T(8,128)(2,1)S(1)}, u32[]{:S(2)}, u32[]{:S(2)}) collective-permute-start(bf16[13,16,256]{2,0,1:T(8,128)(2,1)S(1)} %get-tuple-element.17), channel_id=1, source_target_pairs={{1,0},{2,1},{3,2},{4,3},{5,4},{6,5},{7,6},{9,8},{10,9},{11,10},{12... | collective-permute-start | bytes 319496 | tf_op jit(solution)/shard_map/ppermute | solution.py:24
  45.3 6.3 %copy-start.6 = (f32[4]{0:T(128)S(1)}, f32[4]{0:T(128)}, u32[]{:S(2)}) copy-start(f32[4]{0:T(128)} %param.13) | copy-start | bytes 52
  45.3 6.9 %copy-start.5 = (s32[4,128]{1,0:T(4,128)S(1)}, s32[4,128]{1,0:T(4,128)}, u32[]{:S(2)}) copy-start(s32[4,128]{1,0:T(4,128)} %param.10) | copy-start | bytes 6148
  45.4 7.0 %copy-start.2 = (f32[4,3,21]{2,0,1:T(4,128)S(1)}, f32[4,3,21]{2,0,1:T(4,128)}, u32[]{:S(2)}) copy-start(f32[4,3,21]{2,0,1:T(4,128)} %param.12) | copy-start | bytes 3028
  45.4 7.1 %copy-start.3 = (s32[4,3]{1,0:T(4,128)S(1)}, s32[4,3]{1,0:T(4,128)}, u32[]{:S(2)}) copy-start(s32[4,3]{1,0:T(4,128)} %param.11) | copy-start | bytes 148
  45.4 53.2 %all-to-all-start = ((bf16[8,2,65536]{2,1,0:T(2,128)(2,1)}), bf16[8,2,65536]{2,1,0:T(2,128)(2,1)S(1)}, u32[]{:S(2)}, u32[]{:S(2)}) async-start(bf16[8,2,65536]{2,1,0:T(2,128)(2,1)} %reshape.239), calls=%async_computation | async-start | bytes 4194304 | tf_op jit(solution)/shard_map/all_to_all | solution.py:119
  51.4 171.7 %reduce-scatter.3.cloned.1.call-start = ((), (), s32[]{:S(2)}) async-start(), calls=%async_computation.4 | async-start | bytes 5242880 | tf_op jit(solution)/shard_map/reduce_scatter | solution.py:172
  137.9 4.2 %copy-start = (f32[64,64,256]{2,1,0:T(8,128)S(1)}, f32[64,64,256]{2,1,0:T(8,128)}, u32[]{:S(2)}) copy-start(f32[64,64,256]{2,1,0:T(8,128)} %reshape.207) | copy-start | bytes 12582916
  151.1 20.8 %collective-permute-start.2 = (bf16[13,64,256]{2,1,0:T(8,128)(2,1)S(1)}, bf16[13,64,256]{2,1,0:T(8,128)(2,1)S(1)}, u32[]{:S(2)}, u32[]{:S(2)}) collective-permute-start(bf16[13,64,256]{2,1,0:T(8,128)(2,1)S(1)} %get-tuple-element.12), channel_id=1, source_target_pairs={{0,1},{1,2},{2,3},{3,4},{4,5},{5,6},{6,7},{8,9},{9,10},{10,11},{11... | collective-permute-start | bytes 1277960 | tf_op jit(solution)/shard_map/ppermute | solution.py:22
  154.5 17.4 %collective-permute-start.3 = (bf16[13,64,256]{2,1,0:T(8,128)(2,1)S(1)}, bf16[13,64,256]{2,1,0:T(8,128)(2,1)S(1)}, u32[]{:S(2)}, u32[]{:S(2)}) collective-permute-start(bf16[13,64,256]{2,1,0:T(8,128)(2,1)S(1)} %get-tuple-element.13), channel_id=1, source_target_pairs={{1,0},{2,1},{3,2},{4,3},{5,4},{6,5},{7,6},{9,8},{10,9},{11,10},{12... | collective-permute-start | bytes 1277960 | tf_op jit(solution)/shard_map/ppermute | solution.py:24
  177.3 87.5 %all-gather.6.cloned.1.call-start = ((), (), s32[]{:S(2)}) async-start(), calls=%async_computation.5 | async-start | bytes 3686400 | tf_op jit(solution)/shard_map/all_gather | solution.py:163
  225.4 6.1 %collective-permute-start.4 = (bf16[13,16,256]{2,0,1:T(8,128)(2,1)S(1)}, bf16[13,16,256]{2,0,1:T(8,128)(2,1)S(1)}, u32[]{:S(2)}, u32[]{:S(2)}) collective-permute-start(bf16[13,16,256]{2,0,1:T(8,128)(2,1)S(1)} %get-tuple-element.14), channel_id=1, source_target_pairs={{0,1},{1,2},{2,3},{3,4},{4,5},{5,6},{6,7},{8,9},{9,10},{10,11},{11... | collective-permute-start | bytes 319496 | tf_op jit(solution)/shard_map/ppermute | solution.py:22
  228.8 6.9 %collective-permute-start.5 = (bf16[13,16,256]{2,0,1:T(8,128)(2,1)S(1)}, bf16[13,16,256]{2,0,1:T(8,128)(2,1)S(1)}, u32[]{:S(2)}, u32[]{:S(2)}) collective-permute-start(bf16[13,16,256]{2,0,1:T(8,128)(2,1)S(1)} %get-tuple-element.15), channel_id=1, source_target_pairs={{1,0},{2,1},{3,2},{4,3},{5,4},{6,5},{7,6},{9,8},{10,9},{11,10},{12... | collective-permute-start | bytes 319496 | tf_op jit(solution)/shard_map/ppermute | solution.py:24
  237.2 125.7 %reduce-scatter.5.cloned.1.call-start = ((), (), s32[]{:S(2)}) async-start(), calls=%async_computation.6 | async-start | bytes 5242880 | tf_op jit(solution)/shard_map/reduce_scatter | solution.py:172
  276.9 4.0 copy-start.1
  289.9 22.0 %collective-permute-start.6 = (bf16[13,64,256]{2,1,0:T(8,128)(2,1)S(1)}, bf16[13,64,256]{2,1,0:T(8,128)(2,1)S(1)}, u32[]{:S(2)}, u32[]{:S(2)}) collective-permute-start(bf16[13,64,256]{2,1,0:T(8,128)(2,1)S(1)} %get-tuple-element.10), channel_id=1, source_target_pairs={{0,1},{1,2},{2,3},{3,4},{4,5},{5,6},{6,7},{8,9},{9,10},{10,11},{11... | collective-permute-start | bytes 1277960 | tf_op jit(solution)/shard_map/ppermute | solution.py:22
  293.3 18.6 %collective-permute-start.7 = (bf16[13,64,256]{2,1,0:T(8,128)(2,1)S(1)}, bf16[13,64,256]{2,1,0:T(8,128)(2,1)S(1)}, u32[]{:S(2)}, u32[]{:S(2)}) collective-permute-start(bf16[13,64,256]{2,1,0:T(8,128)(2,1)S(1)} %get-tuple-element.11), channel_id=1, source_target_pairs={{1,0},{2,1},{3,2},{4,3},{5,4},{6,5},{7,6},{9,8},{10,9},{11,10},{12... | collective-permute-start | bytes 1277960 | tf_op jit(solution)/shard_map/ppermute | solution.py:24
  317.2 83.1 %all-gather.8.cloned.1.call-start = ((), (), s32[]{:S(2)}) async-start(), calls=%async_computation.7 | async-start | bytes 5242880 | tf_op jit(solution)/shard_map/all_gather | solution.py:176
Sparse Core Ops, SparseCore 0:
  21.9 28.5 all-gather.3
  177.4 45.6 reduce-scatter.2
  237.3 27.3 all-gather.5
  317.4 45.4 reduce-scatter.4
  365.8 34.4 all-gather.7
where the time goes:
time: 421 us; the launch traced here: 414 us
  waiting for transfers between devices  228 us (54%)
  matrix products  68.1 us (16%)
  local copies, waits for them, and re-layouts  40.2 us (10%)
  other arithmetic  37 us (9%)
  starting transfers between devices  27 us (6%)
  between operations  13.9 us (3%)
    reduce_scatter x2, waiting for transfers between devices, shards(): lax.psum_scatter(along_depth(backward_depth, widened), 'view', scatter_di...  83.3 us
    all_to_all x1, waiting for transfers between devices, shards(): lax.all_to_all(outgoing, 'block', split_axis=0, concat_axis=0, tiled=True)  42.2 us
    all_gather x1, waiting for transfers between devices, shards(): estimate = lax.all_gather(estimate_share, 'view', axis=1, tiled=True)  34.7 us
    ppermute x4, waiting for transfers between devices, with_halo(): lax.ppermute(tail, axis, [(i, (i + 1) % count) for i in range(ends)])  34 us
    all_gather x2, waiting for transfers between devices, shards(): lax.all_gather(rim_cells.astype(jnp.bfloat16), 'view', axis=1, tiled=True)  27.3 us
    all_to_all x2, other arithmetic, shards(): lax.all_to_all(outgoing, 'block', split_axis=0, concat_axis=0, tiled=True)  25.4 us
    dot_general x4, matrix products, along_depth(): result = jnp.dot(matrix, flattened, precision=HIGHEST)  16 us
    ppermute x4, starting transfers between devices, with_halo(): lax.ppermute(tail, axis, [(i, (i + 1) % count) for i in range(ends)])  15 us
  transfers between devices with their start and end apart: 14, of which 10 were waited for; matrix products, arithmetic and copies ran while one was open for 15% of the time, Pallas kernels for 0%

commit v1 on v0

v1 whole, which is shorter than its diff:
```python
import functools

import jax
import jax.numpy as jnp
from jax import lax
from jax.experimental import pallas as pl
from jax.experimental.pallas import tpu as pltpu
from jax.sharding import PartitionSpec as P

CAP = 2
ITERS = 2
HALO = 13
EDGE = 16
CORES = 2
LANES = 128

HIGHEST = lax.Precision.HIGHEST
BF16 = jnp.bfloat16
F32 = jnp.float32


def band_matrix(kernel, shift, row_count, column_count, lead_offset):
    tap_count = kernel.shape[0]
    radius = (tap_count - 1) // 2
    difference = (
        lax.broadcasted_iota(jnp.int32, (row_count, column_count), 1)
        - lax.broadcasted_iota(jnp.int32, (row_count, column_count), 0)
        - lead_offset
        - shift
        + radius
    )
    band = jnp.zeros((row_count, column_count), F32)
    for tap in range(tap_count):
        band = jnp.where(difference == tap, kernel[tap], band)
    return band


def column_sums(kernel, shift, length):
    tap_count = kernel.shape[-1]
    radius = (tap_count - 1) // 2
    source = (
        jnp.arange(length, dtype=jnp.int32)[None, :, None]
        - shift[:, None, None]
        - jnp.arange(tap_count, dtype=jnp.int32)[None, None, :]
        + radius
    )
    inside = (source >= 0) & (source < length)
    return jnp.sum(jnp.where(inside, kernel[:, None, :], 0.0), axis=2)


def copy_body(index_ref, piece_ref, out_ref):
    out_ref[...] = piece_ref[...]


def pick_pieces(pieces, index):
    block = (1,) + pieces.shape[1:]
    return pl.pallas_call(
        copy_body,
        grid_spec=pltpu.PrefetchScalarGridSpec(
            num_scalar_prefetch=1,
            grid=(index.shape[0],),
            in_specs=[pl.BlockSpec(block, lambda i, s: (s[i], 0, 0))],
            out_specs=pl.BlockSpec(block, lambda i, s: (i, 0, 0)),
        ),
        out_shape=jax.ShapeDtypeStruct((index.shape[0],) + pieces.shape[1:], pieces.dtype),
        name="pick_pieces",
    )(index, pieces)


def place_body(order_ref, start_ref, scale_ref, incoming_ref, out_ref):
    view, slot = pl.program_id(0), pl.program_id(1)
    out_ref[...] = jnp.zeros_like(out_ref)

    def add(k, carry):
        out_ref[0, 0] += incoming_ref[0, order_ref[view, k]].astype(F32)
        return carry

    lax.fori_loop(start_ref[view, slot], start_ref[view, slot + 1], add, 0)
    out_ref[...] = out_ref[...] * scale_ref[view, slot]


def place_pieces(incoming, order, start, scale):
    views, slots = scale.shape
    tail = incoming.shape[2:]
    return pl.pallas_call(
        place_body,
        grid=(views, slots),
        in_specs=[
            pl.BlockSpec(memory_space=pltpu.SMEM),
            pl.BlockSpec(memory_space=pltpu.SMEM),
            pl.BlockSpec(memory_space=pltpu.SMEM),
            pl.BlockSpec((1,) + incoming.shape[1:], lambda v, t: (v, 0, 0, 0)),
        ],
        out_specs=pl.BlockSpec((1, 1) + tail, lambda v, t: (v, t, 0, 0)),
        out_shape=jax.ShapeDtypeStruct((views, slots) + tail, F32),
        compiler_params=pltpu.CompilerParams(vmem_limit_bytes=48 * 2**20),
        name="place_pieces",
    )(order, start, scale, incoming)


def split_columns(volume):
    return jnp.stack(jnp.split(volume, volume.shape[-1] // LANES, axis=-1))


def take_rows(ref, y, rows):
    halves, total = ref.shape[:2]
    return jnp.concatenate(
        [ref[h, pl.ds(y, total // rows, stride=rows), :].astype(BF16) for h in range(halves)],
        axis=1,
    )


def forward_body(offset_ref, depth_ref, rows_ref, columns_ref, volume_ref, out_ref, source, middle):
    view = pl.program_id(0)
    halves, depth_in, rows, _ = volume_ref.shape
    depth = out_ref.shape[1]

    @pl.when(view == 0)
    def _():
        for h in range(halves):

            def widen(z, carry):
                source[h, pl.ds(pl.multiple_of(z * rows, rows), rows), :] = volume_ref[h, z].astype(F32)
                return carry

            lax.fori_loop(0, depth_in, widen, 0, unroll=8)

    def row(y, carry):
        column = take_rows(source, y, rows)
        blurred = jnp.dot(depth_ref[0], column, preferred_element_type=F32).astype(BF16)
        blurred = jnp.dot(blurred, columns_ref[0], preferred_element_type=F32)
        for h in range(halves):
            middle[h, pl.ds(y, depth, stride=rows), :] = blurred[:, h * LANES : (h + 1) * LANES]
        return carry

    lax.fori_loop(0, rows, row, 0, unroll=8)

    def plane(z, carry):
        span = pl.ds(pl.multiple_of(z * rows, rows), rows)
        cells = jnp.concatenate([middle[h, span, :].astype(BF16) for h in range(halves)], axis=1)
        out_ref[0, z] = (
            jnp.dot(rows_ref[0], cells, preferred_element_type=F32) + offset_ref[view]
        )
        return carry

    lax.fori_loop(0, depth, plane, 0, unroll=8)


def forward(volume, offset, depth_bands, row_bands, column_bands):
    views, depth = depth_bands.shape[:2]
    halves, depth_in, rows, _ = volume.shape
    width = halves * LANES
    matrix = lambda a: pl.BlockSpec((1,) + a.shape[1:], lambda v: (v, 0, 0))
    return pl.pallas_call(
        forward_body,
        grid=(views,),
        in_specs=[
            pl.BlockSpec(memory_space=pltpu.SMEM),
            matrix(depth_bands),
            matrix(row_bands),
            matrix(column_bands),
            pl.BlockSpec(volume.shape, lambda v: (0, 0, 0, 0)),
        ],
        out_specs=pl.BlockSpec((1, depth, rows, width), lambda v: (v, 0, 0, 0)),
        out_shape=jax.ShapeDtypeStruct((views, depth, rows, width), F32),
        scratch_shapes=[
            pltpu.VMEM((halves, depth_in * rows, LANES), F32),
            pltpu.VMEM((halves, depth * rows, LANES), F32),
        ],
        compiler_params=pltpu.CompilerParams(vmem_limit_bytes=48 * 2**20),
        cost_estimate=pl.CostEstimate(
            flops=2 * views * depth * rows * width * (depth_in + rows + width) * 4,
            bytes_accessed=4 * (views * depth + depth_in) * rows * width,
            transcendentals=0,
        ),
        name="forward_blur",
    )(offset, depth_bands, row_bands, column_bands, volume)


def backward_body(depth_ref, rows_ref, columns_ref, average_ref, blurred_ref, out_ref, middle):
    view = pl.program_id(0)
    _, depth, rows, _ = average_ref.shape
    halves = out_ref.shape[0]
    depth_out = out_ref.shape[1] // rows

    def plane(z, carry):
        quotient = (average_ref[0, z] / blurred_ref[0, z]).astype(BF16)
        cells = jnp.dot(rows_ref[0], quotient, preferred_element_type=F32)
        span = pl.ds(pl.multiple_of(z * rows, rows), rows)
        for h in range(halves):
            middle[h, span, :] = cells[:, h * LANES : (h + 1) * LANES]
        return carry

    lax.fori_loop(0, depth, plane, 0, unroll=8)

    def spread(y):
        column = take_rows(middle, y, rows)
        column = jnp.dot(column, columns_ref[0], preferred_element_type=F32).astype(BF16)
        return jnp.dot(depth_ref[0], column, preferred_element_type=F32)

    @pl.when(view == 0)
    def _():
        def row(y, carry):
            cells = spread(y)
            for h in range(halves):
                out_ref[h, pl.ds(y, depth_out, stride=rows), :] = cells[:, h * LANES : (h + 1) * LANES]
            return carry

        lax.fori_loop(0, rows, row, 0, unroll=8)

    @pl.when(view > 0)
    def _():
        def row(y, carry):
            cells = spread(y)
            for h in range(halves):
                out_ref[h, pl.ds(y, depth_out, stride=rows), :] += cells[:, h * LANES : (h + 1) * LANES]
            return carry

        lax.fori_loop(0, rows, row, 0, unroll=8)


def backward(average, blurred, depth_bands, row_bands, column_bands):
    views, depth_out = depth_bands.shape[:2]
    _, depth, rows, width = blurred.shape
    halves = width // LANES
    matrix = lambda a: pl.BlockSpec((1,) + a.shape[1:], lambda v: (v, 0, 0))
    whole = pl.BlockSpec((1, depth, rows, width), lambda v: (v, 0, 0, 0))
    out = pl.pallas_call(
        backward_body,
        grid=(views,),
        in_specs=[matrix(depth_bands), matrix(row_bands), matrix(column_bands), whole, whole],
        out_specs=pl.BlockSpec((halves, depth_out * rows, LANES), lambda v: (0, 0, 0)),
        out_shape=jax.ShapeDtypeStruct((halves, depth_out * rows, LANES), F32),
        scratch_shapes=[pltpu.VMEM((halves, depth * rows, LANES), F32)],
        compiler_params=pltpu.CompilerParams(vmem_limit_bytes=56 * 2**20),
        name="backward_blur",
    )(depth_bands, row_bands, column_bands, average, blurred)
    return out.reshape(halves, depth_out, rows, LANES)


def shards(estimate0, pieces, dest_block, slot_index, psf_shift, psf_taps, background):
    block_count = lax.axis_size("block")
    view_count = lax.axis_size("view")
    my_view = lax.axis_index("view")
    my_block = lax.axis_index("block")
    slab_depth, plane_rows, plane_columns = estimate0.shape
    slot_count = pieces.shape[1]
    piece_depth = pieces.shape[2]
    chips = view_count // CORES
    my_core = lax.rem(my_view, CORES)

    def of_own_views(cells):
        return jnp.concatenate(
            [
                lax.dynamic_slice_in_dim(cells, lax.rem(my_view + CORES * hop, view_count), 1, 0)
                for hop in range(chips)
            ]
        )

    targets = dest_block[:, :, 0].reshape(view_count, block_count, slot_count)
    slots = slot_index.reshape(view_count, block_count, slot_count)
    earlier = lax.broadcasted_iota(jnp.int32, (slot_count, slot_count), 1) < lax.broadcasted_iota(
        jnp.int32, (slot_count, slot_count), 0
    )
    here = lax.dynamic_slice(targets, (my_view, my_block, 0), (1, 1, slot_count))[0, 0]
    here_rank = jnp.sum(((here[:, None] == here[None, :]) & earlier).astype(jnp.int32), axis=1)
    buffer_slots = jnp.arange(block_count * CAP, dtype=jnp.int32)
    hit = buffer_slots[:, None] == (here * CAP + here_rank)[None, :]
    pick = jnp.sum(
        jnp.where(hit, lax.broadcasted_iota(jnp.int32, hit.shape, 1), 0), axis=1
    )
    outgoing = pick_pieces(
        pieces.reshape(slot_count, piece_depth * plane_rows, plane_columns), pick
    ).reshape(block_count, CAP, piece_depth * plane_rows, plane_columns)
    incoming = lax.all_to_all(outgoing, "block", split_axis=0, concat_axis=0, tiled=True)
    incoming = incoming.reshape(block_count * CAP, piece_depth * plane_rows, plane_columns)
    arrived = [incoming]
    for hop in range(1, chips):
        arrived.append(
            lax.ppermute(
                incoming,
                "view",
                [((v + CORES * hop) % view_count, v) for v in range(view_count)],
            )
        )
    arrived = jnp.stack(arrived)

    view_targets = of_own_views(targets)
    view_slots = of_own_views(slots)
    ranks = jnp.sum(
        ((view_targets[..., :, None] == view_targets[..., None, :]) & earlier).astype(jnp.int32),
        axis=-1,
    )
    column = jnp.where(
        view_targets == my_block,
        lax.broadcasted_iota(jnp.int32, view_targets.shape, 1) * CAP + ranks,
        -1,
    )
    matches = column[..., None] == buffer_slots
    slot_of = jnp.sum(jnp.where(matches, view_slots[..., None] + 1, 0), axis=(1, 2)) - 1
    slot_of = jnp.where(slot_of < 0, slot_count, slot_of)
    before = (slot_of[:, None, :] < slot_of[:, :, None]) | (
        (slot_of[:, None, :] == slot_of[:, :, None])
        & (buffer_slots[None, None, :] < buffer_slots[None, :, None])
    )
    position = jnp.sum(before.astype(jnp.int32), axis=2)
    order = jnp.sum(
        jnp.where(
            position[:, None, :] == buffer_slots[None, :, None], buffer_slots[None, None, :], 0
        ),
        axis=2,
    )
    thresholds = jnp.arange(slot_count + 1, dtype=jnp.int32)
    start = jnp.sum((slot_of[:, None, :] < thresholds[None, :, None]).astype(jnp.int32), axis=2)
    slab_counts = start[:, 1:] - start[:, :-1]
    scale = 1.0 / jnp.maximum(slab_counts, 1).astype(F32)
    average = place_pieces(arrived, order, start, scale)
    average = average.reshape(chips, slab_depth, plane_rows, plane_columns)

    kernel = psf_taps / jnp.sum(psf_taps, axis=2, keepdims=True)
    own_kernel = of_own_views(kernel)
    own_shift = of_own_views(psf_shift)
    own_offset = of_own_views(background)
    wide_depth = slab_depth + 2 * EDGE

    def bands(one_kernel, one_shift):
        return (
            band_matrix(one_kernel[0], one_shift[0], slab_depth, wide_depth, EDGE).astype(BF16),
            band_matrix(one_kernel[1], one_shift[1], plane_rows, plane_rows, 0).astype(BF16),
            band_matrix(one_kernel[2], one_shift[2], plane_columns, plane_columns, 0).astype(BF16),
        )

    depth_bands, row_bands, column_bands = jax.vmap(bands)(own_kernel, own_shift)
    depth_back = jnp.swapaxes(depth_bands, 1, 2)
    rows_back = jnp.swapaxes(row_bands, 1, 2)
    columns_forward = jnp.swapaxes(column_bands, 1, 2)

    global_slot = targets * slot_count + slots
    slot_total = block_count * slot_count
    counts_all = jnp.sum(
        (
            global_slot.reshape(view_count, slot_total)[:, :, None]
            == jnp.arange(slot_total, dtype=jnp.int32)[None, None, :]
        ).astype(jnp.int32),
        axis=1,
    )
    plane_mask = jnp.repeat((counts_all > 0).astype(F32), piece_depth, axis=1)
    padded_mask = jnp.pad(plane_mask, ((0, 0), (HALO, HALO)))
    window = lax.dynamic_slice_in_dim(padded_mask, my_block * slab_depth, slab_depth + 2 * HALO, 1)

    def depth_adjoint(one_kernel, one_shift):
        return band_matrix(one_kernel, one_shift, slab_depth + 2 * HALO, slab_depth, -HALO).T

    adjoint_all = jax.vmap(depth_adjoint)(kernel[:, 0], psf_shift[:, 0])
    weight_depth = jnp.einsum("vze,ve->vz", adjoint_all, window, precision=HIGHEST)
    weight_rows = column_sums(kernel[:, 1], psf_shift[:, 1], plane_rows)
    weight_columns = column_sums(kernel[:, 2], psf_shift[:, 2], plane_columns)
    weight_columns = lax.dynamic_slice_in_dim(weight_columns, my_core * LANES, LANES, 1)
    weight = 0.0
    for view in range(view_count):
        weight = weight + (
            weight_depth[view][:, None, None]
            * (weight_rows[view][:, None] * weight_columns[view][None, :])[None]
        )
    floor_weight = jnp.maximum(weight, 1.0)

    up = [(i, i + 1) for i in range(block_count - 1)]
    down = [(i + 1, i) for i in range(block_count - 1)]
    swap = [(v, v + 1 - 2 * (v % CORES)) for v in range(view_count)]

    def widen(cells):
        low = lax.ppermute(cells[slab_depth - HALO :], "block", up)
        high = lax.ppermute(cells[:HALO], "block", down)
        blank = jnp.zeros((EDGE - HALO,) + cells.shape[1:], cells.dtype)
        return jnp.concatenate([blank, low, cells, high, blank], axis=0)

    def pair(mine):
        theirs = lax.ppermute(mine, "view", swap)
        first = my_core == 0
        return jnp.where(first, mine, theirs), jnp.where(first, theirs, mine)

    def half(cells, core):
        return lax.dynamic_index_in_dim(cells, core, 0, keepdims=False)

    share = lax.dynamic_slice_in_dim(estimate0, my_core * LANES, LANES, 2)
    for iteration in range(ITERS):
        if iteration == 0:
            wide = split_columns(widen(estimate0.astype(BF16)))
        else:
            wide = jnp.stack(pair(widen(share.astype(BF16))))
        blurred = forward(wide, own_offset, depth_bands, row_bands, columns_forward)
        spread = backward(average, blurred, depth_back, rows_back, column_bands)
        total = half(spread, my_core) + lax.ppermute(half(spread, 1 - my_core), "view", swap)
        from_low = lax.ppermute(
            total[slab_depth + EDGE : slab_depth + EDGE + HALO], "block", up
        )
        from_high = lax.ppermute(total[EDGE - HALO : EDGE], "block", down)
        summed = total[EDGE : EDGE + slab_depth]
        summed = summed + jnp.concatenate(
            [
                from_low,
                jnp.zeros((slab_depth - 2 * HALO,) + from_low.shape[1:], F32),
                from_high,
            ],
            axis=0,
        )
        share = share * summed / floor_weight
    return jnp.concatenate(pair(share), axis=2)


def solution(mesh):
    return jax.shard_map(
        shards,
        mesh=mesh,
        in_specs=(
            P("block", None, None),
            P("view", "block", None, None, None),
            P(),
            P(),
            P(),
            P(),
            P(),
        ),
        out_specs=P("block", None, None),
        check_vma=False,
    )
```

time: 421 us -> 343 us (0.81); the launches traced: 414 us -> 342 us
  Pallas kernels: 0 us -> 160 us
  waiting for transfers between devices: 228 us -> 100 us
  matrix products: 68.1 us -> 0.63 us
  local copies, waits for them, and re-layouts: 40.2 us -> 17.1 us
  between operations: 13.9 us -> 0.57 us
  starting transfers between devices: 27 us -> 33.8 us
  other arithmetic: 37 us -> 30.3 us
    pallas_call x0 -> x6, Pallas kernels: none -> 160 us  [the longest x2 85.9 us: backward(): pl.pallas_call(backward_body, grid=(views,), in_specs=[matrix(depth_bands...]
    reduce_scatter x2 -> x0, waiting for transfers between devices: 83.3 us -> none  [shards(): lax.psum_scatter(along_depth(backward_depth, widened), 'view', scatter_di...]
    dot_general x15 -> x0, matrix products: 67.8 us -> none  [the longest x4 16 us: along_depth(): result = jnp.dot(matrix, flattened, precision=HIGHEST)]
    all_gather x3 -> x0, waiting for transfers between devices: 62 us -> none  [the longest x1 34.7 us: shards(): estimate = lax.all_gather(estimate_share, 'view', axis=1, tiled=True)]
    ppermute x8 -> x13, waiting for transfers between devices: 40.1 us -> 68.6 us  [the longest x2 34.2 us: shards(): lax.ppermute(total[slab_depth + EDGE:slab_depth + EDGE + HALO], 'block', up)]
    all_to_all x2 -> x0, other arithmetic: 25.4 us -> none  [shards(): lax.all_to_all(outgoing, 'block', split_axis=0, concat_axis=0, tiled=True)]
    all_to_all x1, waiting for transfers between devices: 42.2 us -> 31.4 us  [shards(): lax.all_to_all(outgoing, 'block', split_axis=0, concat_axis=0, tiled=True)]
    all_gather x1 -> x0, local copies, waits for them, and re-layouts: 6.63 us -> none  [shards(): estimate = lax.all_gather(estimate_share, 'view', axis=1, tiled=True)]
  transfers between devices with their start and end apart: 14 -> 14, of which waited for: 10 -> 9; matrix products, arithmetic and copies ran while one was open for 15% -> 7% of each run, Pallas kernels for 0% -> 7%
where the time goes in v1:
time: 343 us; the launch traced here: 342 us
  Pallas kernels  160 us (47%)
  waiting for transfers between devices  100 us (29%)
  starting transfers between devices  33.8 us (10%)
  other arithmetic  30.3 us (9%)
  local copies, waits for them, and re-layouts  17.1 us (5%)
    pallas_call x2, Pallas kernels, backward(): pl.pallas_call(backward_body, grid=(views,), in_specs=[matrix(depth_bands...  85.9 us
    pallas_call x2, Pallas kernels, forward(): pl.pallas_call(forward_body, grid=(views,), in_specs=[pl.BlockSpec(memory...  50.3 us
    ppermute x2, waiting for transfers between devices, shards(): lax.ppermute(total[slab_depth + EDGE:slab_depth + EDGE + HALO], 'block', up)  34.2 us
    all_to_all x1, waiting for transfers between devices, shards(): lax.all_to_all(outgoing, 'block', split_axis=0, concat_axis=0, tiled=True)  31.4 us
    pallas_call x1, Pallas kernels, place_pieces(): pl.pallas_call(place_body, grid=(views, slots), in_specs=[pl.BlockSpec(me...  13.3 us
    ppermute x1, waiting for transfers between devices, shards(): lax.ppermute(incoming, 'view', [((v + CORES * hop) % view_count, v) for v...  13.1 us
    ppermute x2, starting transfers between devices, shards(): lax.ppermute(total[slab_depth + EDGE:slab_depth + EDGE + HALO], 'block', up)  10.6 us
    pallas_call x1, Pallas kernels, pick_pieces(): pl.pallas_call(copy_body, grid_spec=pltpu.PrefetchScalarGridSpec(num_scal...  10.1 us
  transfers between devices with their start and end apart: 14, of which 9 were waited for; matrix products, arithmetic and copies ran while one was open for 7% of the time, Pallas kernels for 7%

profile of v1, /device:TPU:0, one launch (start us, length us, event | category | flops | bytes accessed | tf_op | source)
XLA Modules:
  0.0 342.0 jit_solution(6365780802247845711)
XLA Ops:
  0.5 1.3 reduce.183
  2.1 0.7 select_reduce_fusion.4.index_ref
  2.9 10.1 %pick_pieces.1 = bf16[16,256,256]{2,1,0:T(8,128)(2,1)} custom-call(s32[16]{0:T(128)} %select_reduce_fusion.4.index_ref, bf16[16,256,256]{2,1,0:T(8,128)(2,1)} %bitcast.87), custom_call_target="tpu_custom_call" | custom-call | tf_op jit(solution)/shard_map/pick_pieces/pallas_call | solution.py:57
  13.0 7.3 %all-to-all-start = ((bf16[8,2,256,256]{3,2,1,0:T(8,128)(2,1)}), bf16[8,2,256,256]{3,2,1,0:T(8,128)(2,1)S(1)}, u32[]{:S(2)}, u32[]{:S(2)}) async-start(bf16[8,2,256,256]{3,2,1,0:T(8,128)(2,1)} %bitcast.84), calls=%async_computation | async-start | bytes 4194304 | tf_op jit(solution)/shard_map/all_to_all | solution.py:275
  20.3 2.5 convert_element_type.55
  22.8 1.0 fusion.278
  23.8 1.3 collective-permute-start.2
  25.1 4.6 %collective-permute-start.1 = (bf16[13,64,256]{2,1,0:T(8,128)(2,1)}, bf16[13,64,256]{2,1,0:T(8,128)(2,1)S(1)}, u32[]{:S(2)}, u32[]{:S(2)}) collective-permute-start(bf16[13,64,256]{2,1,0:T(8,128)(2,1)} %get-tuple-element.108), channel_id=1, source_target_pairs={{0,1},{1,2},{2,3},{3,4},{4,5},{5,6},{6,7},{8,9},{9,10},{10,11},{11... | collective-permute-start | bytes 1277960 | tf_op jit(solution)/shard_map/ppermute | solution.py:372
  34.1 0.8 select_convert_fusion.5.rows_ref
  35.2 0.8 select_convert_fusion.2.depth_ref
  36.1 1.5 select_convert_fusion.1.columns_ref
  37.6 0.8 select_convert_fusion.columns_ref
  38.5 31.4 %all-to-all-done = bf16[8,2,256,256]{3,2,1,0:T(8,128)(2,1)S(1)} async-done(((bf16[8,2,256,256]{3,2,1,0:T(8,128)(2,1)}), bf16[8,2,256,256]{3,2,1,0:T(8,128)(2,1)S(1)}, u32[]{:S(2)}, u32[]{:S(2)}) %all-to-all-start) | async-done | bytes 2097184 | tf_op jit(solution)/shard_map/all_to_all | solution.py:275
  69.9 1.5 collective-permute-start
  71.4 1.3 pad_maximum_fusion.5.offset_ref
  72.8 2.5 constant_dynamic-update-slice_fusion.1
  75.3 0.9 slice_bitcast_fusion.1
  76.6 25.1 %forward_blur.2.blurred_ref = f32[2,64,64,256]{3,2,1,0:T(8,128)} custom-call(f32[2]{0:T(128)S(1)} %pad_maximum_fusion.5.offset_ref, bf16[2,64,96]{2,1,0:T(8,128)(2,1)S(1)} %select_convert_fusion.4.depth_ref, bf16[2,64,64]{2,1,0:T(8,128)(2,1)S(1)} %select_convert_fusion.3.rows_ref, bf16[2,256,256]{2,1,0:T(8,128)(2,1)S(1)} %select_convert_fusion.columns_ref, ...), custom_call_target="tpu_custom_call" | custom-call | flops 6979321856 | bytes 14680064 | tf_op jit(solution)/shard_map/forward_blur/pallas_call | solution.py:154
  101.7 13.1 %collective-permute-done = bf16[16,256,256]{2,1,0:T(8,128)(2,1)} collective-permute-done((bf16[16,256,256]{2,1,0:T(8,128)(2,1)S(1)}, bf16[16,256,256]{2,1,0:T(8,128)(2,1)}, u32[]{:S(2)}, u32[]{:S(2)}) %collective-permute-start) | collective-permute-done | bytes 2097184 | tf_op jit(solution)/shard_map/ppermute | solution.py:280
  114.8 2.0 pad_maximum_fusion.incoming_ref
  116.8 13.3 %place_pieces.1 = f32[2,16,256,256]{3,2,1,0:T(8,128)} custom-call(s32[2,16]{1,0:T(2,128)S(1)} %select_reduce_fusion.3.order_ref, s32[2,17]{1,0:T(2,128)S(1)} %convert_reduce_fusion.2.start_ref, f32[2,16]{1,0:T(2,128)S(1)} %convert_divide_fusion.scale_ref, bf16[2,16,256,256]{3,2,1,0:T(8,128)(2,1)S(1)} %pad_maximum_fusion.incoming_ref), custom_call_target="tpu_custom_call" | custom-call | tf_op jit(solution)/shard_map/place_pieces/pallas_call | solution.py:85
  130.1 42.9 %backward_blur.2 = f32[2,6144,128]{2,1,0:T(8,128)} custom-call(bf16[2,96,64]{2,1,0:T(8,128)(2,1)} %select_convert_fusion.2.depth_ref, bf16[2,64,64]{2,1,0:T(8,128)(2,1)} %select_convert_fusion.5.rows_ref, bf16[2,256,256]{2,1,0:T(8,128)(2,1)} %select_convert_fusion.1.columns_ref, f32[2,64,64,256]{3,2,1,0:T(8,128)} %bitcast.78, ...), custom_call_target="tpu_custom_call" | custom-call | tf_op jit(solution)/shard_map/backward_blur/pallas_call | solution.py:228
  173.0 2.1 dynamic-slice_bitcast_fusion.1
  175.6 0.8 broadcast_in_dim.548
  176.5 1.1 reshape.327
  179.8 1.2 collective-permute-done.3
  181.0 3.9 %bitcast_add_fusion.1 = f32[96,64,128]{2,1,0:T(8,128)S(1)} fusion(f32[96,64,128]{2,1,0:T(8,128)} %collective-permute-done.3, f32[2,96,64,128]{3,2,1,0:T(8,128)} %bitcast.81, s32[]{:T(128)S(6)} %select_n.686), kind=kLoop, calls=%fused_computation.5 | loop fusion | flops 786432 | bytes 9437188 | tf_op jit(solution)/shard_map/add | solution.py:393
  185.1 6.2 %collective-permute-start.4 = (f32[13,64,128]{2,1,0:T(8,128)S(1)}, f32[13,64,128]{2,1,0:T(8,128)S(1)}, u32[]{:S(2)}, u32[]{:S(2)}) collective-permute-start(f32[13,64,128]{2,1,0:T(8,128)S(1)} %get-tuple-element.103), channel_id=1, source_target_pairs={{0,1},{1,2},{2,3},{3,4},{4,5},{5,6},{6,7},{8,9},{9,10},{10,11},{11... | collective-permute-start | bytes 1277960 | tf_op jit(solution)/shard_map/ppermute | solution.py:394
  191.2 1.3 collective-permute-start.5
  192.6 17.1 %collective-permute-done.4 = f32[13,64,128]{2,1,0:T(8,128)S(1)} collective-permute-done((f32[13,64,128]{2,1,0:T(8,128)S(1)}, f32[13,64,128]{2,1,0:T(8,128)S(1)}, u32[]{:S(2)}, u32[]{:S(2)}) %collective-permute-start.4) | collective-permute-done | bytes 426016 | tf_op jit(solution)/shard_map/ppermute | solution.py:394
  209.7 1.6 fusion.274
  211.3 4.4 %collective-permute-start.6 = (bf16[13,64,128]{2,1,0:T(8,128)(2,1)S(1)}, bf16[13,64,128]{2,1,0:T(8,128)(2,1)S(1)}, u32[]{:S(2)}, u32[]{:S(2)}) collective-permute-start(bf16[13,64,128]{2,1,0:T(8,128)(2,1)S(1)} %get-tuple-element.110), channel_id=1, source_target_pairs={{0,1},{1,2},{2,3},{3,4},{4,5},{5,6},{6,7},{8,9},{9,10},{10,11},{11... | collective-permute-start | bytes 638984 | tf_op jit(solution)/shard_map/ppermute | solution.py:372
  216.4 1.3 collective-permute-start.7
  217.7 6.6 %collective-permute-done.6 = bf16[13,64,128]{2,1,0:T(8,128)(2,1)S(1)} collective-permute-done((bf16[13,64,128]{2,1,0:T(8,128)(2,1)S(1)}, bf16[13,64,128]{2,1,0:T(8,128)(2,1)S(1)}, u32[]{:S(2)}, u32[]{:S(2)}) %collective-permute-start.6) | collective-permute-done | bytes 213024 | tf_op jit(solution)/shard_map/ppermute | solution.py:372
  225.0 1.0 constant_dynamic-update-slice_fusion.4
  227.4 3.7 %collective-permute-done.8 = bf16[96,64,128]{2,1,0:T(8,128)(2,1)} collective-permute-done((bf16[96,64,128]{2,1,0:T(8,128)(2,1)}, bf16[96,64,128]{2,1,0:T(8,128)(2,1)}, u32[]{:S(2)}, u32[]{:S(2)}) %collective-permute-start.8) | collective-permute-done | bytes 1572896 | tf_op jit(solution)/shard_map/ppermute | solution.py:378
  231.1 2.1 select_bitcast_fusion.1
  233.5 25.1 %forward_blur.3.blurred_ref = f32[2,64,64,256]{3,2,1,0:T(8,128)} custom-call(f32[2]{0:T(128)S(1)} %pad_maximum_fusion.5.offset_ref, bf16[2,64,96]{2,1,0:T(8,128)(2,1)S(1)} %select_convert_fusion.4.depth_ref, bf16[2,64,64]{2,1,0:T(8,128)(2,1)S(1)} %select_convert_fusion.3.rows_ref, bf16[2,256,256]{2,1,0:T(8,128)(2,1)S(1)} %select_convert_fusion.columns_ref, ...), custom_call_target="tpu_custom_call" | custom-call | flops 6979321856 | bytes 14680064 | tf_op jit(solution)/shard_map/forward_blur/pallas_call | solution.py:154
  258.6 42.9 %backward_blur.3 = f32[2,6144,128]{2,1,0:T(8,128)} custom-call(bf16[2,96,64]{2,1,0:T(8,128)(2,1)} %select_convert_fusion.2.depth_ref, bf16[2,64,64]{2,1,0:T(8,128)(2,1)} %select_convert_fusion.5.rows_ref, bf16[2,256,256]{2,1,0:T(8,128)(2,1)} %select_convert_fusion.1.columns_ref, f32[2,64,64,256]{3,2,1,0:T(8,128)} %bitcast.79, ...), custom_call_target="tpu_custom_call" | custom-call | tf_op jit(solution)/shard_map/backward_blur/pallas_call | solution.py:228
  301.6 2.3 dynamic-slice_bitcast_fusion
  304.1 5.5 %collective-permute-done.9 = f32[96,64,128]{2,1,0:T(8,128)S(1)} collective-permute-done((f32[96,64,128]{2,1,0:T(8,128)S(1)}, f32[96,64,128]{2,1,0:T(8,128)S(1)}, u32[]{:S(2)}, u32[]{:S(2)}) %collective-permute-start.9) | collective-permute-done | bytes 3145760 | tf_op jit(solution)/shard_map/ppermute | solution.py:393
  309.6 1.0 bitcast_add_fusion
  310.6 4.4 %collective-permute-start.10 = (f32[13,64,128]{2,1,0:T(8,128)S(1)}, f32[13,64,128]{2,1,0:T(8,128)S(1)}, u32[]{:S(2)}, u32[]{:S(2)}) collective-permute-start(f32[13,64,128]{2,1,0:T(8,128)S(1)} %get-tuple-element.99), channel_id=1, source_target_pairs={{0,1},{1,2},{2,3},{3,4},{4,5},{5,6},{6,7},{8,9},{9,10},{10,11},{11... | collective-permute-start | bytes 1277960 | tf_op jit(solution)/shard_map/ppermute | solution.py:394
  315.1 1.3 collective-permute-start.11
  316.4 17.2 %collective-permute-done.10 = f32[13,64,128]{2,1,0:T(8,128)S(1)} collective-permute-done((f32[13,64,128]{2,1,0:T(8,128)S(1)}, f32[13,64,128]{2,1,0:T(8,128)S(1)}, u32[]{:S(2)}, u32[]{:S(2)}) %collective-permute-start.10) | collective-permute-done | bytes 426016 | tf_op jit(solution)/shard_map/ppermute | solution.py:394
  333.5 1.4 fusion.1
  335.0 4.1 %collective-permute-done.12 = f32[64,64,128]{2,1,0:T(8,128)S(1)} collective-permute-done((f32[64,64,128]{2,1,0:T(8,128)S(1)}, f32[64,64,128]{2,1,0:T(8,128)S(1)}, u32[]{:S(2)}, u32[]{:S(2)}) %collective-permute-start.12) | collective-permute-done | bytes 2097184 | tf_op jit(solution)/shard_map/ppermute | solution.py:378
  339.6 2.4 pad_maximum_fusion.1
  (101 shorter events, 12.4 us)
Async XLA Ops:
  13.0 56.9 %all-to-all-start = ((bf16[8,2,256,256]{3,2,1,0:T(8,128)(2,1)}), bf16[8,2,256,256]{3,2,1,0:T(8,128)(2,1)S(1)}, u32[]{:S(2)}, u32[]{:S(2)}) async-start(bf16[8,2,256,256]{3,2,1,0:T(8,128)(2,1)} %bitcast.84), calls=%async_computation | async-start | bytes 4194304 | tf_op jit(solution)/shard_map/all_to_all | solution.py:275
  20.3 9.5 %copy-start.6 = (f32[4]{0:T(128)S(1)}, f32[4]{0:T(128)}, u32[]{:S(2)}) copy-start(f32[4]{0:T(128)} %param.13) | copy-start | bytes 52
  20.3 10.1 %copy-start.2 = (s32[4,3]{1,0:T(4,128)S(1)}, s32[4,3]{1,0:T(4,128)}, u32[]{:S(2)}) copy-start(s32[4,3]{1,0:T(4,128)} %param.11) | copy-start | bytes 148
  20.3 10.3 %copy-start.3 = (f32[4,3,21]{2,0,1:T(4,128)S(1)}, f32[4,3,21]{2,0,1:T(4,128)}, u32[]{:S(2)}) copy-start(f32[4,3,21]{2,0,1:T(4,128)} %param.12) | copy-start | bytes 3028
  20.3 10.7 %copy-start.4 = (s32[4,128]{1,0:T(4,128)S(1)}, s32[4,128]{1,0:T(4,128)}, u32[]{:S(2)}) copy-start(s32[4,128]{1,0:T(4,128)} %param.10) | copy-start | bytes 6148
  23.8 51.5 %collective-permute-start.2 = (bf16[13,64,256]{2,1,0:T(8,128)(2,1)}, bf16[13,64,256]{2,1,0:T(8,128)(2,1)S(1)}, u32[]{:S(2)}, u32[]{:S(2)}) collective-permute-start(bf16[13,64,256]{2,1,0:T(8,128)(2,1)} %get-tuple-element.107), channel_id=1, source_target_pairs={{1,0},{2,1},{3,2},{4,3},{5,4},{6,5},{7,6},{9,8},{10,9},{11,10},{12... | collective-permute-start | bytes 1277960 | tf_op jit(solution)/shard_map/ppermute | solution.py:373
  25.1 47.6 %collective-permute-start.1 = (bf16[13,64,256]{2,1,0:T(8,128)(2,1)}, bf16[13,64,256]{2,1,0:T(8,128)(2,1)S(1)}, u32[]{:S(2)}, u32[]{:S(2)}) collective-permute-start(bf16[13,64,256]{2,1,0:T(8,128)(2,1)} %get-tuple-element.108), channel_id=1, source_target_pairs={{0,1},{1,2},{2,3},{3,4},{4,5},{5,6},{6,7},{8,9},{9,10},{10,11},{11... | collective-permute-start | bytes 1277960 | tf_op jit(solution)/shard_map/ppermute | solution.py:372
  69.9 44.9 %collective-permute-start = (bf16[16,256,256]{2,1,0:T(8,128)(2,1)S(1)}, bf16[16,256,256]{2,1,0:T(8,128)(2,1)}, u32[]{:S(2)}, u32[]{:S(2)}) collective-permute-start(bf16[16,256,256]{2,1,0:T(8,128)(2,1)S(1)} %bitcast.85), channel_id=1, source_target_pairs={{16,0},{24,8},{0,16},{8,24},{17,1},{25,9},{1,17},{9,25},{18,2},{26... | collective-permute-start | bytes 6291464 | tf_op jit(solution)/shard_map/ppermute | solution.py:280
  173.0 2.4 copy-start.5
  175.2 5.9 %collective-permute-start.3 = (f32[96,64,128]{2,1,0:T(8,128)S(1)}, f32[96,64,128]{2,1,0:T(8,128)}, u32[]{:S(2)}, u32[]{:S(2)}) collective-permute-start(f32[96,64,128]{2,1,0:T(8,128)S(1)} %dynamic-slice_bitcast_fusion.1), channel_id=1, source_target_pairs={{0,8},{8,0},{16,24},{24,16},{1,9},{9,1},{17,25},{25,17},{2,10},{10... | collective-permute-start | bytes 9437192 | tf_op jit(solution)/shard_map/ppermute | solution.py:393
  181.0 28.7 %copy-start = (f32[64,64,256]{2,1,0:T(8,128)S(1)}, f32[64,64,256]{2,1,0:T(8,128)}, u32[]{:S(2)}) copy-start(f32[64,64,256]{2,1,0:T(8,128)} %param.7) | copy-start | bytes 12582916
  185.1 24.6 %collective-permute-start.4 = (f32[13,64,128]{2,1,0:T(8,128)S(1)}, f32[13,64,128]{2,1,0:T(8,128)S(1)}, u32[]{:S(2)}, u32[]{:S(2)}) collective-permute-start(f32[13,64,128]{2,1,0:T(8,128)S(1)} %get-tuple-element.103), channel_id=1, source_target_pairs={{0,1},{1,2},{2,3},{3,4},{4,5},{5,6},{6,7},{8,9},{9,10},{10,11},{11... | collective-permute-start | bytes 1277960 | tf_op jit(solution)/shard_map/ppermute | solution.py:394
  191.2 18.5 %collective-permute-start.5 = (f32[13,64,128]{2,1,0:T(8,128)S(1)}, f32[13,64,128]{2,1,0:T(8,128)S(1)}, u32[]{:S(2)}, u32[]{:S(2)}) collective-permute-start(f32[13,64,128]{2,1,0:T(8,128)S(1)} %get-tuple-element.104), channel_id=1, source_target_pairs={{1,0},{2,1},{3,2},{4,3},{5,4},{6,5},{7,6},{9,8},{10,9},{11,10},{12... | collective-permute-start | bytes 1277960 | tf_op jit(solution)/shard_map/ppermute | solution.py:397
  211.3 13.0 %collective-permute-start.6 = (bf16[13,64,128]{2,1,0:T(8,128)(2,1)S(1)}, bf16[13,64,128]{2,1,0:T(8,128)(2,1)S(1)}, u32[]{:S(2)}, u32[]{:S(2)}) collective-permute-start(bf16[13,64,128]{2,1,0:T(8,128)(2,1)S(1)} %get-tuple-element.110), channel_id=1, source_target_pairs={{0,1},{1,2},{2,3},{3,4},{4,5},{5,6},{6,7},{8,9},{9,10},{10,11},{11... | collective-permute-start | bytes 638984 | tf_op jit(solution)/shard_map/ppermute | solution.py:372
  216.4 9.7 %collective-permute-start.7 = (bf16[13,64,128]{2,1,0:T(8,128)(2,1)S(1)}, bf16[13,64,128]{2,1,0:T(8,128)(2,1)S(1)}, u32[]{:S(2)}, u32[]{:S(2)}) collective-permute-start(bf16[13,64,128]{2,1,0:T(8,128)(2,1)S(1)} %get-tuple-element.109), channel_id=1, source_target_pairs={{1,0},{2,1},{3,2},{4,3},{5,4},{6,5},{7,6},{9,8},{10,9},{11,10},{12... | collective-permute-start | bytes 638984 | tf_op jit(solution)/shard_map/ppermute | solution.py:373
  227.4 3.8 %collective-permute-start.8 = (bf16[96,64,128]{2,1,0:T(8,128)(2,1)}, bf16[96,64,128]{2,1,0:T(8,128)(2,1)}, u32[]{:S(2)}, u32[]{:S(2)}) collective-permute-start(bf16[96,64,128]{2,1,0:T(8,128)(2,1)} %broadcast_dynamic-update-slice_fusion.3), channel_id=1, source_target_pairs={{0,8},{8,0},{16,24},{24,16},{1,9},{9,1},{17,25},{25,17},{2,10},{10... | collective-permute-start | bytes 4718600 | tf_op jit(solution)/shard_map/ppermute | solution.py:378
  301.6 8.0 %copy-start.1 = (f32[2,6144,128]{2,1,0:T(8,128)S(1)}, f32[2,6144,128]{2,1,0:T(8,128)}, u32[]{:S(2)}) copy-start(f32[2,6144,128]{2,1,0:T(8,128)} %backward_blur.3) | copy-start | bytes 18874372
  303.9 5.7 %collective-permute-start.9 = (f32[96,64,128]{2,1,0:T(8,128)S(1)}, f32[96,64,128]{2,1,0:T(8,128)S(1)}, u32[]{:S(2)}, u32[]{:S(2)}) collective-permute-start(f32[96,64,128]{2,1,0:T(8,128)S(1)} %dynamic-slice_bitcast_fusion), channel_id=1, source_target_pairs={{0,8},{8,0},{16,24},{24,16},{1,9},{9,1},{17,25},{25,17},{2,10},{10... | collective-permute-start | bytes 9437192 | tf_op jit(solution)/shard_map/ppermute | solution.py:393
  310.6 22.9 %collective-permute-start.10 = (f32[13,64,128]{2,1,0:T(8,128)S(1)}, f32[13,64,128]{2,1,0:T(8,128)S(1)}, u32[]{:S(2)}, u32[]{:S(2)}) collective-permute-start(f32[13,64,128]{2,1,0:T(8,128)S(1)} %get-tuple-element.99), channel_id=1, source_target_pairs={{0,1},{1,2},{2,3},{3,4},{4,5},{5,6},{6,7},{8,9},{9,10},{10,11},{11... | collective-permute-start | bytes 1277960 | tf_op jit(solution)/shard_map/ppermute | solution.py:394
  315.1 18.5 %collective-permute-start.11 = (f32[13,64,128]{2,1,0:T(8,128)S(1)}, f32[13,64,128]{2,1,0:T(8,128)S(1)}, u32[]{:S(2)}, u32[]{:S(2)}) collective-permute-start(f32[13,64,128]{2,1,0:T(8,128)S(1)} %get-tuple-element.100), channel_id=1, source_target_pairs={{1,0},{2,1},{3,2},{4,3},{5,4},{6,5},{7,6},{9,8},{10,9},{11,10},{12... | collective-permute-start | bytes 1277960 | tf_op jit(solution)/shard_map/ppermute | solution.py:397
  335.0 4.2 %collective-permute-start.12 = (f32[64,64,128]{2,1,0:T(8,128)S(1)}, f32[64,64,128]{2,1,0:T(8,128)S(1)}, u32[]{:S(2)}, u32[]{:S(2)}) collective-permute-start(f32[64,64,128]{2,1,0:T(8,128)S(1)} %fusion.1), channel_id=1, source_target_pairs={{0,8},{8,0},{16,24},{24,16},{1,9},{9,1},{17,25},{25,17},{2,10},{10... | collective-permute-start | bytes 6291464 | tf_op jit(solution)/shard_map/ppermute | solution.py:378

commit v2 on v1

--- a/solution.py
+++ b/solution.py
@@ -1,5 +1,3 @@
-import functools
-
 import jax
 import jax.numpy as jnp
 from jax import lax
@@ -48,50 +46,58 @@
     return jnp.sum(jnp.where(inside, kernel[:, None, :], 0.0), axis=2)
 
 
-def copy_body(index_ref, piece_ref, out_ref):
-    out_ref[...] = piece_ref[...]
+def pick_body(index_ref, piece_ref, out_ref, sems):
+    copies = [
+        pltpu.make_async_copy(piece_ref.at[index_ref[i]], out_ref.at[i], sems.at[i])
+        for i in range(out_ref.shape[0])
+    ]
+    for copy in copies:
+        copy.start()
+    for copy in copies:
+        copy.wait()
 
 
 def pick_pieces(pieces, index):
-    block = (1,) + pieces.shape[1:]
+    count = index.shape[0]
     return pl.pallas_call(
-        copy_body,
-        grid_spec=pltpu.PrefetchScalarGridSpec(
-            num_scalar_prefetch=1,
-            grid=(index.shape[0],),
-            in_specs=[pl.BlockSpec(block, lambda i, s: (s[i], 0, 0))],
-            out_specs=pl.BlockSpec(block, lambda i, s: (i, 0, 0)),
-        ),
-        out_shape=jax.ShapeDtypeStruct((index.shape[0],) + pieces.shape[1:], pieces.dtype),
+        pick_body,
+        in_specs=[pl.BlockSpec(memory_space=pltpu.SMEM), pl.BlockSpec(memory_space=pl.ANY)],
+        out_specs=pl.BlockSpec(memory_space=pl.ANY),
+        out_shape=jax.ShapeDtypeStruct((count,) + pieces.shape[1:], pieces.dtype),
+        scratch_shapes=[pltpu.SemaphoreType.DMA((count,))],
         name="pick_pieces",
     )(index, pieces)
 
 
 def place_body(order_ref, start_ref, scale_ref, incoming_ref, out_ref):
-    view, slot = pl.program_id(0), pl.program_id(1)
-    out_ref[...] = jnp.zeros_like(out_ref)
-
-    def add(k, carry):
-        out_ref[0, 0] += incoming_ref[0, order_ref[view, k]].astype(F32)
-        return carry
-
-    lax.fori_loop(start_ref[view, slot], start_ref[view, slot + 1], add, 0)
-    out_ref[...] = out_ref[...] * scale_ref[view, slot]
+    view, step = pl.program_id(0), pl.program_id(1)
+    group = out_ref.shape[1]
+    for i in range(group):
+        slot = step * group + i
+        out_ref[0, i] = jnp.zeros(out_ref.shape[2:], F32)
+
+        def add(k, carry):
+            out_ref[0, i] += incoming_ref[0, order_ref[view, k]].astype(F32)
+            return carry
+
+        lax.fori_loop(start_ref[view, slot], start_ref[view, slot + 1], add, 0)
+        out_ref[0, i] = out_ref[0, i] * scale_ref[view, slot]
 
 
 def place_pieces(incoming, order, start, scale):
     views, slots = scale.shape
     tail = incoming.shape[2:]
+    group = 4 if slots % 4 == 0 else 1
     return pl.pallas_call(
         place_body,
-        grid=(views, slots),
+        grid=(views, slots // group),
         in_specs=[
             pl.BlockSpec(memory_space=pltpu.SMEM),
             pl.BlockSpec(memory_space=pltpu.SMEM),
             pl.BlockSpec(memory_space=pltpu.SMEM),
             pl.BlockSpec((1,) + incoming.shape[1:], lambda v, t: (v, 0, 0, 0)),
         ],
-        out_specs=pl.BlockSpec((1, 1) + tail, lambda v, t: (v, t, 0, 0)),
+        out_specs=pl.BlockSpec((1, group) + tail, lambda v, t: (v, t, 0, 0)),
         out_shape=jax.ShapeDtypeStruct((views, slots) + tail, F32),
         compiler_params=pltpu.CompilerParams(vmem_limit_bytes=48 * 2**20),
         name="place_pieces",
@@ -110,132 +116,158 @@
     )
 
 
-def forward_body(offset_ref, depth_ref, rows_ref, columns_ref, volume_ref, out_ref, source, middle):
-    view = pl.program_id(0)
+def blur_depth_columns(depth_ref, columns_ref, volume_ref, source, middle):
     halves, depth_in, rows, _ = volume_ref.shape
-    depth = out_ref.shape[1]
-
-    @pl.when(view == 0)
-    def _():
-        for h in range(halves):
-
-            def widen(z, carry):
-                source[h, pl.ds(pl.multiple_of(z * rows, rows), rows), :] = volume_ref[h, z].astype(F32)
-                return carry
-
-            lax.fori_loop(0, depth_in, widen, 0, unroll=8)
+    views = columns_ref.shape[0]
+    depth = depth_ref.shape[0] // views
+    for h in range(halves):
+
+        def widen(z, carry):
+            span = pl.ds(pl.multiple_of(z * rows, rows), rows)
+            source[h, span, :] = volume_ref[h, z].astype(F32)
+            return carry
+
+        lax.fori_loop(0, depth_in, widen, 0, unroll=8)
 
     def row(y, carry):
         column = take_rows(source, y, rows)
-        blurred = jnp.dot(depth_ref[0], column, preferred_element_type=F32).astype(BF16)
-        blurred = jnp.dot(blurred, columns_ref[0], preferred_element_type=F32)
-        for h in range(halves):
-            middle[h, pl.ds(y, depth, stride=rows), :] = blurred[:, h * LANES : (h + 1) * LANES]
+        deep = jnp.dot(depth_ref[...], column, preferred_element_type=F32).astype(BF16)
+        for v in range(views):
+            cells = jnp.dot(
+                deep[v * depth : (v + 1) * depth], columns_ref[v], preferred_element_type=F32
+            )
+            for h in range(halves):
+                middle[v, h, pl.ds(y, depth, stride=rows), :] = cells[:, h * LANES : (h + 1) * LANES]
         return carry
 
-    lax.fori_loop(0, rows, row, 0, unroll=8)
+    lax.fori_loop(0, rows, row, 0, unroll=4)
+
+
+def spread_quotients(
+    offset_ref, depth_ref, rows_ref, rows_back_ref, columns_ref, average_ref, middle, turned, out_ref
+):
+    views, depth, rows, _ = average_ref.shape
+    halves = out_ref.shape[0]
+    depth_out = out_ref.shape[1] // rows
 
     def plane(z, carry):
         span = pl.ds(pl.multiple_of(z * rows, rows), rows)
-        cells = jnp.concatenate([middle[h, span, :].astype(BF16) for h in range(halves)], axis=1)
-        out_ref[0, z] = (
-            jnp.dot(rows_ref[0], cells, preferred_element_type=F32) + offset_ref[view]
+        for v in range(views):
+            cells = jnp.concatenate(
+                [middle[v, h, span, :].astype(BF16) for h in range(halves)], axis=1
+            )
+            blurred = jnp.dot(rows_ref[v], cells, preferred_element_type=F32) + offset_ref[v]
+            quotient = (average_ref[v, z] / blurred).astype(BF16)
+            cells = jnp.dot(rows_back_ref[v], quotient, preferred_element_type=F32)
+            for h in range(halves):
+                turned[v, h, span, :] = cells[:, h * LANES : (h + 1) * LANES]
+        return carry
+
+    lax.fori_loop(0, depth, plane, 0, unroll=4)
+
+    def row(y, carry):
+        columns = [
+            jnp.dot(
+                take_rows(turned.at[v], y, rows), columns_ref[v], preferred_element_type=F32
+            ).astype(BF16)
+            for v in range(views)
+        ]
+        cells = jnp.dot(
+            depth_ref[...], jnp.concatenate(columns, axis=0), preferred_element_type=F32
         )
+        for h in range(halves):
+            out_ref[h, pl.ds(y, depth_out, stride=rows), :] = cells[:, h * LANES : (h + 1) * LANES]
         return carry
 
-    lax.fori_loop(0, depth, plane, 0, unroll=8)
-
-
-def forward(volume, offset, depth_bands, row_bands, column_bands):
-    views, depth = depth_bands.shape[:2]
+    lax.fori_loop(0, rows, row, 0, unroll=4)
+
+
+def whole_step_body(
+    offset_ref, depth_ref, depth_back_ref, rows_ref, rows_back_ref, columns_ref, columns_back_ref,
+    average_ref, volume_ref, out_ref, source, middle,
+):
+    blur_depth_columns(depth_ref, columns_ref, volume_ref, source, middle)
+    spread_quotients(
+        offset_ref, depth_back_ref, rows_ref, rows_back_ref, columns_back_ref, average_ref,
+        middle, middle, out_ref,
+    )
+
+
+IN_SMEM = pl.BlockSpec(memory_space=pltpu.SMEM)
+IN_VMEM = pl.BlockSpec(memory_space=pltpu.VMEM)
+ROOM = pltpu.CompilerParams(vmem_limit_bytes=60 * 2**20)
+
+
+def first_half(volume, bands):
     halves, depth_in, rows, _ = volume.shape
+    views = bands["columns"].shape[0]
+    depth = bands["depth"].shape[0] // views
+    shape = (views, halves, depth * rows, LANES)
     width = halves * LANES
-    matrix = lambda a: pl.BlockSpec((1,) + a.shape[1:], lambda v: (v, 0, 0))
     return pl.pallas_call(
-        forward_body,
-        grid=(views,),
-        in_specs=[
-            pl.BlockSpec(memory_space=pltpu.SMEM),
-            matrix(depth_bands),
-            matrix(row_bands),
-            matrix(column_bands),
-            pl.BlockSpec(volume.shape, lambda v: (0, 0, 0, 0)),
+        blur_depth_columns,
+        in_specs=[IN_VMEM] * 3,
+        out_specs=[IN_VMEM] * 2,
+        out_shape=[
+            jax.ShapeDtypeStruct((halves, depth_in * rows, LANES), F32),
+            jax.ShapeDtypeStruct(shape, F32),
         ],
-        out_specs=pl.BlockSpec((1, depth, rows, width), lambda v: (v, 0, 0, 0)),
-        out_shape=jax.ShapeDtypeStruct((views, depth, rows, width), F32),
-        scratch_shapes=[
-            pltpu.VMEM((halves, depth_in * rows, LANES), F32),
-            pltpu.VMEM((halves, depth * rows, LANES), F32),
-        ],
-        compiler_params=pltpu.CompilerParams(vmem_limit_bytes=48 * 2**20),
+        compiler_params=ROOM,
         cost_estimate=pl.CostEstimate(
-            flops=2 * views * depth * rows * width * (depth_in + rows + width) * 4,
+            flops=8 * views * depth * rows * width * (depth_in + width),
             bytes_accessed=4 * (views * depth + depth_in) * rows * width,
             transcendentals=0,
         ),
-        name="forward_blur",
-    )(offset, depth_bands, row_bands, column_bands, volume)
-
-
-def backward_body(depth_ref, rows_ref, columns_ref, average_ref, blurred_ref, out_ref, middle):
-    view = pl.program_id(0)
-    _, depth, rows, _ = average_ref.shape
-    halves = out_ref.shape[0]
-    depth_out = out_ref.shape[1] // rows
-
-    def plane(z, carry):
-        quotient = (average_ref[0, z] / blurred_ref[0, z]).astype(BF16)
-        cells = jnp.dot(rows_ref[0], quotient, preferred_element_type=F32)
-        span = pl.ds(pl.multiple_of(z * rows, rows), rows)
-        for h in range(halves):
-            middle[h, span, :] = cells[:, h * LANES : (h + 1) * LANES]
-        return carry
-
-    lax.fori_loop(0, depth, plane, 0, unroll=8)
-
-    def spread(y):
-        column = take_rows(middle, y, rows)
-        column = jnp.dot(column, columns_ref[0], preferred_element_type=F32).astype(BF16)
-        return jnp.dot(depth_ref[0], column, preferred_element_type=F32)
-
-    @pl.when(view == 0)
-    def _():
-        def row(y, carry):
-            cells = spread(y)
-            for h in range(halves):
-                out_ref[h, pl.ds(y, depth_out, stride=rows), :] = cells[:, h * LANES : (h + 1) * LANES]
-            return carry
-
-        lax.fori_loop(0, rows, row, 0, unroll=8)
-
-    @pl.when(view > 0)
-    def _():
-        def row(y, carry):
-            cells = spread(y)
-            for h in range(halves):
-                out_ref[h, pl.ds(y, depth_out, stride=rows), :] += cells[:, h * LANES : (h + 1) * LANES]
-            return carry
-
-        lax.fori_loop(0, rows, row, 0, unroll=8)
-
-
-def backward(average, blurred, depth_bands, row_bands, column_bands):
-    views, depth_out = depth_bands.shape[:2]
-    _, depth, rows, width = blurred.shape
-    halves = width // LANES
-    matrix = lambda a: pl.BlockSpec((1,) + a.shape[1:], lambda v: (v, 0, 0))
-    whole = pl.BlockSpec((1, depth, rows, width), lambda v: (v, 0, 0, 0))
-    out = pl.pallas_call(
-        backward_body,
-        grid=(views,),
-        in_specs=[matrix(depth_bands), matrix(row_bands), matrix(column_bands), whole, whole],
-        out_specs=pl.BlockSpec((halves, depth_out * rows, LANES), lambda v: (0, 0, 0)),
+        name="blur_depth_columns",
+    )(bands["depth"], bands["columns"], volume)[1]
+
+
+def second_half(middle, average, bands):
+    views, halves, _, _ = middle.shape
+    rows = average.shape[2]
+    depth_out = bands["depth_back"].shape[0]
+    return pl.pallas_call(
+        spread_quotients_apart,
+        in_specs=[IN_SMEM] + [IN_VMEM] * 6,
+        out_specs=IN_VMEM,
         out_shape=jax.ShapeDtypeStruct((halves, depth_out * rows, LANES), F32),
-        scratch_shapes=[pltpu.VMEM((halves, depth * rows, LANES), F32)],
-        compiler_params=pltpu.CompilerParams(vmem_limit_bytes=56 * 2**20),
-        name="backward_blur",
-    )(depth_bands, row_bands, column_bands, average, blurred)
-    return out.reshape(halves, depth_out, rows, LANES)
+        scratch_shapes=[pltpu.VMEM(middle.shape, F32)],
+        compiler_params=ROOM,
+        name="spread_quotients",
+    )(
+        bands["offset"], bands["depth_back"], bands["rows"], bands["rows_back"],
+        bands["columns_back"], average, middle,
+    ).reshape(halves, depth_out, rows, LANES)
+
+
+def spread_quotients_apart(
+    offset_ref, depth_ref, rows_ref, rows_back_ref, columns_ref, average_ref, middle, out_ref, turned
+):
+    spread_quotients(
+        offset_ref, depth_ref, rows_ref, rows_back_ref, columns_ref, average_ref, middle, turned,
+        out_ref,
+    )
+
+
+def whole_step(volume, average, bands):
+    halves, depth_in, rows, _ = volume.shape
+    views, depth = average.shape[:2]
+    depth_out = bands["depth_back"].shape[0]
+    return pl.pallas_call(
+        whole_step_body,
+        in_specs=[IN_SMEM] + [IN_VMEM] * 8,
+        out_specs=IN_VMEM,
+        out_shape=jax.ShapeDtypeStruct((halves, depth_out * rows, LANES), F32),
+        scratch_shapes=[
+            pltpu.VMEM((halves, depth_in * rows, LANES), F32),
+            pltpu.VMEM((views, halves, depth * rows, LANES), F32),
+        ],
+        compiler_params=ROOM,
+        name="whole_step",
+    )(
+        bands["offset"], bands["depth"], bands["depth_back"], bands["rows"], bands["rows_back"],
+        bands["columns"], bands["columns_back"], average, volume,
+    ).reshape(halves, depth_out, rows, LANES)
 
 
 def shards(estimate0, pieces, dest_block, slot_index, psf_shift, psf_taps, background):
@@ -272,18 +304,19 @@
     outgoing = pick_pieces(
         pieces.reshape(slot_count, piece_depth * plane_rows, plane_columns), pick
     ).reshape(block_count, CAP, piece_depth * plane_rows, plane_columns)
-    incoming = lax.all_to_all(outgoing, "block", split_axis=0, concat_axis=0, tiled=True)
-    incoming = incoming.reshape(block_count * CAP, piece_depth * plane_rows, plane_columns)
-    arrived = [incoming]
-    for hop in range(1, chips):
-        arrived.append(
-            lax.ppermute(
-                incoming,
-                "view",
-                [((v + CORES * hop) % view_count, v) for v in range(view_count)],
+    parts = [[] for _ in range(chips)]
+    for part in range(CAP):
+        incoming = lax.all_to_all(outgoing[:, part], "block", split_axis=0, concat_axis=0, tiled=True)
+        parts[0].append(incoming)
+        for hop in range(1, chips):
+            parts[hop].append(
+                lax.ppermute(
+                    incoming,
+                    "view",
+                    [((v + CORES * hop) % view_count, v) for v in range(view_count)],
+                )
             )
-        )
-    arrived = jnp.stack(arrived)
+    arrived = jnp.stack([jnp.concatenate(group, axis=0) for group in parts])
 
     view_targets = of_own_views(targets)
     view_slots = of_own_views(slots)
@@ -293,7 +326,7 @@
     )
     column = jnp.where(
         view_targets == my_block,
-        lax.broadcasted_iota(jnp.int32, view_targets.shape, 1) * CAP + ranks,
+        ranks * block_count + lax.broadcasted_iota(jnp.int32, view_targets.shape, 1),
         -1,
     )
     matches = column[..., None] == buffer_slots
@@ -331,9 +364,16 @@
         )
 
     depth_bands, row_bands, column_bands = jax.vmap(bands)(own_kernel, own_shift)
-    depth_back = jnp.swapaxes(depth_bands, 1, 2)
-    rows_back = jnp.swapaxes(row_bands, 1, 2)
-    columns_forward = jnp.swapaxes(column_bands, 1, 2)
+    depth_bands = depth_bands.reshape(chips * slab_depth, wide_depth)
+    banded = {
+        "offset": own_offset,
+        "depth": depth_bands,
+        "depth_back": depth_bands.T,
+        "rows": row_bands,
+        "rows_back": jnp.swapaxes(row_bands, 1, 2),
+        "columns": jnp.swapaxes(column_bands, 1, 2),
+        "columns_back": column_bands,
+    }
 
     global_slot = targets * slot_count + slots
     slot_total = block_count * slot_count
@@ -385,16 +425,18 @@
     share = lax.dynamic_slice_in_dim(estimate0, my_core * LANES, LANES, 2)
     for iteration in range(ITERS):
         if iteration == 0:
-            wide = split_columns(widen(estimate0.astype(BF16)))
+            middle = first_half(split_columns(widen(estimate0.astype(BF16))), banded)
+            spread = second_half(middle, average, banded)
         else:
             wide = jnp.stack(pair(widen(share.astype(BF16))))
-        blurred = forward(wide, own_offset, depth_bands, row_bands, columns_forward)
-        spread = backward(average, blurred, depth_back, rows_back, column_bands)
+            spread = whole_step(wide, average, banded)
         total = half(spread, my_core) + lax.ppermute(half(spread, 1 - my_core), "view", swap)
         from_low = lax.ppermute(
-            total[slab_depth + EDGE : slab_depth + EDGE + HALO], "block", up
-        )
-        from_high = lax.ppermute(total[EDGE - HALO : EDGE], "block", down)
+            total[slab_depth + EDGE : slab_depth + EDGE + HALO].astype(BF16), "block", up
+        ).astype(F32)
+        from_high = lax.ppermute(
+            total[EDGE - HALO : EDGE].astype(BF16), "block", down
+        ).astype(F32)
         summed = total[EDGE : EDGE + slab_depth]
         summed = summed + jnp.concatenate(
             [

time: 343 us -> 357 us (1.041)
  waiting for transfers between devices: 100 us -> 67 us
  Pallas kernels: 160 us -> 179 us
  local copies, waits for them, and re-layouts: 17.1 us -> 30.6 us
  other arithmetic: 30.3 us -> 39.8 us
    pallas_call x6 -> x5, Pallas kernels: 160 us -> 179 us  [the longest x1 65.4 us: pick_pieces(): pl.pallas_call(pick_body, in_specs=[pl.BlockSpec(memory_space=pltpu.SMEM)...]
    ppermute x4, waiting for transfers between devices: 34.2 us -> 16.2 us  [the longest x2 11.5 us: shards(): lax.ppermute(total[slab_depth + EDGE:slab_depth + EDGE + HALO].astype(BF1...]
    all_to_all x1 -> x2, waiting for transfers between devices: 31.4 us -> 21.9 us  [shards(): lax.all_to_all(outgoing[:, part], 'block', split_axis=0, concat_axis=0, t...]
    ppermute x1 -> x2, waiting for transfers between devices: 13.1 us -> 6.32 us  [shards(): lax.ppermute(incoming, 'view', [((v + CORES * hop) % view_count, v) for v...]
    ppermute x2, waiting for transfers between devices: 6.64 us -> 1.2 us  [widen(): low = lax.ppermute(cells[slab_depth - HALO:], 'block', up)]
    ppermute x2, waiting for transfers between devices: 0.01 us -> 5.02 us  [widen(): high = lax.ppermute(cells[:HALO], 'block', down)]
    add x2 -> x0, other arithmetic: 4.9 us -> none  [shards(): half(spread, my_core)]
    another operation x1 -> x5, other arithmetic: 1.97 us -> 6.81 us  [shards(): arrived = jnp.stack(arrived)]
  transfers between devices with their start and end apart: 14 -> 16, of which waited for: 9 -> 12; matrix products, arithmetic and copies ran while one was open for 7% -> 12% of each run, Pallas kernels for 7% -> 25%
where the time goes in v2:
time: 357 us; the launch traced here: 355 us
  Pallas kernels  179 us (50%)
  waiting for transfers between devices  67 us (19%)
  other arithmetic  39.8 us (11%)
  starting transfers between devices  36.9 us (10%)
  local copies, waits for them, and re-layouts  30.6 us (9%)
    pallas_call x1, Pallas kernels, pick_pieces(): pl.pallas_call(pick_body, in_specs=[pl.BlockSpec(memory_space=pltpu.SMEM)...  65.4 us
    pallas_call x1, Pallas kernels, whole_step(): pl.pallas_call(whole_step_body, in_specs=[IN_SMEM] + [IN_VMEM] * 8, out_s...  50.3 us
    pallas_call x1, Pallas kernels, second_half(): pl.pallas_call(spread_quotients_apart, in_specs=[IN_SMEM] + [IN_VMEM] * 6...  34.2 us
    pallas_call x1, Pallas kernels, first_half(): pl.pallas_call(blur_depth_columns, in_specs=[IN_VMEM] * 3, out_specs=[IN_...  23.5 us
    all_to_all x2, waiting for transfers between devices, shards(): lax.all_to_all(outgoing[:, part], 'block', split_axis=0, concat_axis=0, t...  21.9 us
    ppermute x2, waiting for transfers between devices, shards(): lax.ppermute(total[slab_depth + EDGE:slab_depth + EDGE + HALO].astype(BF1...  11.5 us
    all_to_all x2, starting transfers between devices, shards(): lax.all_to_all(outgoing[:, part], 'block', split_axis=0, concat_axis=0, t...  10.8 us
    ppermute x2, starting transfers between devices, widen(): low = lax.ppermute(cells[slab_depth - HALO:], 'block', up)  9.22 us
  transfers between devices with their start and end apart: 16, of which 12 were waited for; matrix products, arithmetic and copies ran while one was open for 12% of the time, Pallas kernels for 25%

profile of v2, /device:TPU:0, one launch (start us, length us, event | category | flops | bytes accessed | tf_op | source)
XLA Modules:
  0.0 355.1 jit_solution(8280394350400499460)
XLA Ops:
  0.0 2.5 convert_element_type.69
  3.5 4.9 %collective-permute-start.2 = (bf16[13,64,256]{2,1,0:T(8,128)(2,1)}, bf16[13,64,256]{2,1,0:T(8,128)(2,1)S(1)}, u32[]{:S(2)}, u32[]{:S(2)}) collective-permute-start(bf16[13,64,256]{2,1,0:T(8,128)(2,1)} %get-tuple-element.110), channel_id=1, source_target_pairs={{0,1},{1,2},{2,3},{3,4},{4,5},{5,6},{6,7},{8,9},{9,10},{10,11},{11... | collective-permute-start | bytes 1277960 | tf_op jit(solution)/shard_map/ppermute | solution.py:412
  8.4 1.3 collective-permute-start.3
  11.9 65.4 %pick_pieces.1 = bf16[16,256,256]{2,1,0:T(8,128)(2,1)} custom-call(s32[16]{0:T(128)} %select_reduce_fusion.4.index_ref, bf16[16,256,256]{2,1,0:T(8,128)(2,1)} %bitcast.99), custom_call_target="tpu_custom_call" | custom-call | tf_op jit(solution)/shard_map/pick_pieces/pallas_call | solution.py:62
  77.3 3.1 slice_bitcast_fusion.3
  80.4 7.1 %all-to-all-start = ((bf16[8,256,256]{2,1,0:T(8,128)(2,1)}), bf16[8,256,256]{2,1,0:T(8,128)(2,1)S(1)}, u32[]{:S(2)}, u32[]{:S(2)}) async-start(bf16[8,256,256]{2,1,0:T(8,128)(2,1)} %get-tuple-element.111), calls=%async_computation | async-start | bytes 2097152 | tf_op jit(solution)/shard_map/all_to_all | solution.py:309
  88.5 1.1 slice_reduce_fusion.44
  100.5 12.4 %all-to-all-done = bf16[8,256,256]{2,1,0:T(8,128)(2,1)S(1)} async-done(((bf16[8,256,256]{2,1,0:T(8,128)(2,1)}), bf16[8,256,256]{2,1,0:T(8,128)(2,1)S(1)}, u32[]{:S(2)}, u32[]{:S(2)}) %all-to-all-start) | async-done | bytes 1048608 | tf_op jit(solution)/shard_map/all_to_all | solution.py:309
  113.1 3.7 %all-to-all-start.1 = ((bf16[8,256,256]{2,1,0:T(8,128)(2,1)}), bf16[8,256,256]{2,1,0:T(8,128)(2,1)S(1)}, u32[]{:S(2)}, u32[]{:S(2)}) async-start(bf16[8,256,256]{2,1,0:T(8,128)(2,1)} %get-tuple-element.112), calls=%async_computation.1 | async-start | bytes 2097152 | tf_op jit(solution)/shard_map/all_to_all | solution.py:309
  117.6 1.5 fusion.242.depth_ref.depth_back_ref
  119.1 2.3 select_convert_fusion.columns_ref
  121.4 1.9 pad_maximum_fusion.5.offset_ref
  123.3 2.3 select_convert_fusion.1.columns_ref.columns_back_ref
  126.3 3.8 %constant_dynamic-update-slice_fusion.1 = bf16[96,64,256]{2,1,0:T(8,128)(2,1)} fusion(bf16[96,64,256]{2,1,0:T(8,128)(2,1)} %constant_dynamic-update-slice_fusion.2, f32[64,64,256]{2,1,0:T(8,128)} %param.7), kind=kLoop, calls=%fused_computation.234 | loop fusion | flops 1048576 | bytes 6291456
  131.6 1.5 collective-permute-start
  133.1 9.4 %all-to-all-done.1 = bf16[8,256,256]{2,1,0:T(8,128)(2,1)S(1)} async-done(((bf16[8,256,256]{2,1,0:T(8,128)(2,1)}), bf16[8,256,256]{2,1,0:T(8,128)(2,1)S(1)}, u32[]{:S(2)}, u32[]{:S(2)}) %all-to-all-start.1) | async-done | bytes 1048608 | tf_op jit(solution)/shard_map/all_to_all | solution.py:309
  142.6 1.5 collective-permute-start.1
  144.1 2.6 slice_bitcast_fusion.1
  146.7 1.9 pad_maximum_fusion.2.volume_ref
  148.6 23.5 %blur_depth_columns.1 = (f32[2,6144,128]{2,1,0:T(8,128)}, f32[2,2,4096,128]{3,2,1,0:T(8,128)}) custom-call(bf16[128,96]{1,0:T(8,128)(2,1)} %copy.20.depth_ref, bf16[2,256,256]{2,1,0:T(8,128)(2,1)} %select_convert_fusion.columns_ref, bf16[2,96,64,128]{3,2,1,0:T(8,128)(2,1)} %pad_maximum_fusion.2.volume_ref), custom_call_target="tpu_custom_call" | custom-call | flops 5905580032 | bytes 14680064 | tf_op jit(solution)/shard_map/blur_depth_columns/pallas_call | solution.py:207
  172.3 6.3 %collective-permute-done.1 = bf16[8,256,256]{2,1,0:T(8,128)(2,1)} collective-permute-done((bf16[8,256,256]{2,1,0:T(8,128)(2,1)S(1)}, bf16[8,256,256]{2,1,0:T(8,128)(2,1)}, u32[]{:S(2)}, u32[]{:S(2)}) %collective-permute-start.1) | collective-permute-done | bytes 1048608 | tf_op jit(solution)/shard_map/ppermute | solution.py:313
  178.6 1.4 maximum_bitcast_fusion.1
  180.4 6.1 %place_pieces.1 = f32[2,16,256,256]{3,2,1,0:T(8,128)} custom-call(s32[2,16]{1,0:T(2,128)S(1)} %select_reduce_fusion.3.order_ref, s32[2,17]{1,0:T(2,128)S(1)} %convert_reduce_fusion.2.start_ref, f32[2,16]{1,0:T(2,128)S(1)} %convert_divide_fusion.scale_ref, bf16[2,16,256,256]{3,2,1,0:T(8,128)(2,1)S(1)} %pad_maximum_fusion.incoming_ref), custom_call_target="tpu_custom_call" | custom-call | tf_op jit(solution)/shard_map/place_pieces/pallas_call | solution.py:91
  186.5 34.2 %spread_quotients.1 = f32[2,6144,128]{2,1,0:T(8,128)} custom-call(f32[2]{0:T(128)} %pad_maximum_fusion.5.offset_ref, bf16[96,128]{1,0:T(8,128)(2,1)} %fusion.242.depth_ref.depth_back_ref, bf16[2,64,64]{2,1,0:T(8,128)(2,1)} %select_convert_fusion.3.rows_ref, bf16[2,64,64]{2,1,0:T(8,128)(2,1)} %select_convert_fusion.2.rows_back_ref, ...), custom_call_target="tpu_custom_call" | custom-call | tf_op jit(solution)/shard_map/spread_quotients/pallas_call | solution.py:229
  220.7 4.0 %dynamic-slice_bitcast_fusion.1 = f32[96,64,128]{2,1,0:T(8,128)} fusion(f32[2,96,64,128]{3,2,1,0:T(8,128)} %bitcast.94, s32[]{:T(128)S(6)} %select_n.624), kind=kLoop, calls=%fused_computation.7 | loop fusion | bytes 6291460 | tf_op jit(solution)/shard_map/jit(dynamic_index_in_dim)/squeeze | solution.py:423
  227.6 3.0 collective-permute-done.4
  230.6 3.8 %fusion.235 = (bf16[96,64,128]{2,1,0:T(8,128)(2,1)S(1)}, f32[96,64,128]{2,1,0:T(8,128)S(1)}) fusion(f32[96,64,128]{2,1,0:T(8,128)} %collective-permute-done.4, f32[2,96,64,128]{3,2,1,0:T(8,128)} %bitcast.95, s32[]{:T(128)S(6)} %select_n.623), kind=kLoop, calls=%fused_computation.417 | loop fusion | flops 1572864 | bytes 11010052 | tf_op jit(solution)/shard_map/convert.3
  234.5 3.5 collective-permute-start.5
  238.0 1.3 collective-permute-start.6
  239.3 8.1 %collective-permute-done.5 = bf16[13,64,128]{2,1,0:T(8,128)(2,1)S(1)} collective-permute-done((bf16[13,64,128]{2,1,0:T(8,128)(2,1)S(1)}, bf16[13,64,128]{2,1,0:T(8,128)(2,1)S(1)}, u32[]{:S(2)}, u32[]{:S(2)}) %collective-permute-start.5) | collective-permute-done | bytes 213024 | tf_op jit(solution)/shard_map/ppermute | solution.py:434
  247.5 1.7 fusion.233
  249.2 4.4 %collective-permute-start.7 = (bf16[13,64,128]{2,1,0:T(8,128)(2,1)S(1)}, bf16[13,64,128]{2,1,0:T(8,128)(2,1)S(1)}, u32[]{:S(2)}, u32[]{:S(2)}) collective-permute-start(bf16[13,64,128]{2,1,0:T(8,128)(2,1)S(1)} %get-tuple-element.118), channel_id=1, source_target_pairs={{0,1},{1,2},{2,3},{3,4},{4,5},{5,6},{6,7},{8,9},{9,10},{10,11},{11... | collective-permute-start | bytes 638984 | tf_op jit(solution)/shard_map/ppermute | solution.py:412
  254.2 1.5 collective-permute-start.8
  255.7 1.2 collective-permute-done.7
  258.6 5.0 %collective-permute-done.8 = bf16[13,64,128]{2,1,0:T(8,128)(2,1)S(1)} collective-permute-done((bf16[13,64,128]{2,1,0:T(8,128)(2,1)S(1)}, bf16[13,64,128]{2,1,0:T(8,128)(2,1)S(1)}, u32[]{:S(2)}, u32[]{:S(2)}) %collective-permute-start.8) | collective-permute-done | bytes 213024 | tf_op jit(solution)/shard_map/ppermute | solution.py:413
  265.0 3.7 %collective-permute-done.9 = bf16[96,64,128]{2,1,0:T(8,128)(2,1)} collective-permute-done((bf16[96,64,128]{2,1,0:T(8,128)(2,1)}, bf16[96,64,128]{2,1,0:T(8,128)(2,1)}, u32[]{:S(2)}, u32[]{:S(2)}) %collective-permute-start.9) | collective-permute-done | bytes 1572896 | tf_op jit(solution)/shard_map/ppermute | solution.py:418
  268.7 2.1 select_bitcast_fusion.1
  270.8 1.9 pad_maximum_fusion.3.volume_ref
  272.7 50.3 %whole_step.1 = f32[2,6144,128]{2,1,0:T(8,128)} custom-call(f32[2]{0:T(128)} %pad_maximum_fusion.5.offset_ref, bf16[128,96]{1,0:T(8,128)(2,1)} %copy.20.depth_ref, bf16[96,128]{1,0:T(8,128)(2,1)} %fusion.242.depth_ref.depth_back_ref, bf16[2,64,64]{2,1,0:T(8,128)(2,1)} %select_convert_fusion.3.rows_ref, ...), custom_call_target="tpu_custom_call" | custom-call | tf_op jit(solution)/shard_map/whole_step/pallas_call | solution.py:256
  323.0 2.3 dynamic-slice_bitcast_fusion
  325.5 5.5 %collective-permute-done.10 = f32[96,64,128]{2,1,0:T(8,128)S(1)} collective-permute-done((f32[96,64,128]{2,1,0:T(8,128)S(1)}, f32[96,64,128]{2,1,0:T(8,128)S(1)}, u32[]{:S(2)}, u32[]{:S(2)}) %collective-permute-start.10) | collective-permute-done | bytes 3145760 | tf_op jit(solution)/shard_map/ppermute | solution.py:433
  332.1 4.5 %collective-permute-start.11 = (bf16[13,64,128]{2,1,0:T(8,128)(2,1)S(1)}, bf16[13,64,128]{2,1,0:T(8,128)(2,1)S(1)}, u32[]{:S(2)}, u32[]{:S(2)}) collective-permute-start(bf16[13,64,128]{2,1,0:T(8,128)(2,1)S(1)} %get-tuple-element.113), channel_id=1, source_target_pairs={{0,1},{1,2},{2,3},{3,4},{4,5},{5,6},{6,7},{8,9},{9,10},{10,11},{11... | collective-permute-start | bytes 638984 | tf_op jit(solution)/shard_map/ppermute | solution.py:434
  336.7 1.3 collective-permute-start.12
  338.0 3.5 collective-permute-done.11
  341.5 4.7 %collective-permute-done.12 = bf16[13,64,128]{2,1,0:T(8,128)(2,1)S(1)} collective-permute-done((bf16[13,64,128]{2,1,0:T(8,128)(2,1)S(1)}, bf16[13,64,128]{2,1,0:T(8,128)(2,1)S(1)}, u32[]{:S(2)}, u32[]{:S(2)}) %collective-permute-start.12) | collective-permute-done | bytes 213024 | tf_op jit(solution)/shard_map/ppermute | solution.py:437
  346.2 1.4 fusion.1
  347.7 4.1 %collective-permute-done.13 = f32[64,64,128]{2,1,0:T(8,128)S(1)} collective-permute-done((f32[64,64,128]{2,1,0:T(8,128)S(1)}, f32[64,64,128]{2,1,0:T(8,128)S(1)}, u32[]{:S(2)}, u32[]{:S(2)}) %collective-permute-start.13) | collective-permute-done | bytes 2097184 | tf_op jit(solution)/shard_map/ppermute | solution.py:418
  352.7 2.4 pad_maximum_fusion.1
  (200 shorter events, 27.5 us)
Async XLA Ops:
  0.0 10.2 %copy-start.5 = (s32[4,128,1]{1,2,0:T(1,128)S(1)}, s32[4,128,1]{1,2,0:T(1,128)}, u32[]{:S(2)}) copy-start(s32[4,128,1]{1,2,0:T(1,128)} %param.9) | copy-start | bytes 6148
  3.5 122.1 %collective-permute-start.2 = (bf16[13,64,256]{2,1,0:T(8,128)(2,1)}, bf16[13,64,256]{2,1,0:T(8,128)(2,1)S(1)}, u32[]{:S(2)}, u32[]{:S(2)}) collective-permute-start(bf16[13,64,256]{2,1,0:T(8,128)(2,1)} %get-tuple-element.110), channel_id=1, source_target_pairs={{0,1},{1,2},{2,3},{3,4},{4,5},{5,6},{6,7},{8,9},{9,10},{10,11},{11... | collective-permute-start | bytes 1277960 | tf_op jit(solution)/shard_map/ppermute | solution.py:412
  8.4 121.8 %collective-permute-start.3 = (bf16[13,64,256]{2,1,0:T(8,128)(2,1)}, bf16[13,64,256]{2,1,0:T(8,128)(2,1)S(1)}, u32[]{:S(2)}, u32[]{:S(2)}) collective-permute-start(bf16[13,64,256]{2,1,0:T(8,128)(2,1)} %get-tuple-element.109), channel_id=1, source_target_pairs={{1,0},{2,1},{3,2},{4,3},{5,4},{6,5},{7,6},{9,8},{10,9},{11,10},{12... | collective-permute-start | bytes 1277960 | tf_op jit(solution)/shard_map/ppermute | solution.py:413
  80.4 7.1 %copy-start.3 = (f32[4,3,21]{2,0,1:T(4,128)S(1)}, f32[4,3,21]{2,0,1:T(4,128)}, u32[]{:S(2)}) copy-start(f32[4,3,21]{2,0,1:T(4,128)} %param.12) | copy-start | bytes 3028
  80.4 10.4 %copy-start.2 = (s32[4,3]{1,0:T(4,128)S(1)}, s32[4,3]{1,0:T(4,128)}, u32[]{:S(2)}) copy-start(s32[4,3]{1,0:T(4,128)} %param.11) | copy-start | bytes 148
  80.4 14.8 %copy-start.4 = (s32[4,128]{1,0:T(4,128)S(1)}, s32[4,128]{1,0:T(4,128)}, u32[]{:S(2)}) copy-start(s32[4,128]{1,0:T(4,128)} %param.10) | copy-start | bytes 6148
  80.4 16.2 %copy-start.28 = (f32[4]{0:T(128)S(1)}, f32[4]{0:T(128)}, u32[]{:S(2)}) copy-start(f32[4]{0:T(128)} %param.13) | copy-start | bytes 52
  80.4 32.5 %all-to-all-start = ((bf16[8,256,256]{2,1,0:T(8,128)(2,1)}), bf16[8,256,256]{2,1,0:T(8,128)(2,1)S(1)}, u32[]{:S(2)}, u32[]{:S(2)}) async-start(bf16[8,256,256]{2,1,0:T(8,128)(2,1)} %get-tuple-element.111), calls=%async_computation | async-start | bytes 2097152 | tf_op jit(solution)/shard_map/all_to_all | solution.py:309
  91.8 5.5 %copy-start.6 = (bf16[128]{0:T(256)(128)(2,1)}, bf16[128]{0:T(256)(128)(2,1)S(1)}, u32[]{:S(2)}) copy-start(bf16[128]{0:T(256)(128)(2,1)S(1)} %broadcast_in_dim.471) | copy-start | bytes 772
  91.9 21.0 %copy-start.7 = (bf16[128]{0:T(256)(128)(2,1)}, bf16[128]{0:T(256)(128)(2,1)S(1)}, u32[]{:S(2)}) copy-start(bf16[128]{0:T(256)(128)(2,1)S(1)} %broadcast_in_dim.480) | copy-start | bytes 772
  92.1 20.9 %copy-start.8 = (bf16[128]{0:T(256)(128)(2,1)}, bf16[128]{0:T(256)(128)(2,1)S(1)}, u32[]{:S(2)}) copy-start(bf16[128]{0:T(256)(128)(2,1)S(1)} %broadcast_in_dim.483) | copy-start | bytes 772
  92.2 20.7 %copy-start.9 = (bf16[128]{0:T(256)(128)(2,1)}, bf16[128]{0:T(256)(128)(2,1)S(1)}, u32[]{:S(2)}) copy-start(bf16[128]{0:T(256)(128)(2,1)S(1)} %broadcast_in_dim.486) | copy-start | bytes 772
  92.4 20.6 %copy-start.10 = (bf16[128]{0:T(256)(128)(2,1)}, bf16[128]{0:T(256)(128)(2,1)S(1)}, u32[]{:S(2)}) copy-start(bf16[128]{0:T(256)(128)(2,1)S(1)} %broadcast_in_dim.489) | copy-start | bytes 772
  92.6 20.4 %copy-start.11 = (bf16[128]{0:T(256)(128)(2,1)}, bf16[128]{0:T(256)(128)(2,1)S(1)}, u32[]{:S(2)}) copy-start(bf16[128]{0:T(256)(128)(2,1)S(1)} %broadcast_in_dim.492) | copy-start | bytes 772
  92.7 20.3 %copy-start.12 = (bf16[128]{0:T(256)(128)(2,1)}, bf16[128]{0:T(256)(128)(2,1)S(1)}, u32[]{:S(2)}) copy-start(bf16[128]{0:T(256)(128)(2,1)S(1)} %broadcast_in_dim.495) | copy-start | bytes 772
  92.9 20.1 %copy-start.13 = (bf16[128]{0:T(256)(128)(2,1)}, bf16[128]{0:T(256)(128)(2,1)S(1)}, u32[]{:S(2)}) copy-start(bf16[128]{0:T(256)(128)(2,1)S(1)} %broadcast_in_dim.498) | copy-start | bytes 772
  93.0 20.0 %copy-start.14 = (bf16[128]{0:T(256)(128)(2,1)}, bf16[128]{0:T(256)(128)(2,1)S(1)}, u32[]{:S(2)}) copy-start(bf16[128]{0:T(256)(128)(2,1)S(1)} %broadcast_in_dim.501) | copy-start | bytes 772
  93.2 19.8 %copy-start.15 = (bf16[128]{0:T(256)(128)(2,1)}, bf16[128]{0:T(256)(128)(2,1)S(1)}, u32[]{:S(2)}) copy-start(bf16[128]{0:T(256)(128)(2,1)S(1)} %broadcast_in_dim.504) | copy-start | bytes 772
  93.4 19.7 %copy-start.16 = (bf16[128]{0:T(256)(128)(2,1)}, bf16[128]{0:T(256)(128)(2,1)S(1)}, u32[]{:S(2)}) copy-start(bf16[128]{0:T(256)(128)(2,1)S(1)} %broadcast_in_dim.507) | copy-start | bytes 772
  93.5 19.5 %copy-start.17 = (bf16[128]{0:T(256)(128)(2,1)}, bf16[128]{0:T(256)(128)(2,1)S(1)}, u32[]{:S(2)}) copy-start(bf16[128]{0:T(256)(128)(2,1)S(1)} %broadcast_in_dim.510) | copy-start | bytes 772
  93.7 19.3 %copy-start.18 = (bf16[128]{0:T(256)(128)(2,1)}, bf16[128]{0:T(256)(128)(2,1)S(1)}, u32[]{:S(2)}) copy-start(bf16[128]{0:T(256)(128)(2,1)S(1)} %broadcast_in_dim.513) | copy-start | bytes 772
  93.8 19.2 %copy-start.19 = (bf16[128]{0:T(256)(128)(2,1)}, bf16[128]{0:T(256)(128)(2,1)S(1)}, u32[]{:S(2)}) copy-start(bf16[128]{0:T(256)(128)(2,1)S(1)} %broadcast_in_dim.516) | copy-start | bytes 772
  94.0 19.0 %copy-start.20 = (bf16[128]{0:T(256)(128)(2,1)}, bf16[128]{0:T(256)(128)(2,1)S(1)}, u32[]{:S(2)}) copy-start(bf16[128]{0:T(256)(128)(2,1)S(1)} %broadcast_in_dim.519) | copy-start | bytes 772
  94.2 18.9 %copy-start.21 = (bf16[128]{0:T(256)(128)(2,1)}, bf16[128]{0:T(256)(128)(2,1)S(1)}, u32[]{:S(2)}) copy-start(bf16[128]{0:T(256)(128)(2,1)S(1)} %broadcast_in_dim.522) | copy-start | bytes 772
  94.3 18.7 %copy-start.22 = (bf16[128]{0:T(256)(128)(2,1)}, bf16[128]{0:T(256)(128)(2,1)S(1)}, u32[]{:S(2)}) copy-start(bf16[128]{0:T(256)(128)(2,1)S(1)} %broadcast_in_dim.525) | copy-start | bytes 772
  94.5 18.6 %copy-start.23 = (bf16[128]{0:T(256)(128)(2,1)}, bf16[128]{0:T(256)(128)(2,1)S(1)}, u32[]{:S(2)}) copy-start(bf16[128]{0:T(256)(128)(2,1)S(1)} %broadcast_in_dim.528) | copy-start | bytes 772
  94.7 18.4 %copy-start.24 = (bf16[128]{0:T(256)(128)(2,1)}, bf16[128]{0:T(256)(128)(2,1)S(1)}, u32[]{:S(2)}) copy-start(bf16[128]{0:T(256)(128)(2,1)S(1)} %broadcast_in_dim.531) | copy-start | bytes 772
  94.8 18.3 %copy-start.25 = (bf16[128]{0:T(256)(128)(2,1)}, bf16[128]{0:T(256)(128)(2,1)S(1)}, u32[]{:S(2)}) copy-start(bf16[128]{0:T(256)(128)(2,1)S(1)} %broadcast_in_dim.474) | copy-start | bytes 772
  95.0 18.1 %copy-start.26 = (bf16[128]{0:T(256)(128)(2,1)}, bf16[128]{0:T(256)(128)(2,1)S(1)}, u32[]{:S(2)}) copy-start(bf16[128]{0:T(256)(128)(2,1)S(1)} %broadcast_in_dim.477) | copy-start | bytes 772
  95.1 18.0 %copy-start.27 = (s32[128]{0:T(128)}, s32[128]{0:T(128)S(1)}, u32[]{:S(2)}) copy-start(s32[128]{0:T(128)S(1)} %sub.197) | copy-start | bytes 1540
  113.1 29.4 %all-to-all-start.1 = ((bf16[8,256,256]{2,1,0:T(8,128)(2,1)}), bf16[8,256,256]{2,1,0:T(8,128)(2,1)S(1)}, u32[]{:S(2)}, u32[]{:S(2)}) async-start(bf16[8,256,256]{2,1,0:T(8,128)(2,1)} %get-tuple-element.112), calls=%async_computation.1 | async-start | bytes 2097152 | tf_op jit(solution)/shard_map/all_to_all | solution.py:309
  131.6 40.7 %collective-permute-start = (bf16[8,256,256]{2,1,0:T(8,128)(2,1)S(1)}, bf16[8,256,256]{2,1,0:T(8,128)(2,1)S(1)}, u32[]{:S(2)}, u32[]{:S(2)}) collective-permute-start(bf16[8,256,256]{2,1,0:T(8,128)(2,1)S(1)} %all-to-all-done), channel_id=1, source_target_pairs={{16,0},{24,8},{0,16},{8,24},{17,1},{25,9},{1,17},{9,25},{18,2},{26... | collective-permute-start | bytes 3145736 | tf_op jit(solution)/shard_map/ppermute | solution.py:313
  142.6 36.0 %collective-permute-start.1 = (bf16[8,256,256]{2,1,0:T(8,128)(2,1)S(1)}, bf16[8,256,256]{2,1,0:T(8,128)(2,1)}, u32[]{:S(2)}, u32[]{:S(2)}) collective-permute-start(bf16[8,256,256]{2,1,0:T(8,128)(2,1)S(1)} %all-to-all-done.1), channel_id=1, source_target_pairs={{16,0},{24,8},{0,16},{8,24},{17,1},{25,9},{1,17},{9,25},{18,2},{26... | collective-permute-start | bytes 3145736 | tf_op jit(solution)/shard_map/ppermute | solution.py:313
  224.6 6.0 %collective-permute-start.4 = (f32[96,64,128]{2,1,0:T(8,128)}, f32[96,64,128]{2,1,0:T(8,128)}, u32[]{:S(2)}, u32[]{:S(2)}) collective-permute-start(f32[96,64,128]{2,1,0:T(8,128)} %dynamic-slice_bitcast_fusion.1), channel_id=1, source_target_pairs={{0,8},{8,0},{16,24},{24,16},{1,9},{9,1},{17,25},{25,17},{2,10},{10... | collective-permute-start | bytes 9437192 | tf_op jit(solution)/shard_map/ppermute | solution.py:433
  230.6 16.8 %copy-start = (f32[64,64,256]{2,1,0:T(8,128)S(1)}, f32[64,64,256]{2,1,0:T(8,128)}, u32[]{:S(2)}) copy-start(f32[64,64,256]{2,1,0:T(8,128)} %param.7) | copy-start | bytes 12582916
  234.5 12.9 %collective-permute-start.5 = (bf16[13,64,128]{2,1,0:T(8,128)(2,1)S(1)}, bf16[13,64,128]{2,1,0:T(8,128)(2,1)S(1)}, u32[]{:S(2)}, u32[]{:S(2)}) collective-permute-start(bf16[13,64,128]{2,1,0:T(8,128)(2,1)S(1)} %get-tuple-element.115), channel_id=1, source_target_pairs={{0,1},{1,2},{2,3},{3,4},{4,5},{5,6},{6,7},{8,9},{9,10},{10,11},{11... | collective-permute-start | bytes 638984 | tf_op jit(solution)/shard_map/ppermute | solution.py:434
  238.0 9.4 %collective-permute-start.6 = (bf16[13,64,128]{2,1,0:T(8,128)(2,1)S(1)}, bf16[13,64,128]{2,1,0:T(8,128)(2,1)S(1)}, u32[]{:S(2)}, u32[]{:S(2)}) collective-permute-start(bf16[13,64,128]{2,1,0:T(8,128)(2,1)S(1)} %get-tuple-element.116), channel_id=1, source_target_pairs={{1,0},{2,1},{3,2},{4,3},{5,4},{6,5},{7,6},{9,8},{10,9},{11,10},{12... | collective-permute-start | bytes 638984 | tf_op jit(solution)/shard_map/ppermute | solution.py:437
  249.2 7.7 %collective-permute-start.7 = (bf16[13,64,128]{2,1,0:T(8,128)(2,1)S(1)}, bf16[13,64,128]{2,1,0:T(8,128)(2,1)S(1)}, u32[]{:S(2)}, u32[]{:S(2)}) collective-permute-start(bf16[13,64,128]{2,1,0:T(8,128)(2,1)S(1)} %get-tuple-element.118), channel_id=1, source_target_pairs={{0,1},{1,2},{2,3},{3,4},{4,5},{5,6},{6,7},{8,9},{9,10},{10,11},{11... | collective-permute-start | bytes 638984 | tf_op jit(solution)/shard_map/ppermute | solution.py:412
  254.2 9.5 %collective-permute-start.8 = (bf16[13,64,128]{2,1,0:T(8,128)(2,1)S(1)}, bf16[13,64,128]{2,1,0:T(8,128)(2,1)S(1)}, u32[]{:S(2)}, u32[]{:S(2)}) collective-permute-start(bf16[13,64,128]{2,1,0:T(8,128)(2,1)S(1)} %get-tuple-element.117), channel_id=1, source_target_pairs={{1,0},{2,1},{3,2},{4,3},{5,4},{6,5},{7,6},{9,8},{10,9},{11,10},{12... | collective-permute-start | bytes 638984 | tf_op jit(solution)/shard_map/ppermute | solution.py:413
  265.0 3.8 %collective-permute-start.9 = (bf16[96,64,128]{2,1,0:T(8,128)(2,1)}, bf16[96,64,128]{2,1,0:T(8,128)(2,1)}, u32[]{:S(2)}, u32[]{:S(2)}) collective-permute-start(bf16[96,64,128]{2,1,0:T(8,128)(2,1)} %broadcast_dynamic-update-slice_fusion.3), channel_id=1, source_target_pairs={{0,8},{8,0},{16,24},{24,16},{1,9},{9,1},{17,25},{25,17},{2,10},{10... | collective-permute-start | bytes 4718600 | tf_op jit(solution)/shard_map/ppermute | solution.py:418
  323.0 8.0 %copy-start.1 = (f32[2,6144,128]{2,1,0:T(8,128)S(1)}, f32[2,6144,128]{2,1,0:T(8,128)}, u32[]{:S(2)}) copy-start(f32[2,6144,128]{2,1,0:T(8,128)} %whole_step.1) | copy-start | bytes 18874372
  325.3 5.7 %collective-permute-start.10 = (f32[96,64,128]{2,1,0:T(8,128)S(1)}, f32[96,64,128]{2,1,0:T(8,128)S(1)}, u32[]{:S(2)}, u32[]{:S(2)}) collective-permute-start(f32[96,64,128]{2,1,0:T(8,128)S(1)} %dynamic-slice_bitcast_fusion), channel_id=1, source_target_pairs={{0,8},{8,0},{16,24},{24,16},{1,9},{9,1},{17,25},{25,17},{2,10},{10... | collective-permute-start | bytes 9437192 | tf_op jit(solution)/shard_map/ppermute | solution.py:433
  332.1 9.3 %collective-permute-start.11 = (bf16[13,64,128]{2,1,0:T(8,128)(2,1)S(1)}, bf16[13,64,128]{2,1,0:T(8,128)(2,1)S(1)}, u32[]{:S(2)}, u32[]{:S(2)}) collective-permute-start(bf16[13,64,128]{2,1,0:T(8,128)(2,1)S(1)} %get-tuple-element.113), channel_id=1, source_target_pairs={{0,1},{1,2},{2,3},{3,4},{4,5},{5,6},{6,7},{8,9},{9,10},{10,11},{11... | collective-permute-start | bytes 638984 | tf_op jit(solution)/shard_map/ppermute | solution.py:434
  336.7 9.5 %collective-permute-start.12 = (bf16[13,64,128]{2,1,0:T(8,128)(2,1)S(1)}, bf16[13,64,128]{2,1,0:T(8,128)(2,1)S(1)}, u32[]{:S(2)}, u32[]{:S(2)}) collective-permute-start(bf16[13,64,128]{2,1,0:T(8,128)(2,1)S(1)} %get-tuple-element.114), channel_id=1, source_target_pairs={{1,0},{2,1},{3,2},{4,3},{5,4},{6,5},{7,6},{9,8},{10,9},{11,10},{12... | collective-permute-start | bytes 638984 | tf_op jit(solution)/shard_map/ppermute | solution.py:437
  347.7 4.2 %collective-permute-start.13 = (f32[64,64,128]{2,1,0:T(8,128)S(1)}, f32[64,64,128]{2,1,0:T(8,128)S(1)}, u32[]{:S(2)}, u32[]{:S(2)}) collective-permute-start(f32[64,64,128]{2,1,0:T(8,128)S(1)} %fusion.1), channel_id=1, source_target_pairs={{0,8},{8,0},{16,24},{24,16},{1,9},{9,1},{17,25},{25,17},{2,10},{10... | collective-permute-start | bytes 6291464 | tf_op jit(solution)/shard_map/ppermute | solution.py:418

commit v3 on v2

--- a/solution.py
+++ b/solution.py
@@ -46,25 +46,20 @@
     return jnp.sum(jnp.where(inside, kernel[:, None, :], 0.0), axis=2)
 
 
-def pick_body(index_ref, piece_ref, out_ref, sems):
-    copies = [
-        pltpu.make_async_copy(piece_ref.at[index_ref[i]], out_ref.at[i], sems.at[i])
-        for i in range(out_ref.shape[0])
-    ]
-    for copy in copies:
-        copy.start()
-    for copy in copies:
-        copy.wait()
+def pick_body(index_ref, piece_ref, *out_refs):
+    for part, out_ref in enumerate(out_refs):
+        for i in range(out_ref.shape[0]):
+            out_ref[i] = piece_ref[index_ref[i * CAP + part]]
 
 
 def pick_pieces(pieces, index):
-    count = index.shape[0]
+    shape = (index.shape[0] // CAP,) + pieces.shape[1:]
     return pl.pallas_call(
         pick_body,
-        in_specs=[pl.BlockSpec(memory_space=pltpu.SMEM), pl.BlockSpec(memory_space=pl.ANY)],
-        out_specs=pl.BlockSpec(memory_space=pl.ANY),
-        out_shape=jax.ShapeDtypeStruct((count,) + pieces.shape[1:], pieces.dtype),
-        scratch_shapes=[pltpu.SemaphoreType.DMA((count,))],
+        in_specs=[pl.BlockSpec(memory_space=pltpu.SMEM), pl.BlockSpec(memory_space=pltpu.VMEM)],
+        out_specs=[pl.BlockSpec(memory_space=pltpu.VMEM)] * CAP,
+        out_shape=[jax.ShapeDtypeStruct(shape, pieces.dtype)] * CAP,
+        compiler_params=pltpu.CompilerParams(vmem_limit_bytes=48 * 2**20),
         name="pick_pieces",
     )(index, pieces)
 
@@ -303,10 +298,10 @@
     )
     outgoing = pick_pieces(
         pieces.reshape(slot_count, piece_depth * plane_rows, plane_columns), pick
-    ).reshape(block_count, CAP, piece_depth * plane_rows, plane_columns)
+    )
     parts = [[] for _ in range(chips)]
     for part in range(CAP):
-        incoming = lax.all_to_all(outgoing[:, part], "block", split_axis=0, concat_axis=0, tiled=True)
+        incoming = lax.all_to_all(outgoing[part], "block", split_axis=0, concat_axis=0, tiled=True)
         parts[0].append(incoming)
         for hop in range(1, chips):
             parts[hop].append(

time: 357 us -> 289 us (0.81)
  Pallas kernels: 179 us -> 116 us
  local copies, waits for them, and re-layouts: 30.6 us -> 25.7 us
    pallas_call x1, Pallas kernels: 65.4 us -> 2.05 us  [pick_pieces(): pl.pallas_call(pick_body, in_specs=[pl.BlockSpec(memory_space=pltpu.SMEM)...]
  transfers between devices with their start and end apart: 16 -> 16, of which waited for: 12 -> 12; matrix products, arithmetic and copies ran while one was open for 12% -> 14% of each run, Pallas kernels for 25% -> 9%
where the time goes in v3:
time: 289 us; the launch traced here: 287 us
  Pallas kernels  116 us (40%)
  waiting for transfers between devices  68 us (24%)
  other arithmetic  39.4 us (14%)
  starting transfers between devices  36.6 us (13%)
  local copies, waits for them, and re-layouts  25.7 us (9%)
    pallas_call x1, Pallas kernels, whole_step(): pl.pallas_call(whole_step_body, in_specs=[IN_SMEM] + [IN_VMEM] * 8, out_s...  50.3 us
    pallas_call x1, Pallas kernels, second_half(): pl.pallas_call(spread_quotients_apart, in_specs=[IN_SMEM] + [IN_VMEM] * 6...  34.2 us
    pallas_call x1, Pallas kernels, first_half(): pl.pallas_call(blur_depth_columns, in_specs=[IN_VMEM] * 3, out_specs=[IN_...  23.5 us
    all_to_all x2, waiting for transfers between devices, shards(): lax.all_to_all(outgoing[part], 'block', split_axis=0, concat_axis=0, tile...  22.8 us
    ppermute x2, waiting for transfers between devices, shards(): lax.ppermute(total[slab_depth + EDGE:slab_depth + EDGE + HALO].astype(BF1...  11.6 us
    all_to_all x2, starting transfers between devices, shards(): lax.all_to_all(outgoing[part], 'block', split_axis=0, concat_axis=0, tile...  10.7 us
    ppermute x2, starting transfers between devices, widen(): low = lax.ppermute(cells[slab_depth - HALO:], 'block', up)  9.22 us
    ppermute x2, waiting for transfers between devices, shards(): lax.ppermute(half(spread, 1 - my_core), 'view', swap)  8.3 us
  transfers between devices with their start and end apart: 16, of which 12 were waited for; matrix products, arithmetic and copies ran while one was open for 14% of the time, Pallas kernels for 9%

profile of v3, /device:TPU:0, one launch (start us, length us, event | category | flops | bytes accessed | tf_op | source)
XLA Modules:
  0.0 287.0 jit_solution(2667985885520640206)
XLA Ops:
  0.0 2.6 convert_element_type.69
  3.6 4.9 %collective-permute-start.2 = (bf16[13,64,256]{2,1,0:T(8,128)(2,1)}, bf16[13,64,256]{2,1,0:T(8,128)(2,1)S(1)}, u32[]{:S(2)}, u32[]{:S(2)}) collective-permute-start(bf16[13,64,256]{2,1,0:T(8,128)(2,1)} %get-tuple-element.114), channel_id=1, source_target_pairs={{0,1},{1,2},{2,3},{3,4},{4,5},{5,6},{6,7},{8,9},{9,10},{10,11},{11... | collective-permute-start | bytes 1277960 | tf_op jit(solution)/shard_map/ppermute | solution.py:407
  8.5 1.3 collective-permute-start.3
  11.4 2.0 pick_pieces.1
  13.5 7.0 %all-to-all-start = ((bf16[8,256,256]{2,1,0:T(8,128)(2,1)}), bf16[8,256,256]{2,1,0:T(8,128)(2,1)S(1)}, u32[]{:S(2)}, u32[]{:S(2)}) async-start(bf16[8,256,256]{2,1,0:T(8,128)(2,1)} %get-tuple-element.8), calls=%async_computation | async-start | bytes 2097152 | tf_op jit(solution)/shard_map/all_to_all | solution.py:304
  21.4 1.1 slice_reduce_fusion.44
  33.7 13.9 %all-to-all-done = bf16[8,256,256]{2,1,0:T(8,128)(2,1)S(1)} async-done(((bf16[8,256,256]{2,1,0:T(8,128)(2,1)}), bf16[8,256,256]{2,1,0:T(8,128)(2,1)S(1)}, u32[]{:S(2)}, u32[]{:S(2)}) %all-to-all-start) | async-done | bytes 1048608 | tf_op jit(solution)/shard_map/all_to_all | solution.py:304
  47.5 3.7 %all-to-all-start.1 = ((bf16[8,256,256]{2,1,0:T(8,128)(2,1)}), bf16[8,256,256]{2,1,0:T(8,128)(2,1)S(1)}, u32[]{:S(2)}, u32[]{:S(2)}) async-start(bf16[8,256,256]{2,1,0:T(8,128)(2,1)} %get-tuple-element.9), calls=%async_computation.1 | async-start | bytes 2097152 | tf_op jit(solution)/shard_map/all_to_all | solution.py:304
  52.0 1.5 fusion.242.depth_ref.depth_back_ref
  53.5 2.3 select_convert_fusion.columns_ref
  55.8 1.9 pad_maximum_fusion.5.offset_ref
  57.7 2.3 select_convert_fusion.1.columns_ref.columns_back_ref
  60.7 3.8 %constant_dynamic-update-slice_fusion.1 = bf16[96,64,256]{2,1,0:T(8,128)(2,1)} fusion(bf16[96,64,256]{2,1,0:T(8,128)(2,1)} %constant_dynamic-update-slice_fusion.2, f32[64,64,256]{2,1,0:T(8,128)} %param.7), kind=kLoop, calls=%fused_computation.232 | loop fusion | flops 1048576 | bytes 6291456
  66.0 1.5 collective-permute-start
  67.5 8.9 %all-to-all-done.1 = bf16[8,256,256]{2,1,0:T(8,128)(2,1)S(1)} async-done(((bf16[8,256,256]{2,1,0:T(8,128)(2,1)}), bf16[8,256,256]{2,1,0:T(8,128)(2,1)S(1)}, u32[]{:S(2)}, u32[]{:S(2)}) %all-to-all-start.1) | async-done | bytes 1048608 | tf_op jit(solution)/shard_map/all_to_all | solution.py:304
  76.5 1.5 collective-permute-start.1
  78.0 2.6 slice_bitcast_fusion.1
  80.6 1.9 pad_maximum_fusion.2.volume_ref
  82.5 23.5 %blur_depth_columns.1 = (f32[2,6144,128]{2,1,0:T(8,128)}, f32[2,2,4096,128]{3,2,1,0:T(8,128)}) custom-call(bf16[128,96]{1,0:T(8,128)(2,1)} %copy.16.depth_ref, bf16[2,256,256]{2,1,0:T(8,128)(2,1)} %select_convert_fusion.columns_ref, bf16[2,96,64,128]{3,2,1,0:T(8,128)(2,1)} %pad_maximum_fusion.2.volume_ref), custom_call_target="tpu_custom_call" | custom-call | flops 5905580032 | bytes 14680064 | tf_op jit(solution)/shard_map/blur_depth_columns/pallas_call | solution.py:202
  106.2 6.7 %collective-permute-done.1 = bf16[8,256,256]{2,1,0:T(8,128)(2,1)} collective-permute-done((bf16[8,256,256]{2,1,0:T(8,128)(2,1)S(1)}, bf16[8,256,256]{2,1,0:T(8,128)(2,1)}, u32[]{:S(2)}, u32[]{:S(2)}) %collective-permute-start.1) | collective-permute-done | bytes 1048608 | tf_op jit(solution)/shard_map/ppermute | solution.py:308
  112.8 1.4 maximum_bitcast_fusion.1
  114.6 6.0 %place_pieces.1 = f32[2,16,256,256]{3,2,1,0:T(8,128)} custom-call(s32[2,16]{1,0:T(2,128)S(1)} %select_reduce_fusion.3.order_ref, s32[2,17]{1,0:T(2,128)S(1)} %convert_reduce_fusion.2.start_ref, f32[2,16]{1,0:T(2,128)S(1)} %convert_divide_fusion.scale_ref, bf16[2,16,256,256]{3,2,1,0:T(8,128)(2,1)S(1)} %pad_maximum_fusion.incoming_ref), custom_call_target="tpu_custom_call" | custom-call | tf_op jit(solution)/shard_map/place_pieces/pallas_call | solution.py:86
  120.6 34.2 %spread_quotients.1 = f32[2,6144,128]{2,1,0:T(8,128)} custom-call(f32[2]{0:T(128)} %pad_maximum_fusion.5.offset_ref, bf16[96,128]{1,0:T(8,128)(2,1)} %fusion.242.depth_ref.depth_back_ref, bf16[2,64,64]{2,1,0:T(8,128)(2,1)} %select_convert_fusion.3.rows_ref, bf16[2,64,64]{2,1,0:T(8,128)(2,1)} %select_convert_fusion.2.rows_back_ref, ...), custom_call_target="tpu_custom_call" | custom-call | tf_op jit(solution)/shard_map/spread_quotients/pallas_call | solution.py:224
  154.8 2.1 dynamic-slice_bitcast_fusion.1
  160.0 2.8 collective-permute-done.4
  162.8 3.8 %fusion.235 = (bf16[96,64,128]{2,1,0:T(8,128)(2,1)S(1)}, f32[96,64,128]{2,1,0:T(8,128)S(1)}) fusion(f32[96,64,128]{2,1,0:T(8,128)} %collective-permute-done.4, f32[2,96,64,128]{3,2,1,0:T(8,128)} %bitcast.87, s32[]{:T(128)S(6)} %select_n.623), kind=kLoop, calls=%fused_computation.415 | loop fusion | flops 1572864 | bytes 11010052 | tf_op jit(solution)/shard_map/convert.3
  166.6 3.4 %collective-permute-start.5 = (bf16[13,64,128]{2,1,0:T(8,128)(2,1)S(1)}, bf16[13,64,128]{2,1,0:T(8,128)(2,1)S(1)}, u32[]{:S(2)}, u32[]{:S(2)}) collective-permute-start(bf16[13,64,128]{2,1,0:T(8,128)(2,1)S(1)} %get-tuple-element.117), channel_id=1, source_target_pairs={{0,1},{1,2},{2,3},{3,4},{4,5},{5,6},{6,7},{8,9},{9,10},{10,11},{11... | collective-permute-start | bytes 638984 | tf_op jit(solution)/shard_map/ppermute | solution.py:429
  170.0 1.3 collective-permute-start.6
  171.3 8.1 %collective-permute-done.5 = bf16[13,64,128]{2,1,0:T(8,128)(2,1)S(1)} collective-permute-done((bf16[13,64,128]{2,1,0:T(8,128)(2,1)S(1)}, bf16[13,64,128]{2,1,0:T(8,128)(2,1)S(1)}, u32[]{:S(2)}, u32[]{:S(2)}) %collective-permute-start.5) | collective-permute-done | bytes 213024 | tf_op jit(solution)/shard_map/ppermute | solution.py:429
  179.5 1.6 fusion.233
  181.2 4.4 %collective-permute-start.7 = (bf16[13,64,128]{2,1,0:T(8,128)(2,1)S(1)}, bf16[13,64,128]{2,1,0:T(8,128)(2,1)S(1)}, u32[]{:S(2)}, u32[]{:S(2)}) collective-permute-start(bf16[13,64,128]{2,1,0:T(8,128)(2,1)S(1)} %get-tuple-element.120), channel_id=1, source_target_pairs={{0,1},{1,2},{2,3},{3,4},{4,5},{5,6},{6,7},{8,9},{9,10},{10,11},{11... | collective-permute-start | bytes 638984 | tf_op jit(solution)/shard_map/ppermute | solution.py:407
  186.2 1.5 collective-permute-start.8
  187.7 1.2 collective-permute-done.7
  190.6 4.9 %collective-permute-done.8 = bf16[13,64,128]{2,1,0:T(8,128)(2,1)S(1)} collective-permute-done((bf16[13,64,128]{2,1,0:T(8,128)(2,1)S(1)}, bf16[13,64,128]{2,1,0:T(8,128)(2,1)S(1)}, u32[]{:S(2)}, u32[]{:S(2)}) %collective-permute-start.8) | collective-permute-done | bytes 213024 | tf_op jit(solution)/shard_map/ppermute | solution.py:408
  196.9 3.7 %collective-permute-done.9 = bf16[96,64,128]{2,1,0:T(8,128)(2,1)} collective-permute-done((bf16[96,64,128]{2,1,0:T(8,128)(2,1)}, bf16[96,64,128]{2,1,0:T(8,128)(2,1)}, u32[]{:S(2)}, u32[]{:S(2)}) %collective-permute-start.9) | collective-permute-done | bytes 1572896 | tf_op jit(solution)/shard_map/ppermute | solution.py:413
  200.6 2.1 select_bitcast_fusion.1
  202.7 1.9 pad_maximum_fusion.3.volume_ref
  204.6 50.3 %whole_step.1 = f32[2,6144,128]{2,1,0:T(8,128)} custom-call(f32[2]{0:T(128)} %pad_maximum_fusion.5.offset_ref, bf16[128,96]{1,0:T(8,128)(2,1)} %copy.16.depth_ref, bf16[96,128]{1,0:T(8,128)(2,1)} %fusion.242.depth_ref.depth_back_ref, bf16[2,64,64]{2,1,0:T(8,128)(2,1)} %select_convert_fusion.3.rows_ref, ...), custom_call_target="tpu_custom_call" | custom-call | tf_op jit(solution)/shard_map/whole_step/pallas_call | solution.py:251
  254.9 2.3 dynamic-slice_bitcast_fusion
  257.4 5.5 %collective-permute-done.10 = f32[96,64,128]{2,1,0:T(8,128)S(1)} collective-permute-done((f32[96,64,128]{2,1,0:T(8,128)S(1)}, f32[96,64,128]{2,1,0:T(8,128)S(1)}, u32[]{:S(2)}, u32[]{:S(2)}) %collective-permute-start.10) | collective-permute-done | bytes 3145760 | tf_op jit(solution)/shard_map/ppermute | solution.py:428
  262.9 1.1 fusion.232
  264.0 4.5 %collective-permute-start.11 = (bf16[13,64,128]{2,1,0:T(8,128)(2,1)S(1)}, bf16[13,64,128]{2,1,0:T(8,128)(2,1)S(1)}, u32[]{:S(2)}, u32[]{:S(2)}) collective-permute-start(bf16[13,64,128]{2,1,0:T(8,128)(2,1)S(1)} %get-tuple-element.115), channel_id=1, source_target_pairs={{0,1},{1,2},{2,3},{3,4},{4,5},{5,6},{6,7},{8,9},{9,10},{10,11},{11... | collective-permute-start | bytes 638984 | tf_op jit(solution)/shard_map/ppermute | solution.py:429
  268.6 1.3 collective-permute-start.12
  269.9 3.5 %collective-permute-done.11 = bf16[13,64,128]{2,1,0:T(8,128)(2,1)S(1)} collective-permute-done((bf16[13,64,128]{2,1,0:T(8,128)(2,1)S(1)}, bf16[13,64,128]{2,1,0:T(8,128)(2,1)S(1)}, u32[]{:S(2)}, u32[]{:S(2)}) %collective-permute-start.11) | collective-permute-done | bytes 213024 | tf_op jit(solution)/shard_map/ppermute | solution.py:429
  273.4 4.7 %collective-permute-done.12 = bf16[13,64,128]{2,1,0:T(8,128)(2,1)S(1)} collective-permute-done((bf16[13,64,128]{2,1,0:T(8,128)(2,1)S(1)}, bf16[13,64,128]{2,1,0:T(8,128)(2,1)S(1)}, u32[]{:S(2)}, u32[]{:S(2)}) %collective-permute-start.12) | collective-permute-done | bytes 213024 | tf_op jit(solution)/shard_map/ppermute | solution.py:432
  278.1 1.4 fusion.1
  279.6 4.1 %collective-permute-done.13 = f32[64,64,128]{2,1,0:T(8,128)S(1)} collective-permute-done((f32[64,64,128]{2,1,0:T(8,128)S(1)}, f32[64,64,128]{2,1,0:T(8,128)S(1)}, u32[]{:S(2)}, u32[]{:S(2)}) %collective-permute-start.13) | collective-permute-done | bytes 2097184 | tf_op jit(solution)/shard_map/ppermute | solution.py:413
  284.6 2.4 pad_maximum_fusion.1
  (201 shorter events, 25.9 us)
Async XLA Ops:
  0.0 10.3 %copy-start.6 = (s32[4,128,1]{1,2,0:T(1,128)S(1)}, s32[4,128,1]{1,2,0:T(1,128)}, u32[]{:S(2)}) copy-start(s32[4,128,1]{1,2,0:T(1,128)} %param.9) | copy-start | bytes 6148
  0.0 11.4 %copy-start = (bf16[1,16,4,64,256]{4,3,2,1,0:T(8,128)(2,1)S(1)}, bf16[1,16,4,64,256]{4,3,2,1,0:T(8,128)(2,1)}, u32[]{:S(2)}) copy-start(bf16[1,16,4,64,256]{4,3,2,1,0:T(8,128)(2,1)} %param.8) | copy-start | bytes 6291460
  3.6 56.3 %collective-permute-start.2 = (bf16[13,64,256]{2,1,0:T(8,128)(2,1)}, bf16[13,64,256]{2,1,0:T(8,128)(2,1)S(1)}, u32[]{:S(2)}, u32[]{:S(2)}) collective-permute-start(bf16[13,64,256]{2,1,0:T(8,128)(2,1)} %get-tuple-element.114), channel_id=1, source_target_pairs={{0,1},{1,2},{2,3},{3,4},{4,5},{5,6},{6,7},{8,9},{9,10},{10,11},{11... | collective-permute-start | bytes 1277960 | tf_op jit(solution)/shard_map/ppermute | solution.py:407
  8.5 56.1 %collective-permute-start.3 = (bf16[13,64,256]{2,1,0:T(8,128)(2,1)}, bf16[13,64,256]{2,1,0:T(8,128)(2,1)S(1)}, u32[]{:S(2)}, u32[]{:S(2)}) collective-permute-start(bf16[13,64,256]{2,1,0:T(8,128)(2,1)} %get-tuple-element.113), channel_id=1, source_target_pairs={{1,0},{2,1},{3,2},{4,3},{5,4},{6,5},{7,6},{9,8},{10,9},{11,10},{12... | collective-permute-start | bytes 1277960 | tf_op jit(solution)/shard_map/ppermute | solution.py:408
  11.4 9.1 %copy-start.4 = (f32[4,3,21]{2,0,1:T(4,128)S(1)}, f32[4,3,21]{2,0,1:T(4,128)}, u32[]{:S(2)}) copy-start(f32[4,3,21]{2,0,1:T(4,128)} %param.12) | copy-start | bytes 3028
  11.4 12.4 %copy-start.3 = (s32[4,3]{1,0:T(4,128)S(1)}, s32[4,3]{1,0:T(4,128)}, u32[]{:S(2)}) copy-start(s32[4,3]{1,0:T(4,128)} %param.11) | copy-start | bytes 148
  11.4 16.7 %copy-start.5 = (s32[4,128]{1,0:T(4,128)S(1)}, s32[4,128]{1,0:T(4,128)}, u32[]{:S(2)}) copy-start(s32[4,128]{1,0:T(4,128)} %param.10) | copy-start | bytes 6148
  11.4 18.1 %copy-start.29 = (f32[4]{0:T(128)S(1)}, f32[4]{0:T(128)}, u32[]{:S(2)}) copy-start(f32[4]{0:T(128)} %param.13) | copy-start | bytes 52
  13.5 34.0 %all-to-all-start = ((bf16[8,256,256]{2,1,0:T(8,128)(2,1)}), bf16[8,256,256]{2,1,0:T(8,128)(2,1)S(1)}, u32[]{:S(2)}, u32[]{:S(2)}) async-start(bf16[8,256,256]{2,1,0:T(8,128)(2,1)} %get-tuple-element.8), calls=%async_computation | async-start | bytes 2097152 | tf_op jit(solution)/shard_map/all_to_all | solution.py:304
  24.7 7.1 %copy-start.7 = (bf16[128]{0:T(256)(128)(2,1)}, bf16[128]{0:T(256)(128)(2,1)S(1)}, u32[]{:S(2)}) copy-start(bf16[128]{0:T(256)(128)(2,1)S(1)} %broadcast_in_dim.471) | copy-start | bytes 772
  24.9 7.0 %copy-start.8 = (bf16[128]{0:T(256)(128)(2,1)}, bf16[128]{0:T(256)(128)(2,1)S(1)}, u32[]{:S(2)}) copy-start(bf16[128]{0:T(256)(128)(2,1)S(1)} %broadcast_in_dim.480) | copy-start | bytes 772
  25.0 6.8 %copy-start.9 = (bf16[128]{0:T(256)(128)(2,1)}, bf16[128]{0:T(256)(128)(2,1)S(1)}, u32[]{:S(2)}) copy-start(bf16[128]{0:T(256)(128)(2,1)S(1)} %broadcast_in_dim.483) | copy-start | bytes 772
  25.2 6.6 %copy-start.10 = (bf16[128]{0:T(256)(128)(2,1)}, bf16[128]{0:T(256)(128)(2,1)S(1)}, u32[]{:S(2)}) copy-start(bf16[128]{0:T(256)(128)(2,1)S(1)} %broadcast_in_dim.486) | copy-start | bytes 772
  25.3 6.5 %copy-start.11 = (bf16[128]{0:T(256)(128)(2,1)}, bf16[128]{0:T(256)(128)(2,1)S(1)}, u32[]{:S(2)}) copy-start(bf16[128]{0:T(256)(128)(2,1)S(1)} %broadcast_in_dim.489) | copy-start | bytes 772
  25.5 6.3 %copy-start.12 = (bf16[128]{0:T(256)(128)(2,1)}, bf16[128]{0:T(256)(128)(2,1)S(1)}, u32[]{:S(2)}) copy-start(bf16[128]{0:T(256)(128)(2,1)S(1)} %broadcast_in_dim.492) | copy-start | bytes 772
  25.7 6.2 %copy-start.13 = (bf16[128]{0:T(256)(128)(2,1)}, bf16[128]{0:T(256)(128)(2,1)S(1)}, u32[]{:S(2)}) copy-start(bf16[128]{0:T(256)(128)(2,1)S(1)} %broadcast_in_dim.495) | copy-start | bytes 772
  25.8 6.0 %copy-start.14 = (bf16[128]{0:T(256)(128)(2,1)}, bf16[128]{0:T(256)(128)(2,1)S(1)}, u32[]{:S(2)}) copy-start(bf16[128]{0:T(256)(128)(2,1)S(1)} %broadcast_in_dim.498) | copy-start | bytes 772
  26.0 5.9 %copy-start.15 = (bf16[128]{0:T(256)(128)(2,1)}, bf16[128]{0:T(256)(128)(2,1)S(1)}, u32[]{:S(2)}) copy-start(bf16[128]{0:T(256)(128)(2,1)S(1)} %broadcast_in_dim.501) | copy-start | bytes 772
  26.1 5.7 %copy-start.16 = (bf16[128]{0:T(256)(128)(2,1)}, bf16[128]{0:T(256)(128)(2,1)S(1)}, u32[]{:S(2)}) copy-start(bf16[128]{0:T(256)(128)(2,1)S(1)} %broadcast_in_dim.504) | copy-start | bytes 772
  26.3 5.6 %copy-start.17 = (bf16[128]{0:T(256)(128)(2,1)}, bf16[128]{0:T(256)(128)(2,1)S(1)}, u32[]{:S(2)}) copy-start(bf16[128]{0:T(256)(128)(2,1)S(1)} %broadcast_in_dim.507) | copy-start | bytes 772
  26.5 5.4 %copy-start.18 = (bf16[128]{0:T(256)(128)(2,1)}, bf16[128]{0:T(256)(128)(2,1)S(1)}, u32[]{:S(2)}) copy-start(bf16[128]{0:T(256)(128)(2,1)S(1)} %broadcast_in_dim.510) | copy-start | bytes 772
  26.6 5.3 %copy-start.19 = (bf16[128]{0:T(256)(128)(2,1)}, bf16[128]{0:T(256)(128)(2,1)S(1)}, u32[]{:S(2)}) copy-start(bf16[128]{0:T(256)(128)(2,1)S(1)} %broadcast_in_dim.513) | copy-start | bytes 772
  26.8 5.1 %copy-start.20 = (bf16[128]{0:T(256)(128)(2,1)}, bf16[128]{0:T(256)(128)(2,1)S(1)}, u32[]{:S(2)}) copy-start(bf16[128]{0:T(256)(128)(2,1)S(1)} %broadcast_in_dim.516) | copy-start | bytes 772
  26.9 5.0 %copy-start.21 = (bf16[128]{0:T(256)(128)(2,1)}, bf16[128]{0:T(256)(128)(2,1)S(1)}, u32[]{:S(2)}) copy-start(bf16[128]{0:T(256)(128)(2,1)S(1)} %broadcast_in_dim.519) | copy-start | bytes 772
  27.1 4.8 %copy-start.22 = (bf16[128]{0:T(256)(128)(2,1)}, bf16[128]{0:T(256)(128)(2,1)S(1)}, u32[]{:S(2)}) copy-start(bf16[128]{0:T(256)(128)(2,1)S(1)} %broadcast_in_dim.522) | copy-start | bytes 772
  27.3 4.7 %copy-start.23 = (bf16[128]{0:T(256)(128)(2,1)}, bf16[128]{0:T(256)(128)(2,1)S(1)}, u32[]{:S(2)}) copy-start(bf16[128]{0:T(256)(128)(2,1)S(1)} %broadcast_in_dim.525) | copy-start | bytes 772
  27.4 4.5 %copy-start.24 = (bf16[128]{0:T(256)(128)(2,1)}, bf16[128]{0:T(256)(128)(2,1)S(1)}, u32[]{:S(2)}) copy-start(bf16[128]{0:T(256)(128)(2,1)S(1)} %broadcast_in_dim.528) | copy-start | bytes 772
  27.6 4.4 %copy-start.25 = (bf16[128]{0:T(256)(128)(2,1)}, bf16[128]{0:T(256)(128)(2,1)S(1)}, u32[]{:S(2)}) copy-start(bf16[128]{0:T(256)(128)(2,1)S(1)} %broadcast_in_dim.531) | copy-start | bytes 772
  27.8 4.2 %copy-start.26 = (bf16[128]{0:T(256)(128)(2,1)}, bf16[128]{0:T(256)(128)(2,1)S(1)}, u32[]{:S(2)}) copy-start(bf16[128]{0:T(256)(128)(2,1)S(1)} %broadcast_in_dim.474) | copy-start | bytes 772
  27.9 4.1 %copy-start.27 = (bf16[128]{0:T(256)(128)(2,1)}, bf16[128]{0:T(256)(128)(2,1)S(1)}, u32[]{:S(2)}) copy-start(bf16[128]{0:T(256)(128)(2,1)S(1)} %broadcast_in_dim.477) | copy-start | bytes 772
  28.1 3.9 %copy-start.28 = (s32[128]{0:T(128)}, s32[128]{0:T(128)S(1)}, u32[]{:S(2)}) copy-start(s32[128]{0:T(128)S(1)} %sub.197) | copy-start | bytes 1540
  47.5 28.9 %all-to-all-start.1 = ((bf16[8,256,256]{2,1,0:T(8,128)(2,1)}), bf16[8,256,256]{2,1,0:T(8,128)(2,1)S(1)}, u32[]{:S(2)}, u32[]{:S(2)}) async-start(bf16[8,256,256]{2,1,0:T(8,128)(2,1)} %get-tuple-element.9), calls=%async_computation.1 | async-start | bytes 2097152 | tf_op jit(solution)/shard_map/all_to_all | solution.py:304
  66.0 40.2 %collective-permute-start = (bf16[8,256,256]{2,1,0:T(8,128)(2,1)S(1)}, bf16[8,256,256]{2,1,0:T(8,128)(2,1)S(1)}, u32[]{:S(2)}, u32[]{:S(2)}) collective-permute-start(bf16[8,256,256]{2,1,0:T(8,128)(2,1)S(1)} %all-to-all-done), channel_id=1, source_target_pairs={{16,0},{24,8},{0,16},{8,24},{17,1},{25,9},{1,17},{9,25},{18,2},{26... | collective-permute-start | bytes 3145736 | tf_op jit(solution)/shard_map/ppermute | solution.py:308
  76.5 36.4 %collective-permute-start.1 = (bf16[8,256,256]{2,1,0:T(8,128)(2,1)S(1)}, bf16[8,256,256]{2,1,0:T(8,128)(2,1)}, u32[]{:S(2)}, u32[]{:S(2)}) collective-permute-start(bf16[8,256,256]{2,1,0:T(8,128)(2,1)S(1)} %all-to-all-done.1), channel_id=1, source_target_pairs={{16,0},{24,8},{0,16},{8,24},{17,1},{25,9},{1,17},{9,25},{18,2},{26... | collective-permute-start | bytes 3145736 | tf_op jit(solution)/shard_map/ppermute | solution.py:308
  157.0 5.9 %collective-permute-start.4 = (f32[96,64,128]{2,1,0:T(8,128)S(1)}, f32[96,64,128]{2,1,0:T(8,128)}, u32[]{:S(2)}, u32[]{:S(2)}) collective-permute-start(f32[96,64,128]{2,1,0:T(8,128)S(1)} %dynamic-slice_bitcast_fusion.1), channel_id=1, source_target_pairs={{0,8},{8,0},{16,24},{24,16},{1,9},{9,1},{17,25},{25,17},{2,10},{10... | collective-permute-start | bytes 9437192 | tf_op jit(solution)/shard_map/ppermute | solution.py:428
  162.8 16.7 %copy-start.1 = (f32[64,64,256]{2,1,0:T(8,128)S(1)}, f32[64,64,256]{2,1,0:T(8,128)}, u32[]{:S(2)}) copy-start(f32[64,64,256]{2,1,0:T(8,128)} %param.7) | copy-start | bytes 12582916
  166.6 12.8 %collective-permute-start.5 = (bf16[13,64,128]{2,1,0:T(8,128)(2,1)S(1)}, bf16[13,64,128]{2,1,0:T(8,128)(2,1)S(1)}, u32[]{:S(2)}, u32[]{:S(2)}) collective-permute-start(bf16[13,64,128]{2,1,0:T(8,128)(2,1)S(1)} %get-tuple-element.117), channel_id=1, source_target_pairs={{0,1},{1,2},{2,3},{3,4},{4,5},{5,6},{6,7},{8,9},{9,10},{10,11},{11... | collective-permute-start | bytes 638984 | tf_op jit(solution)/shard_map/ppermute | solution.py:429
  170.0 9.4 %collective-permute-start.6 = (bf16[13,64,128]{2,1,0:T(8,128)(2,1)S(1)}, bf16[13,64,128]{2,1,0:T(8,128)(2,1)S(1)}, u32[]{:S(2)}, u32[]{:S(2)}) collective-permute-start(bf16[13,64,128]{2,1,0:T(8,128)(2,1)S(1)} %get-tuple-element.118), channel_id=1, source_target_pairs={{1,0},{2,1},{3,2},{4,3},{5,4},{6,5},{7,6},{9,8},{10,9},{11,10},{12... | collective-permute-start | bytes 638984 | tf_op jit(solution)/shard_map/ppermute | solution.py:432
  181.2 7.7 %collective-permute-start.7 = (bf16[13,64,128]{2,1,0:T(8,128)(2,1)S(1)}, bf16[13,64,128]{2,1,0:T(8,128)(2,1)S(1)}, u32[]{:S(2)}, u32[]{:S(2)}) collective-permute-start(bf16[13,64,128]{2,1,0:T(8,128)(2,1)S(1)} %get-tuple-element.120), channel_id=1, source_target_pairs={{0,1},{1,2},{2,3},{3,4},{4,5},{5,6},{6,7},{8,9},{9,10},{10,11},{11... | collective-permute-start | bytes 638984 | tf_op jit(solution)/shard_map/ppermute | solution.py:407
  186.2 9.4 %collective-permute-start.8 = (bf16[13,64,128]{2,1,0:T(8,128)(2,1)S(1)}, bf16[13,64,128]{2,1,0:T(8,128)(2,1)S(1)}, u32[]{:S(2)}, u32[]{:S(2)}) collective-permute-start(bf16[13,64,128]{2,1,0:T(8,128)(2,1)S(1)} %get-tuple-element.119), channel_id=1, source_target_pairs={{1,0},{2,1},{3,2},{4,3},{5,4},{6,5},{7,6},{9,8},{10,9},{11,10},{12... | collective-permute-start | bytes 638984 | tf_op jit(solution)/shard_map/ppermute | solution.py:408
  196.9 3.8 %collective-permute-start.9 = (bf16[96,64,128]{2,1,0:T(8,128)(2,1)}, bf16[96,64,128]{2,1,0:T(8,128)(2,1)}, u32[]{:S(2)}, u32[]{:S(2)}) collective-permute-start(bf16[96,64,128]{2,1,0:T(8,128)(2,1)} %broadcast_dynamic-update-slice_fusion.3), channel_id=1, source_target_pairs={{0,8},{8,0},{16,24},{24,16},{1,9},{9,1},{17,25},{25,17},{2,10},{10... | collective-permute-start | bytes 4718600 | tf_op jit(solution)/shard_map/ppermute | solution.py:413
  254.9 8.0 %copy-start.2 = (f32[2,6144,128]{2,1,0:T(8,128)S(1)}, f32[2,6144,128]{2,1,0:T(8,128)}, u32[]{:S(2)}) copy-start(f32[2,6144,128]{2,1,0:T(8,128)} %whole_step.1) | copy-start | bytes 18874372
  257.2 5.7 %collective-permute-start.10 = (f32[96,64,128]{2,1,0:T(8,128)S(1)}, f32[96,64,128]{2,1,0:T(8,128)S(1)}, u32[]{:S(2)}, u32[]{:S(2)}) collective-permute-start(f32[96,64,128]{2,1,0:T(8,128)S(1)} %dynamic-slice_bitcast_fusion), channel_id=1, source_target_pairs={{0,8},{8,0},{16,24},{24,16},{1,9},{9,1},{17,25},{25,17},{2,10},{10... | collective-permute-start | bytes 9437192 | tf_op jit(solution)/shard_map/ppermute | solution.py:428
  264.0 9.3 %collective-permute-start.11 = (bf16[13,64,128]{2,1,0:T(8,128)(2,1)S(1)}, bf16[13,64,128]{2,1,0:T(8,128)(2,1)S(1)}, u32[]{:S(2)}, u32[]{:S(2)}) collective-permute-start(bf16[13,64,128]{2,1,0:T(8,128)(2,1)S(1)} %get-tuple-element.115), channel_id=1, source_target_pairs={{0,1},{1,2},{2,3},{3,4},{4,5},{5,6},{6,7},{8,9},{9,10},{10,11},{11... | collective-permute-start | bytes 638984 | tf_op jit(solution)/shard_map/ppermute | solution.py:429
  268.6 9.5 %collective-permute-start.12 = (bf16[13,64,128]{2,1,0:T(8,128)(2,1)S(1)}, bf16[13,64,128]{2,1,0:T(8,128)(2,1)S(1)}, u32[]{:S(2)}, u32[]{:S(2)}) collective-permute-start(bf16[13,64,128]{2,1,0:T(8,128)(2,1)S(1)} %get-tuple-element.116), channel_id=1, source_target_pairs={{1,0},{2,1},{3,2},{4,3},{5,4},{6,5},{7,6},{9,8},{10,9},{11,10},{12... | collective-permute-start | bytes 638984 | tf_op jit(solution)/shard_map/ppermute | solution.py:432
  279.6 4.2 %collective-permute-start.13 = (f32[64,64,128]{2,1,0:T(8,128)S(1)}, f32[64,64,128]{2,1,0:T(8,128)S(1)}, u32[]{:S(2)}, u32[]{:S(2)}) collective-permute-start(f32[64,64,128]{2,1,0:T(8,128)S(1)} %fusion.1), channel_id=1, source_target_pairs={{0,8},{8,0},{16,24},{24,16},{1,9},{9,1},{17,25},{25,17},{2,10},{10... | collective-permute-start | bytes 6291464 | tf_op jit(solution)/shard_map/ppermute | solution.py:413

commit v4 on v3

--- a/solution.py
+++ b/solution.py
@@ -135,7 +135,7 @@
                 middle[v, h, pl.ds(y, depth, stride=rows), :] = cells[:, h * LANES : (h + 1) * LANES]
         return carry
 
-    lax.fori_loop(0, rows, row, 0, unroll=4)
+    lax.fori_loop(0, rows, row, 0, unroll=16)
 
 
 def spread_quotients(
@@ -158,7 +158,7 @@
                 turned[v, h, span, :] = cells[:, h * LANES : (h + 1) * LANES]
         return carry
 
-    lax.fori_loop(0, depth, plane, 0, unroll=4)
+    lax.fori_loop(0, depth, plane, 0, unroll=16)
 
     def row(y, carry):
         columns = [
@@ -174,7 +174,7 @@
             out_ref[h, pl.ds(y, depth_out, stride=rows), :] = cells[:, h * LANES : (h + 1) * LANES]
         return carry
 
-    lax.fori_loop(0, rows, row, 0, unroll=4)
+    lax.fori_loop(0, rows, row, 0, unroll=16)
 
 
 def whole_step_body(

time: 289 us -> 275 us (0.952)
  Pallas kernels: 116 us -> 99 us
  waiting for transfers between devices: 68 us -> 71.4 us
    pallas_call x1, Pallas kernels: 50.3 us -> 42.2 us  [whole_step(): pl.pallas_call(whole_step_body, in_specs=[IN_SMEM] + [IN_VMEM] * 8, out_s...]
    pallas_call x1, Pallas kernels: 34.2 us -> 28.4 us  [second_half(): pl.pallas_call(spread_quotients_apart, in_specs=[IN_SMEM] + [IN_VMEM] * 6...]
    ppermute x2, waiting for transfers between devices: 6.67 us -> 9.79 us  [shards(): lax.ppermute(incoming, 'view', [((v + CORES * hop) % view_count, v) for v...]
    pallas_call x1, Pallas kernels: 23.5 us -> 20.4 us  [first_half(): pl.pallas_call(blur_depth_columns, in_specs=[IN_VMEM] * 3, out_specs=[IN_...]
  transfers between devices with their start and end apart: 16 -> 16, of which waited for: 12 -> 12; matrix products, arithmetic and copies ran while one was open for 14% -> 14% of each run, Pallas kernels for 9% -> 8%
where the time goes in v4:
time: 275 us; the launch traced here: 273 us
  Pallas kernels  99 us (36%)
  waiting for transfers between devices  71.4 us (26%)
  other arithmetic  39.4 us (14%)
  starting transfers between devices  36.4 us (13%)
  local copies, waits for them, and re-layouts  25.7 us (9%)
    pallas_call x1, Pallas kernels, whole_step(): pl.pallas_call(whole_step_body, in_specs=[IN_SMEM] + [IN_VMEM] * 8, out_s...  42.2 us
    pallas_call x1, Pallas kernels, second_half(): pl.pallas_call(spread_quotients_apart, in_specs=[IN_SMEM] + [IN_VMEM] * 6...  28.4 us
    all_to_all x2, waiting for transfers between devices, shards(): lax.all_to_all(outgoing[part], 'block', split_axis=0, concat_axis=0, tile...  22.8 us
    pallas_call x1, Pallas kernels, first_half(): pl.pallas_call(blur_depth_columns, in_specs=[IN_VMEM] * 3, out_specs=[IN_...  20.4 us
    ppermute x2, waiting for transfers between devices, shards(): lax.ppermute(total[slab_depth + EDGE:slab_depth + EDGE + HALO].astype(BF1...  11.6 us
    all_to_all x2, starting transfers between devices, shards(): lax.all_to_all(outgoing[part], 'block', split_axis=0, concat_axis=0, tile...  10.7 us
    ppermute x2, waiting for transfers between devices, shards(): lax.ppermute(incoming, 'view', [((v + CORES * hop) % view_count, v) for v...  9.79 us
    ppermute x2, starting transfers between devices, widen(): low = lax.ppermute(cells[slab_depth - HALO:], 'block', up)  9.22 us
  transfers between devices with their start and end apart: 16, of which 12 were waited for; matrix products, arithmetic and copies ran while one was open for 14% of the time, Pallas kernels for 8%

profile of v4, /device:TPU:0, one launch (start us, length us, event | category | flops | bytes accessed | tf_op | source)
XLA Modules:
  0.0 273.1 jit_solution(11627055531425291320)
XLA Ops:
  0.0 2.6 convert_element_type.69
  3.6 4.9 %collective-permute-start.2 = (bf16[13,64,256]{2,1,0:T(8,128)(2,1)}, bf16[13,64,256]{2,1,0:T(8,128)(2,1)S(1)}, u32[]{:S(2)}, u32[]{:S(2)}) collective-permute-start(bf16[13,64,256]{2,1,0:T(8,128)(2,1)} %get-tuple-element.114), channel_id=1, source_target_pairs={{0,1},{1,2},{2,3},{3,4},{4,5},{5,6},{6,7},{8,9},{9,10},{10,11},{11... | collective-permute-start | bytes 1277960 | tf_op jit(solution)/shard_map/ppermute | solution.py:407
  8.5 1.3 collective-permute-start.3
  11.4 2.0 pick_pieces.1
  13.5 7.0 %all-to-all-start = ((bf16[8,256,256]{2,1,0:T(8,128)(2,1)}), bf16[8,256,256]{2,1,0:T(8,128)(2,1)S(1)}, u32[]{:S(2)}, u32[]{:S(2)}) async-start(bf16[8,256,256]{2,1,0:T(8,128)(2,1)} %get-tuple-element.8), calls=%async_computation | async-start | bytes 2097152 | tf_op jit(solution)/shard_map/all_to_all | solution.py:304
  21.4 1.1 slice_reduce_fusion.44
  33.7 13.9 %all-to-all-done = bf16[8,256,256]{2,1,0:T(8,128)(2,1)S(1)} async-done(((bf16[8,256,256]{2,1,0:T(8,128)(2,1)}), bf16[8,256,256]{2,1,0:T(8,128)(2,1)S(1)}, u32[]{:S(2)}, u32[]{:S(2)}) %all-to-all-start) | async-done | bytes 1048608 | tf_op jit(solution)/shard_map/all_to_all | solution.py:304
  47.5 3.7 %all-to-all-start.1 = ((bf16[8,256,256]{2,1,0:T(8,128)(2,1)}), bf16[8,256,256]{2,1,0:T(8,128)(2,1)S(1)}, u32[]{:S(2)}, u32[]{:S(2)}) async-start(bf16[8,256,256]{2,1,0:T(8,128)(2,1)} %get-tuple-element.9), calls=%async_computation.1 | async-start | bytes 2097152 | tf_op jit(solution)/shard_map/all_to_all | solution.py:304
  52.0 1.5 fusion.242.depth_ref.depth_back_ref
  53.5 2.3 select_convert_fusion.columns_ref
  55.8 1.9 pad_maximum_fusion.5.offset_ref
  57.7 2.3 select_convert_fusion.1.columns_ref.columns_back_ref
  60.7 3.8 %constant_dynamic-update-slice_fusion.1 = bf16[96,64,256]{2,1,0:T(8,128)(2,1)} fusion(bf16[96,64,256]{2,1,0:T(8,128)(2,1)} %constant_dynamic-update-slice_fusion.2, f32[64,64,256]{2,1,0:T(8,128)} %param.7), kind=kLoop, calls=%fused_computation.232 | loop fusion | flops 1048576 | bytes 6291456
  66.0 1.5 collective-permute-start
  67.5 8.9 %all-to-all-done.1 = bf16[8,256,256]{2,1,0:T(8,128)(2,1)S(1)} async-done(((bf16[8,256,256]{2,1,0:T(8,128)(2,1)}), bf16[8,256,256]{2,1,0:T(8,128)(2,1)S(1)}, u32[]{:S(2)}, u32[]{:S(2)}) %all-to-all-start.1) | async-done | bytes 1048608 | tf_op jit(solution)/shard_map/all_to_all | solution.py:304
  76.5 1.5 collective-permute-start.1
  78.0 2.6 slice_bitcast_fusion.1
  80.6 1.9 pad_maximum_fusion.2.volume_ref
  82.5 20.4 %blur_depth_columns.1 = (f32[2,6144,128]{2,1,0:T(8,128)}, f32[2,2,4096,128]{3,2,1,0:T(8,128)}) custom-call(bf16[128,96]{1,0:T(8,128)(2,1)} %copy.16.depth_ref, bf16[2,256,256]{2,1,0:T(8,128)(2,1)} %select_convert_fusion.columns_ref, bf16[2,96,64,128]{3,2,1,0:T(8,128)(2,1)} %pad_maximum_fusion.2.volume_ref), custom_call_target="tpu_custom_call" | custom-call | flops 5905580032 | bytes 14680064 | tf_op jit(solution)/shard_map/blur_depth_columns/pallas_call | solution.py:202
  103.1 9.8 %collective-permute-done.1 = bf16[8,256,256]{2,1,0:T(8,128)(2,1)} collective-permute-done((bf16[8,256,256]{2,1,0:T(8,128)(2,1)S(1)}, bf16[8,256,256]{2,1,0:T(8,128)(2,1)}, u32[]{:S(2)}, u32[]{:S(2)}) %collective-permute-start.1) | collective-permute-done | bytes 1048608 | tf_op jit(solution)/shard_map/ppermute | solution.py:308
  112.8 1.4 maximum_bitcast_fusion.1
  114.6 5.9 %place_pieces.1 = f32[2,16,256,256]{3,2,1,0:T(8,128)} custom-call(s32[2,16]{1,0:T(2,128)S(1)} %select_reduce_fusion.3.order_ref, s32[2,17]{1,0:T(2,128)S(1)} %convert_reduce_fusion.2.start_ref, f32[2,16]{1,0:T(2,128)S(1)} %convert_divide_fusion.scale_ref, bf16[2,16,256,256]{3,2,1,0:T(8,128)(2,1)S(1)} %pad_maximum_fusion.incoming_ref), custom_call_target="tpu_custom_call" | custom-call | tf_op jit(solution)/shard_map/place_pieces/pallas_call | solution.py:86
  120.6 28.4 %spread_quotients.1 = f32[2,6144,128]{2,1,0:T(8,128)} custom-call(f32[2]{0:T(128)} %pad_maximum_fusion.5.offset_ref, bf16[96,128]{1,0:T(8,128)(2,1)} %fusion.242.depth_ref.depth_back_ref, bf16[2,64,64]{2,1,0:T(8,128)(2,1)} %select_convert_fusion.3.rows_ref, bf16[2,64,64]{2,1,0:T(8,128)(2,1)} %select_convert_fusion.2.rows_back_ref, ...), custom_call_target="tpu_custom_call" | custom-call | tf_op jit(solution)/shard_map/spread_quotients/pallas_call | solution.py:224
  149.0 2.1 dynamic-slice_bitcast_fusion.1
  154.2 2.8 %collective-permute-done.4 = f32[96,64,128]{2,1,0:T(8,128)} collective-permute-done((f32[96,64,128]{2,1,0:T(8,128)S(1)}, f32[96,64,128]{2,1,0:T(8,128)}, u32[]{:S(2)}, u32[]{:S(2)}) %collective-permute-start.4) | collective-permute-done | bytes 3145760 | tf_op jit(solution)/shard_map/ppermute | solution.py:428
  157.0 3.8 %fusion.235 = (bf16[96,64,128]{2,1,0:T(8,128)(2,1)S(1)}, f32[96,64,128]{2,1,0:T(8,128)S(1)}) fusion(f32[96,64,128]{2,1,0:T(8,128)} %collective-permute-done.4, f32[2,96,64,128]{3,2,1,0:T(8,128)} %bitcast.87, s32[]{:T(128)S(6)} %select_n.623), kind=kLoop, calls=%fused_computation.415 | loop fusion | flops 1572864 | bytes 11010052 | tf_op jit(solution)/shard_map/convert.3
  160.8 3.4 %collective-permute-start.5 = (bf16[13,64,128]{2,1,0:T(8,128)(2,1)S(1)}, bf16[13,64,128]{2,1,0:T(8,128)(2,1)S(1)}, u32[]{:S(2)}, u32[]{:S(2)}) collective-permute-start(bf16[13,64,128]{2,1,0:T(8,128)(2,1)S(1)} %get-tuple-element.117), channel_id=1, source_target_pairs={{0,1},{1,2},{2,3},{3,4},{4,5},{5,6},{6,7},{8,9},{9,10},{10,11},{11... | collective-permute-start | bytes 638984 | tf_op jit(solution)/shard_map/ppermute | solution.py:429
  164.2 1.3 collective-permute-start.6
  165.5 8.1 %collective-permute-done.5 = bf16[13,64,128]{2,1,0:T(8,128)(2,1)S(1)} collective-permute-done((bf16[13,64,128]{2,1,0:T(8,128)(2,1)S(1)}, bf16[13,64,128]{2,1,0:T(8,128)(2,1)S(1)}, u32[]{:S(2)}, u32[]{:S(2)}) %collective-permute-start.5) | collective-permute-done | bytes 213024 | tf_op jit(solution)/shard_map/ppermute | solution.py:429
  173.7 1.6 fusion.233
  175.4 4.4 %collective-permute-start.7 = (bf16[13,64,128]{2,1,0:T(8,128)(2,1)S(1)}, bf16[13,64,128]{2,1,0:T(8,128)(2,1)S(1)}, u32[]{:S(2)}, u32[]{:S(2)}) collective-permute-start(bf16[13,64,128]{2,1,0:T(8,128)(2,1)S(1)} %get-tuple-element.120), channel_id=1, source_target_pairs={{0,1},{1,2},{2,3},{3,4},{4,5},{5,6},{6,7},{8,9},{9,10},{10,11},{11... | collective-permute-start | bytes 638984 | tf_op jit(solution)/shard_map/ppermute | solution.py:407
  180.4 1.3 collective-permute-start.8
  181.7 1.4 collective-permute-done.7
  184.8 4.9 %collective-permute-done.8 = bf16[13,64,128]{2,1,0:T(8,128)(2,1)S(1)} collective-permute-done((bf16[13,64,128]{2,1,0:T(8,128)(2,1)S(1)}, bf16[13,64,128]{2,1,0:T(8,128)(2,1)S(1)}, u32[]{:S(2)}, u32[]{:S(2)}) %collective-permute-start.8) | collective-permute-done | bytes 213024 | tf_op jit(solution)/shard_map/ppermute | solution.py:408
  191.1 3.7 %collective-permute-done.9 = bf16[96,64,128]{2,1,0:T(8,128)(2,1)} collective-permute-done((bf16[96,64,128]{2,1,0:T(8,128)(2,1)}, bf16[96,64,128]{2,1,0:T(8,128)(2,1)}, u32[]{:S(2)}, u32[]{:S(2)}) %collective-permute-start.9) | collective-permute-done | bytes 1572896 | tf_op jit(solution)/shard_map/ppermute | solution.py:413
  194.8 2.1 select_bitcast_fusion.1
  196.9 1.9 pad_maximum_fusion.3.volume_ref
  198.9 42.2 %whole_step.1 = f32[2,6144,128]{2,1,0:T(8,128)} custom-call(f32[2]{0:T(128)} %pad_maximum_fusion.5.offset_ref, bf16[128,96]{1,0:T(8,128)(2,1)} %copy.16.depth_ref, bf16[96,128]{1,0:T(8,128)(2,1)} %fusion.242.depth_ref.depth_back_ref, bf16[2,64,64]{2,1,0:T(8,128)(2,1)} %select_convert_fusion.3.rows_ref, ...), custom_call_target="tpu_custom_call" | custom-call | tf_op jit(solution)/shard_map/whole_step/pallas_call | solution.py:251
  241.0 2.3 dynamic-slice_bitcast_fusion
  243.5 5.5 %collective-permute-done.10 = f32[96,64,128]{2,1,0:T(8,128)S(1)} collective-permute-done((f32[96,64,128]{2,1,0:T(8,128)S(1)}, f32[96,64,128]{2,1,0:T(8,128)S(1)}, u32[]{:S(2)}, u32[]{:S(2)}) %collective-permute-start.10) | collective-permute-done | bytes 3145760 | tf_op jit(solution)/shard_map/ppermute | solution.py:428
  249.0 1.1 fusion.232
  250.2 4.5 %collective-permute-start.11 = (bf16[13,64,128]{2,1,0:T(8,128)(2,1)S(1)}, bf16[13,64,128]{2,1,0:T(8,128)(2,1)S(1)}, u32[]{:S(2)}, u32[]{:S(2)}) collective-permute-start(bf16[13,64,128]{2,1,0:T(8,128)(2,1)S(1)} %get-tuple-element.115), channel_id=1, source_target_pairs={{0,1},{1,2},{2,3},{3,4},{4,5},{5,6},{6,7},{8,9},{9,10},{10,11},{11... | collective-permute-start | bytes 638984 | tf_op jit(solution)/shard_map/ppermute | solution.py:429
  254.7 1.3 collective-permute-start.12
  256.0 3.5 %collective-permute-done.11 = bf16[13,64,128]{2,1,0:T(8,128)(2,1)S(1)} collective-permute-done((bf16[13,64,128]{2,1,0:T(8,128)(2,1)S(1)}, bf16[13,64,128]{2,1,0:T(8,128)(2,1)S(1)}, u32[]{:S(2)}, u32[]{:S(2)}) %collective-permute-start.11) | collective-permute-done | bytes 213024 | tf_op jit(solution)/shard_map/ppermute | solution.py:429
  259.5 4.7 %collective-permute-done.12 = bf16[13,64,128]{2,1,0:T(8,128)(2,1)S(1)} collective-permute-done((bf16[13,64,128]{2,1,0:T(8,128)(2,1)S(1)}, bf16[13,64,128]{2,1,0:T(8,128)(2,1)S(1)}, u32[]{:S(2)}, u32[]{:S(2)}) %collective-permute-start.12) | collective-permute-done | bytes 213024 | tf_op jit(solution)/shard_map/ppermute | solution.py:432
  264.2 1.4 fusion.1
  265.8 4.1 %collective-permute-done.13 = f32[64,64,128]{2,1,0:T(8,128)S(1)} collective-permute-done((f32[64,64,128]{2,1,0:T(8,128)S(1)}, f32[64,64,128]{2,1,0:T(8,128)S(1)}, u32[]{:S(2)}, u32[]{:S(2)}) %collective-permute-start.13) | collective-permute-done | bytes 2097184 | tf_op jit(solution)/shard_map/ppermute | solution.py:413
  270.7 2.4 pad_maximum_fusion.1
  (201 shorter events, 25.9 us)
Async XLA Ops:
  0.0 10.3 %copy-start.6 = (s32[4,128,1]{1,2,0:T(1,128)S(1)}, s32[4,128,1]{1,2,0:T(1,128)}, u32[]{:S(2)}) copy-start(s32[4,128,1]{1,2,0:T(1,128)} %param.9) | copy-start | bytes 6148
  0.0 11.4 %copy-start = (bf16[1,16,4,64,256]{4,3,2,1,0:T(8,128)(2,1)S(1)}, bf16[1,16,4,64,256]{4,3,2,1,0:T(8,128)(2,1)}, u32[]{:S(2)}) copy-start(bf16[1,16,4,64,256]{4,3,2,1,0:T(8,128)(2,1)} %param.8) | copy-start | bytes 6291460
  3.6 56.3 %collective-permute-start.2 = (bf16[13,64,256]{2,1,0:T(8,128)(2,1)}, bf16[13,64,256]{2,1,0:T(8,128)(2,1)S(1)}, u32[]{:S(2)}, u32[]{:S(2)}) collective-permute-start(bf16[13,64,256]{2,1,0:T(8,128)(2,1)} %get-tuple-element.114), channel_id=1, source_target_pairs={{0,1},{1,2},{2,3},{3,4},{4,5},{5,6},{6,7},{8,9},{9,10},{10,11},{11... | collective-permute-start | bytes 1277960 | tf_op jit(solution)/shard_map/ppermute | solution.py:407
  8.5 56.1 %collective-permute-start.3 = (bf16[13,64,256]{2,1,0:T(8,128)(2,1)}, bf16[13,64,256]{2,1,0:T(8,128)(2,1)S(1)}, u32[]{:S(2)}, u32[]{:S(2)}) collective-permute-start(bf16[13,64,256]{2,1,0:T(8,128)(2,1)} %get-tuple-element.113), channel_id=1, source_target_pairs={{1,0},{2,1},{3,2},{4,3},{5,4},{6,5},{7,6},{9,8},{10,9},{11,10},{12... | collective-permute-start | bytes 1277960 | tf_op jit(solution)/shard_map/ppermute | solution.py:408
  11.4 9.1 %copy-start.4 = (f32[4,3,21]{2,0,1:T(4,128)S(1)}, f32[4,3,21]{2,0,1:T(4,128)}, u32[]{:S(2)}) copy-start(f32[4,3,21]{2,0,1:T(4,128)} %param.12) | copy-start | bytes 3028
  11.4 12.4 %copy-start.3 = (s32[4,3]{1,0:T(4,128)S(1)}, s32[4,3]{1,0:T(4,128)}, u32[]{:S(2)}) copy-start(s32[4,3]{1,0:T(4,128)} %param.11) | copy-start | bytes 148
  11.4 16.7 %copy-start.5 = (s32[4,128]{1,0:T(4,128)S(1)}, s32[4,128]{1,0:T(4,128)}, u32[]{:S(2)}) copy-start(s32[4,128]{1,0:T(4,128)} %param.10) | copy-start | bytes 6148
  11.4 18.1 %copy-start.29 = (f32[4]{0:T(128)S(1)}, f32[4]{0:T(128)}, u32[]{:S(2)}) copy-start(f32[4]{0:T(128)} %param.13) | copy-start | bytes 52
  13.5 34.0 %all-to-all-start = ((bf16[8,256,256]{2,1,0:T(8,128)(2,1)}), bf16[8,256,256]{2,1,0:T(8,128)(2,1)S(1)}, u32[]{:S(2)}, u32[]{:S(2)}) async-start(bf16[8,256,256]{2,1,0:T(8,128)(2,1)} %get-tuple-element.8), calls=%async_computation | async-start | bytes 2097152 | tf_op jit(solution)/shard_map/all_to_all | solution.py:304
  24.7 7.1 %copy-start.7 = (bf16[128]{0:T(256)(128)(2,1)}, bf16[128]{0:T(256)(128)(2,1)S(1)}, u32[]{:S(2)}) copy-start(bf16[128]{0:T(256)(128)(2,1)S(1)} %broadcast_in_dim.471) | copy-start | bytes 772
  24.9 7.0 %copy-start.8 = (bf16[128]{0:T(256)(128)(2,1)}, bf16[128]{0:T(256)(128)(2,1)S(1)}, u32[]{:S(2)}) copy-start(bf16[128]{0:T(256)(128)(2,1)S(1)} %broadcast_in_dim.480) | copy-start | bytes 772
  25.0 6.8 %copy-start.9 = (bf16[128]{0:T(256)(128)(2,1)}, bf16[128]{0:T(256)(128)(2,1)S(1)}, u32[]{:S(2)}) copy-start(bf16[128]{0:T(256)(128)(2,1)S(1)} %broadcast_in_dim.483) | copy-start | bytes 772
  25.2 6.6 %copy-start.10 = (bf16[128]{0:T(256)(128)(2,1)}, bf16[128]{0:T(256)(128)(2,1)S(1)}, u32[]{:S(2)}) copy-start(bf16[128]{0:T(256)(128)(2,1)S(1)} %broadcast_in_dim.486) | copy-start | bytes 772
  25.3 6.5 %copy-start.11 = (bf16[128]{0:T(256)(128)(2,1)}, bf16[128]{0:T(256)(128)(2,1)S(1)}, u32[]{:S(2)}) copy-start(bf16[128]{0:T(256)(128)(2,1)S(1)} %broadcast_in_dim.489) | copy-start | bytes 772
  25.5 6.3 %copy-start.12 = (bf16[128]{0:T(256)(128)(2,1)}, bf16[128]{0:T(256)(128)(2,1)S(1)}, u32[]{:S(2)}) copy-start(bf16[128]{0:T(256)(128)(2,1)S(1)} %broadcast_in_dim.492) | copy-start | bytes 772
  25.7 6.2 %copy-start.13 = (bf16[128]{0:T(256)(128)(2,1)}, bf16[128]{0:T(256)(128)(2,1)S(1)}, u32[]{:S(2)}) copy-start(bf16[128]{0:T(256)(128)(2,1)S(1)} %broadcast_in_dim.495) | copy-start | bytes 772
  25.8 6.0 %copy-start.14 = (bf16[128]{0:T(256)(128)(2,1)}, bf16[128]{0:T(256)(128)(2,1)S(1)}, u32[]{:S(2)}) copy-start(bf16[128]{0:T(256)(128)(2,1)S(1)} %broadcast_in_dim.498) | copy-start | bytes 772
  26.0 5.9 %copy-start.15 = (bf16[128]{0:T(256)(128)(2,1)}, bf16[128]{0:T(256)(128)(2,1)S(1)}, u32[]{:S(2)}) copy-start(bf16[128]{0:T(256)(128)(2,1)S(1)} %broadcast_in_dim.501) | copy-start | bytes 772
  26.1 5.7 %copy-start.16 = (bf16[128]{0:T(256)(128)(2,1)}, bf16[128]{0:T(256)(128)(2,1)S(1)}, u32[]{:S(2)}) copy-start(bf16[128]{0:T(256)(128)(2,1)S(1)} %broadcast_in_dim.504) | copy-start | bytes 772
  26.3 5.6 %copy-start.17 = (bf16[128]{0:T(256)(128)(2,1)}, bf16[128]{0:T(256)(128)(2,1)S(1)}, u32[]{:S(2)}) copy-start(bf16[128]{0:T(256)(128)(2,1)S(1)} %broadcast_in_dim.507) | copy-start | bytes 772
  26.5 5.4 %copy-start.18 = (bf16[128]{0:T(256)(128)(2,1)}, bf16[128]{0:T(256)(128)(2,1)S(1)}, u32[]{:S(2)}) copy-start(bf16[128]{0:T(256)(128)(2,1)S(1)} %broadcast_in_dim.510) | copy-start | bytes 772
  26.6 5.3 %copy-start.19 = (bf16[128]{0:T(256)(128)(2,1)}, bf16[128]{0:T(256)(128)(2,1)S(1)}, u32[]{:S(2)}) copy-start(bf16[128]{0:T(256)(128)(2,1)S(1)} %broadcast_in_dim.513) | copy-start | bytes 772
  26.8 5.1 %copy-start.20 = (bf16[128]{0:T(256)(128)(2,1)}, bf16[128]{0:T(256)(128)(2,1)S(1)}, u32[]{:S(2)}) copy-start(bf16[128]{0:T(256)(128)(2,1)S(1)} %broadcast_in_dim.516) | copy-start | bytes 772
  26.9 5.0 %copy-start.21 = (bf16[128]{0:T(256)(128)(2,1)}, bf16[128]{0:T(256)(128)(2,1)S(1)}, u32[]{:S(2)}) copy-start(bf16[128]{0:T(256)(128)(2,1)S(1)} %broadcast_in_dim.519) | copy-start | bytes 772
  27.1 4.8 %copy-start.22 = (bf16[128]{0:T(256)(128)(2,1)}, bf16[128]{0:T(256)(128)(2,1)S(1)}, u32[]{:S(2)}) copy-start(bf16[128]{0:T(256)(128)(2,1)S(1)} %broadcast_in_dim.522) | copy-start | bytes 772
  27.3 4.7 %copy-start.23 = (bf16[128]{0:T(256)(128)(2,1)}, bf16[128]{0:T(256)(128)(2,1)S(1)}, u32[]{:S(2)}) copy-start(bf16[128]{0:T(256)(128)(2,1)S(1)} %broadcast_in_dim.525) | copy-start | bytes 772
  27.4 4.5 %copy-start.24 = (bf16[128]{0:T(256)(128)(2,1)}, bf16[128]{0:T(256)(128)(2,1)S(1)}, u32[]{:S(2)}) copy-start(bf16[128]{0:T(256)(128)(2,1)S(1)} %broadcast_in_dim.528) | copy-start | bytes 772
  27.6 4.4 %copy-start.25 = (bf16[128]{0:T(256)(128)(2,1)}, bf16[128]{0:T(256)(128)(2,1)S(1)}, u32[]{:S(2)}) copy-start(bf16[128]{0:T(256)(128)(2,1)S(1)} %broadcast_in_dim.531) | copy-start | bytes 772
  27.8 4.2 %copy-start.26 = (bf16[128]{0:T(256)(128)(2,1)}, bf16[128]{0:T(256)(128)(2,1)S(1)}, u32[]{:S(2)}) copy-start(bf16[128]{0:T(256)(128)(2,1)S(1)} %broadcast_in_dim.474) | copy-start | bytes 772
  27.9 4.1 %copy-start.27 = (bf16[128]{0:T(256)(128)(2,1)}, bf16[128]{0:T(256)(128)(2,1)S(1)}, u32[]{:S(2)}) copy-start(bf16[128]{0:T(256)(128)(2,1)S(1)} %broadcast_in_dim.477) | copy-start | bytes 772
  28.1 3.9 %copy-start.28 = (s32[128]{0:T(128)}, s32[128]{0:T(128)S(1)}, u32[]{:S(2)}) copy-start(s32[128]{0:T(128)S(1)} %sub.197) | copy-start | bytes 1540
  47.5 28.9 %all-to-all-start.1 = ((bf16[8,256,256]{2,1,0:T(8,128)(2,1)}), bf16[8,256,256]{2,1,0:T(8,128)(2,1)S(1)}, u32[]{:S(2)}, u32[]{:S(2)}) async-start(bf16[8,256,256]{2,1,0:T(8,128)(2,1)} %get-tuple-element.9), calls=%async_computation.1 | async-start | bytes 2097152 | tf_op jit(solution)/shard_map/all_to_all | solution.py:304
  66.0 37.1 %collective-permute-start = (bf16[8,256,256]{2,1,0:T(8,128)(2,1)S(1)}, bf16[8,256,256]{2,1,0:T(8,128)(2,1)S(1)}, u32[]{:S(2)}, u32[]{:S(2)}) collective-permute-start(bf16[8,256,256]{2,1,0:T(8,128)(2,1)S(1)} %all-to-all-done), channel_id=1, source_target_pairs={{16,0},{24,8},{0,16},{8,24},{17,1},{25,9},{1,17},{9,25},{18,2},{26... | collective-permute-start | bytes 3145736 | tf_op jit(solution)/shard_map/ppermute | solution.py:308
  76.5 36.4 %collective-permute-start.1 = (bf16[8,256,256]{2,1,0:T(8,128)(2,1)S(1)}, bf16[8,256,256]{2,1,0:T(8,128)(2,1)}, u32[]{:S(2)}, u32[]{:S(2)}) collective-permute-start(bf16[8,256,256]{2,1,0:T(8,128)(2,1)S(1)} %all-to-all-done.1), channel_id=1, source_target_pairs={{16,0},{24,8},{0,16},{8,24},{17,1},{25,9},{1,17},{9,25},{18,2},{26... | collective-permute-start | bytes 3145736 | tf_op jit(solution)/shard_map/ppermute | solution.py:308
  151.1 5.9 %collective-permute-start.4 = (f32[96,64,128]{2,1,0:T(8,128)S(1)}, f32[96,64,128]{2,1,0:T(8,128)}, u32[]{:S(2)}, u32[]{:S(2)}) collective-permute-start(f32[96,64,128]{2,1,0:T(8,128)S(1)} %dynamic-slice_bitcast_fusion.1), channel_id=1, source_target_pairs={{0,8},{8,0},{16,24},{24,16},{1,9},{9,1},{17,25},{25,17},{2,10},{10... | collective-permute-start | bytes 9437192 | tf_op jit(solution)/shard_map/ppermute | solution.py:428
  157.0 16.7 %copy-start.1 = (f32[64,64,256]{2,1,0:T(8,128)S(1)}, f32[64,64,256]{2,1,0:T(8,128)}, u32[]{:S(2)}) copy-start(f32[64,64,256]{2,1,0:T(8,128)} %param.7) | copy-start | bytes 12582916
  160.8 12.8 %collective-permute-start.5 = (bf16[13,64,128]{2,1,0:T(8,128)(2,1)S(1)}, bf16[13,64,128]{2,1,0:T(8,128)(2,1)S(1)}, u32[]{:S(2)}, u32[]{:S(2)}) collective-permute-start(bf16[13,64,128]{2,1,0:T(8,128)(2,1)S(1)} %get-tuple-element.117), channel_id=1, source_target_pairs={{0,1},{1,2},{2,3},{3,4},{4,5},{5,6},{6,7},{8,9},{9,10},{10,11},{11... | collective-permute-start | bytes 638984 | tf_op jit(solution)/shard_map/ppermute | solution.py:429
  164.2 9.4 %collective-permute-start.6 = (bf16[13,64,128]{2,1,0:T(8,128)(2,1)S(1)}, bf16[13,64,128]{2,1,0:T(8,128)(2,1)S(1)}, u32[]{:S(2)}, u32[]{:S(2)}) collective-permute-start(bf16[13,64,128]{2,1,0:T(8,128)(2,1)S(1)} %get-tuple-element.118), channel_id=1, source_target_pairs={{1,0},{2,1},{3,2},{4,3},{5,4},{6,5},{7,6},{9,8},{10,9},{11,10},{12... | collective-permute-start | bytes 638984 | tf_op jit(solution)/shard_map/ppermute | solution.py:432
  175.4 7.7 %collective-permute-start.7 = (bf16[13,64,128]{2,1,0:T(8,128)(2,1)S(1)}, bf16[13,64,128]{2,1,0:T(8,128)(2,1)S(1)}, u32[]{:S(2)}, u32[]{:S(2)}) collective-permute-start(bf16[13,64,128]{2,1,0:T(8,128)(2,1)S(1)} %get-tuple-element.120), channel_id=1, source_target_pairs={{0,1},{1,2},{2,3},{3,4},{4,5},{5,6},{6,7},{8,9},{9,10},{10,11},{11... | collective-permute-start | bytes 638984 | tf_op jit(solution)/shard_map/ppermute | solution.py:407
  180.4 9.4 %collective-permute-start.8 = (bf16[13,64,128]{2,1,0:T(8,128)(2,1)S(1)}, bf16[13,64,128]{2,1,0:T(8,128)(2,1)S(1)}, u32[]{:S(2)}, u32[]{:S(2)}) collective-permute-start(bf16[13,64,128]{2,1,0:T(8,128)(2,1)S(1)} %get-tuple-element.119), channel_id=1, source_target_pairs={{1,0},{2,1},{3,2},{4,3},{5,4},{6,5},{7,6},{9,8},{10,9},{11,10},{12... | collective-permute-start | bytes 638984 | tf_op jit(solution)/shard_map/ppermute | solution.py:408
  191.1 3.8 %collective-permute-start.9 = (bf16[96,64,128]{2,1,0:T(8,128)(2,1)}, bf16[96,64,128]{2,1,0:T(8,128)(2,1)}, u32[]{:S(2)}, u32[]{:S(2)}) collective-permute-start(bf16[96,64,128]{2,1,0:T(8,128)(2,1)} %broadcast_dynamic-update-slice_fusion.3), channel_id=1, source_target_pairs={{0,8},{8,0},{16,24},{24,16},{1,9},{9,1},{17,25},{25,17},{2,10},{10... | collective-permute-start | bytes 4718600 | tf_op jit(solution)/shard_map/ppermute | solution.py:413
  241.0 8.0 %copy-start.2 = (f32[2,6144,128]{2,1,0:T(8,128)S(1)}, f32[2,6144,128]{2,1,0:T(8,128)}, u32[]{:S(2)}) copy-start(f32[2,6144,128]{2,1,0:T(8,128)} %whole_step.1) | copy-start | bytes 18874372
  243.3 5.7 %collective-permute-start.10 = (f32[96,64,128]{2,1,0:T(8,128)S(1)}, f32[96,64,128]{2,1,0:T(8,128)S(1)}, u32[]{:S(2)}, u32[]{:S(2)}) collective-permute-start(f32[96,64,128]{2,1,0:T(8,128)S(1)} %dynamic-slice_bitcast_fusion), channel_id=1, source_target_pairs={{0,8},{8,0},{16,24},{24,16},{1,9},{9,1},{17,25},{25,17},{2,10},{10... | collective-permute-start | bytes 9437192 | tf_op jit(solution)/shard_map/ppermute | solution.py:428
  250.2 9.3 %collective-permute-start.11 = (bf16[13,64,128]{2,1,0:T(8,128)(2,1)S(1)}, bf16[13,64,128]{2,1,0:T(8,128)(2,1)S(1)}, u32[]{:S(2)}, u32[]{:S(2)}) collective-permute-start(bf16[13,64,128]{2,1,0:T(8,128)(2,1)S(1)} %get-tuple-element.115), channel_id=1, source_target_pairs={{0,1},{1,2},{2,3},{3,4},{4,5},{5,6},{6,7},{8,9},{9,10},{10,11},{11... | collective-permute-start | bytes 638984 | tf_op jit(solution)/shard_map/ppermute | solution.py:429
  254.7 9.5 %collective-permute-start.12 = (bf16[13,64,128]{2,1,0:T(8,128)(2,1)S(1)}, bf16[13,64,128]{2,1,0:T(8,128)(2,1)S(1)}, u32[]{:S(2)}, u32[]{:S(2)}) collective-permute-start(bf16[13,64,128]{2,1,0:T(8,128)(2,1)S(1)} %get-tuple-element.116), channel_id=1, source_target_pairs={{1,0},{2,1},{3,2},{4,3},{5,4},{6,5},{7,6},{9,8},{10,9},{11,10},{12... | collective-permute-start | bytes 638984 | tf_op jit(solution)/shard_map/ppermute | solution.py:432
  265.7 4.2 %collective-permute-start.13 = (f32[64,64,128]{2,1,0:T(8,128)S(1)}, f32[64,64,128]{2,1,0:T(8,128)S(1)}, u32[]{:S(2)}, u32[]{:S(2)}) collective-permute-start(f32[64,64,128]{2,1,0:T(8,128)S(1)} %fusion.1), channel_id=1, source_target_pairs={{0,8},{8,0},{16,24},{24,16},{1,9},{9,1},{17,25},{25,17},{2,10},{10... | collective-permute-start | bytes 6291464 | tf_op jit(solution)/shard_map/ppermute | solution.py:413
